TPU v7x, 256 devices: a whole 4x4x8 slice. The times are simulated.
256 devices in a mesh: vrow: 32 (over z_hi, y, core), vcol: 8 (over x, z_lo).
Axes of the slice: x: 4, y: 4, z: 8 (z_hi: 4, z_lo: 2; z = z_hi * 2 + z_lo), core: 2. Of those that a mesh axis runs over, the one named last changes fastest.
Arguments:
- pairs: int32 [64, 2], replicated, may hold values from 0 to 119, as said below
- offsets: int32 [2, 2], replicated, may hold values from 0 to 1016, as said below
- amplitudes: bfloat16 [64, 1024, 1024], P(None, 'vrow', 'vcol'), may hold values from -0.59765625 to 0.59765625
- slabs: bfloat16 [2, 2, 1024, 8, 2304], P(None, None, ('vrow', 'vcol')), may hold values from -0.86328125 to 0.86328125
Outputs:
- residual: float32 [64, 1024, 1024], P(None, 'vrow', 'vcol')
Inputs may be any that keep to these rules, and one draw needn't show every extreme that they name: `pairs`: each row is an occupied pair i <= j; some rows have i = j. `offsets`: every offset is a multiple of 8.
All inputs are finite; a program needn't handle non-finite values.
Results may differ from a plain program's by a relative error of at most 0.0003.
Values may be sent and summed in bfloat16 or wider, within the bound.
No kernel may reach another device: no remote copies, remote signals or barrier semaphores. Data moves between devices by JAX's collectives and lax.ppermute only.
A program may use at most 128 MiB of HBM per device.

v0:
```python
import jax
import jax.numpy as jnp
from jax import lax
from jax.sharding import PartitionSpec as P

BLK = 8
P_SIZE = 64
STEPS = 2


def broadcast(block, axis, holder):
    block = jnp.where(lax.axis_index(axis) == holder, block, jnp.zeros_like(block))
    return lax.psum(block, axis)


def ladder_part(rows, upper, lower, piece):
    depth = rows.shape[-1]
    count_a = rows.shape[2]
    count_b = piece.shape[2]
    rows_c = rows[0, 0].reshape(count_a * BLK, depth)
    rows_d = rows[0, 1].reshape(count_a * BLK, depth)
    piece_c = piece[0, 0].reshape(count_b * BLK, depth)
    piece_d = piece[0, 1].reshape(count_b * BLK, depth)
    direct = lax.dot_general(
        rows_c, piece_d, (((1,), (1,)), ((), ())), preferred_element_type=jnp.float32
    ).reshape(count_a, BLK, count_b, BLK)
    swapped = lax.dot_general(
        rows_d, piece_c, (((1,), (1,)), ((), ())), preferred_element_type=jnp.float32
    ).reshape(count_a, BLK, count_b, BLK)
    term = jnp.einsum("acbd,pcd->pab", direct, upper[0], precision=lax.Precision.HIGHEST)
    term = term + jnp.einsum("adbc,pcd->pab", swapped, lower[0], precision=lax.Precision.HIGHEST)
    term = term[None]
    return term


def on_device(pairs, offsets, amplitudes, slabs):
    row_count = lax.axis_size("vrow")
    col_count = lax.axis_size("vcol")
    rows_loc = amplitudes.shape[1]
    cols_loc = amplitudes.shape[2]
    offdiag = (pairs[:, 0] != pairs[:, 1]).astype(jnp.float32)
    zero = jnp.zeros((), jnp.int32)
    upper_list = []
    lower_list = []
    for k in range(STEPS):
        first = offsets[k, 0]
        second = offsets[k, 1]
        own_forward = lax.dynamic_slice(
            amplitudes, (zero, first % rows_loc, second % cols_loc), (P_SIZE, BLK, BLK)
        )
        own_mirror = lax.dynamic_slice(
            amplitudes, (zero, second % rows_loc, first % cols_loc), (P_SIZE, BLK, BLK)
        )
        root_forward = first // rows_loc * col_count + second // cols_loc
        root_mirror = second // rows_loc * col_count + first // cols_loc
        forward = broadcast(own_forward, ("vrow", "vcol"), root_forward).astype(jnp.float32)
        mirror_raw = broadcast(own_mirror, ("vrow", "vcol"), root_mirror).astype(jnp.float32)
        mirror = jnp.transpose(mirror_raw, (0, 2, 1))
        plus = 0.5 * (forward + mirror)
        minus = 0.5 * (forward - mirror) * offdiag[:, None, None]
        upper_list.append(plus + minus)
        lower_list.append(plus - minus)
    results = None
    for k in range(STEPS):
        rows = lax.all_gather(slabs[k], "vcol", axis=1, tiled=True)

        def single(piece, start, rows=rows, k=k):
            return ladder_part(rows[None], upper_list[k][None], lower_list[k][None], piece[None])

        term = single(lax.all_gather(slabs[k], "vrow", axis=1, tiled=True), jnp.int32(0))
        results = term if results is None else results + term
    groups = row_count // col_count
    inner = cols_loc // row_count
    shaped = results[0].reshape(P_SIZE, rows_loc, col_count, groups, 1, inner)
    moved = lax.all_to_all(shaped, "vcol", split_axis=2, concat_axis=4, tiled=True)
    combined = moved.reshape(P_SIZE, rows_loc, cols_loc)
    return combined


def solution(mesh):
    in_specs = (P(), P(), P(None, "vrow", "vcol"), P(None, None, ("vrow", "vcol"), None, None))
    out_specs = P(None, "vrow", "vcol")
    return jax.shard_map(
        on_device, mesh=mesh, in_specs=in_specs, out_specs=out_specs, check_vma=False
    )
```

profile of v0, /device:TPU:33, one launch (start us, length us, event | category | flops | bytes accessed | tf_op | source)
XLA Modules:
  0.0 345.4 jit_solution(7817607009388530173)
XLA Ops:
  6.5 0.0 copy-start.4
  6.5 0.0 all-gather.15.cloned.1.call-start
  6.5 1.1 fusion.46
  7.6 0.7 copy.117
  8.4 0.0 all-gather.15.cloned.1.call-update
  8.4 0.0 all-gather.13.cloned.1.call-start
  8.4 0.7 all-gather.13.cloned.1.call-update
  9.2 0.0 all-gather.11.cloned.1.call-start
  9.2 0.7 copy.110
  9.9 0.0 all-gather.11.cloned.1.call-update
  10.0 0.0 all-gather.9.cloned.1.call-start
  10.0 0.5 all-gather.9.cloned.1.call-update
  10.5 1.5 fusion.47
  22.3 1.5 constant_dynamic-slice_fusion.3
  23.8 0.1 copy.116
  23.9 0.1 copy.109
  24.1 0.1 copy.115
  24.2 0.1 copy.108
  24.4 87.0 %all-reduce = (bf16[64,8,8]{0,2,1:T(8,128)(2,1)S(1)}, bf16[64,8,8]{0,1,2:T(8,128)(2,1)S(1)}, bf16[64,8,8]{0,2,1:T(8,128)(2,1)S(1)}, bf16[64,8,8]{0,1,2:T(8,128)(2,1)S(1)}) all-reduce(bf16[64,8,8]{0,2,1:T(8,128)(2,1)S(1)} %get-tuple-element.23, ...), channel_id=1, replica_groups=mesh['vrow'=32,'vcol'=8] {'vrow','vcol'}, use_global_device_ids=true, to_apply=%region_3.4 | all-reduce | flops 16384 | bytes 65536 | tf_op jit(solution)/shard_map/psum | solution.py:13
  111.4 0.0 copy-done.4
  111.4 0.0 all-gather.15.cloned.1.call-done
  111.5 8.2 %fusion.45 = (bf16[1,1,128,8,2304]{4,3,1,0,2:T(8,128)(2,1)}, bf16[1,1,128,8,2304]{4,3,1,0,2:T(8,128)(2,1)}) fusion(bf16[1,2,128,8,2304]{4,3,1,0,2:T(8,128)(2,1)} %all-gather.15.cloned.1.call-done), kind=kLoop, calls=%fused_computation.62 | loop fusion | bytes 18874368 | tf_op jit(solution)/shard_map/slice | solution.py:23
  119.6 36.2 %all-gather.13.cloned.1.call-done = bf16[1,2,32,8,2304]{4,3,1,0,2:T(8,128)(2,1)} async-done(((bf16[1,2,4,8,2304]{4,3,1,0,2:T(8,128)(2,1)}), bf16[1,2,32,8,2304]{4,3,1,0,2:T(8,128)(2,1)}) %all-gather.13.cloned.1.call-update) | async-done | bytes 2359312 | tf_op jit(solution)/shard_map/all_gather | solution.py:65
  155.8 0.0 copy-start.1
  155.8 0.0 copy-start.3
  155.8 4.4 %fusion = f32[32,8,128,8]{2,1,3,0:T(8,128)S(1)} fusion(bf16[1,1,128,8,2304]{4,3,1,0,2:T(8,128)(2,1)} %get-tuple-element.12, bf16[1,2,32,8,2304]{4,3,1,0,2:T(8,128)(2,1)} %all-gather.13.cloned.1.call-done), kind=kOutput, calls=%fused_computation.1 | convolution fusion | flops 1207959552 | bytes 6946816 | tf_op jit(solution)/shard_map/dot_general | solution.py:27
  160.3 1.0 convolution_bitcast_fusion
  161.3 0.0 copy-done.1
  161.3 0.0 copy-done.3
  161.3 1.6 fusion.1
  163.0 1.1 fusion.6
  164.1 78.9 %all-gather.11.cloned.1.call-done = bf16[1,2,128,8,2304]{4,3,1,0,2:T(8,128)(2,1)} async-done(((bf16[1,2,4,8,2304]{4,3,1,0,2:T(8,128)(2,1)}), bf16[1,2,128,8,2304]{4,3,1,0,2:T(8,128)(2,1)}) %all-gather.11.cloned.1.call-update) | async-done | bytes 9437200 | tf_op jit(solution)/shard_map/all_gather | solution.py:70
  243.0 8.1 %fusion.44 = (bf16[1,1,128,8,2304]{4,3,1,0,2:T(8,128)(2,1)}, bf16[1,1,128,8,2304]{4,3,1,0,2:T(8,128)(2,1)}) fusion(bf16[1,2,128,8,2304]{4,3,1,0,2:T(8,128)(2,1)} %all-gather.11.cloned.1.call-done), kind=kLoop, calls=%fused_computation.61 | loop fusion | bytes 18874368 | tf_op jit(solution)/shard_map/slice | solution.py:23
  251.0 50.2 %all-gather.9.cloned.1.call-done = bf16[1,2,32,8,2304]{4,3,1,0,2:T(8,128)(2,1)} async-done(((bf16[1,2,4,8,2304]{4,3,1,0,2:T(8,128)(2,1)}), bf16[1,2,32,8,2304]{4,3,1,0,2:T(8,128)(2,1)}) %all-gather.9.cloned.1.call-update) | async-done | bytes 2359312 | tf_op jit(solution)/shard_map/all_gather | solution.py:65
  301.2 0.0 copy-start
  301.2 0.0 copy-start.2
  301.2 4.4 %fusion.2 = f32[32,8,128,8]{2,1,3,0:T(8,128)S(1)} fusion(bf16[1,1,128,8,2304]{4,3,1,0,2:T(8,128)(2,1)} %get-tuple-element.10, bf16[1,2,32,8,2304]{4,3,1,0,2:T(8,128)(2,1)} %all-gather.9.cloned.1.call-done), kind=kOutput, calls=%fused_computation.5 | convolution fusion | flops 1207959552 | bytes 6946816 | tf_op jit(solution)/shard_map/dot_general | solution.py:27
  305.6 1.0 convolution_bitcast_fusion.2
  306.7 0.0 copy-done
  306.7 0.0 copy-done.2
  306.7 1.6 fusion.3
  308.3 1.1 fusion.5
  309.4 2.0 copy.90
  311.5 1.3 reshape.65
  312.9 18.6 %all_to_all.15 = f32[8,1,32768]{2,1,0:T(1,128)S(1)} all-to-all(f32[8,1,32768]{2,1,0:T(1,128)S(1)} %reshape.65), channel_id=1, replica_groups=mesh['vrow'=32,'vcol'=8] {'vcol'}, dimensions={0} | all-to-all | bytes 2097152 | tf_op jit(solution)/shard_map/all_to_all | solution.py:75
  331.4 0.5 broadcast.57
  331.9 3.1 reduce
  335.1 0.8 reshape.66
  335.9 0.2 bitcast_bitcast_fusion
  336.1 0.2 copy.92
  336.4 2.5 copy.93
  (4 shorter events, 0.0 us)
Async XLA Ops:
  6.5 104.9 %copy-start.4 = (s32[64,2]{0,1:T(2,128)S(1)}, s32[64,2]{0,1:T(2,128)}, u32[]{:S(2)}) copy-start(s32[64,2]{0,1:T(2,128)} %param.4) | copy-start | bytes 1540
  6.5 104.9 %all-gather.15.cloned.1.call-start = ((), (), s32[]{:S(2)}) async-start(), calls=%async_computation.4 | async-start | bytes 9732096 | tf_op jit(solution)/shard_map/all_gather | solution.py:70
  8.4 147.4 %all-gather.13.cloned.1.call-start = ((), (), s32[]{:S(2)}) async-start(), calls=%async_computation.3 | async-start | bytes 2654208 | tf_op jit(solution)/shard_map/all_gather | solution.py:65
  9.2 233.8 %all-gather.11.cloned.1.call-start = ((), (), s32[]{:S(2)}) async-start(), calls=%async_computation.2 | async-start | bytes 9732096 | tf_op jit(solution)/shard_map/all_gather | solution.py:70
  10.0 291.2 %all-gather.9.cloned.1.call-start = ((), (), s32[]{:S(2)}) async-start(), calls=%async_computation.1 | async-start | bytes 2654208 | tf_op jit(solution)/shard_map/all_gather | solution.py:65
  155.8 5.5 %copy-start.1 = (bf16[1,1,128,8,2304]{4,3,1,0,2:T(8,128)(2,1)S(1)}, bf16[1,1,128,8,2304]{4,3,1,0,2:T(8,128)(2,1)}, u32[]{:S(2)}) copy-start(bf16[1,1,128,8,2304]{4,3,1,0,2:T(8,128)(2,1)} %get-tuple-element.11) | copy-start | bytes 14155780
  155.8 5.5 %copy-start.3 = (bf16[1,2,32,8,2304]{4,3,1,0,2:T(8,128)(2,1)S(1)}, bf16[1,2,32,8,2304]{4,3,1,0,2:T(8,128)(2,1)}, u32[]{:S(2)}) copy-start(bf16[1,2,32,8,2304]{4,3,1,0,2:T(8,128)(2,1)} %all-gather.13.cloned.1.call-done) | copy-start | bytes 7077892
  301.2 5.5 %copy-start = (bf16[1,1,128,8,2304]{4,3,1,0,2:T(8,128)(2,1)S(1)}, bf16[1,1,128,8,2304]{4,3,1,0,2:T(8,128)(2,1)}, u32[]{:S(2)}) copy-start(bf16[1,1,128,8,2304]{4,3,1,0,2:T(8,128)(2,1)} %get-tuple-element.9) | copy-start | bytes 14155780
  301.2 5.5 %copy-start.2 = (bf16[1,2,32,8,2304]{4,3,1,0,2:T(8,128)(2,1)S(1)}, bf16[1,2,32,8,2304]{4,3,1,0,2:T(8,128)(2,1)}, u32[]{:S(2)}) copy-start(bf16[1,2,32,8,2304]{4,3,1,0,2:T(8,128)(2,1)} %all-gather.9.cloned.1.call-done) | copy-start | bytes 7077892
Sparse Core Ops, SparseCore 0:
  9.9 87.5 all-gather.14
  99.3 56.5 all-gather.12
  158.4 84.5 all-gather.10
  244.6 56.5 all-gather.8
where the time goes:
time: 348 us; the launch traced here: 345 us
  waiting for transfers between devices  167 us (48%)
  blocking collectives  106 us (30%)
  local copies, waits for them, and re-layouts  30 us (9%)
  between operations  23.6 us (7%)
  matrix products  16.4 us (5%)
    psum x1, blocking collectives, broadcast(): return lax.psum(block, axis)  87 us
    all_gather x2, waiting for transfers between devices, on_device(): rows = lax.all_gather(slabs[k], 'vcol', axis=1, tiled=True)  86.4 us
    all_gather x2, waiting for transfers between devices, on_device(): lax.all_gather(slabs[k], 'vrow', axis=1, tiled=True)  78.9 us
    all_to_all x1, blocking collectives, on_device(): lax.all_to_all(shaped, 'vcol', split_axis=2, concat_axis=4, tiled=True)  18.6 us
    slice x2, local copies, waits for them, and re-layouts, ladder_part(): piece_d = piece[0, 1].reshape(count_b * BLK, depth)  16.2 us
    dot_general x2, matrix products, ladder_part(): lax.dot_general(rows_d, piece_c, (((1,), (1,)), ((), ())), preferred_elem...  8.84 us
  transfers between devices with their start and end apart: 4, of which 3 were waited for; matrix products, arithmetic and copies ran while one was open for 8% of the time, Pallas kernels for 0%

commit v1 on v0

v1 whole, which is shorter than its diff:
```python
import jax
import jax.numpy as jnp
import numpy as np
from jax import lax
from jax.experimental import pallas as pl
from jax.experimental.pallas import tpu as pltpu
from jax.sharding import PartitionSpec as P

BLK = 8
P_SIZE = 64
STEPS = 2
AXES = ("vrow", "vcol")
X, Y, Z, CORES = 4, 4, 8, 2
DEPTH = 2304
OWN = 4


SMEM = pl.BlockSpec(memory_space=pltpu.SMEM)
VMEM = pl.BlockSpec(memory_space=pltpu.VMEM)
HBM = pl.BlockSpec(memory_space=pl.ANY)


def coords(me):
    return me >> 1 & 3, me >> 4 & 3, me >> 6 << 1 | me & 1, me >> 3 & 1


def flat(x, y, z, c):
    x, y, z, c = x % X, y % Y, z % Z, c % CORES
    return z // 2 << 6 | y << 4 | c << 3 | x << 1 | z % 2


def send(block, where):
    pairs = []
    for me in range(X * Y * Z * CORES):
        pairs.append((me, flat(*where(*coords(me)))))
    return lax.ppermute(block, AXES, pairs)


def rehome(x, y, z, c):
    return x, z % 2 * 2 + y % 2, z // 2 * 2 + y // 2, c


def blocks_kernel(me, offsets, amplitudes, _, out, window, sem):
    out[...] = jnp.zeros_like(out)
    for j in range(2 * STEPS):
        first, second = offsets[j // 2, j % 2], offsets[j // 2, 1 - j % 2]
        row, at_lane = first & 31, second & 127

        @pl.when(me[0] == (first >> 5 << 3 | second >> 7))
        def _(j=j, row=row, at_lane=at_lane):
            rows = pl.ds(pl.multiple_of(row & 16, 16), 16)
            copy = pltpu.make_async_copy(amplitudes.at[:, rows, :], window, sem)
            copy.start()
            copy.wait()
            block = window[...].astype(jnp.float32)
            block = jnp.where(row & 8 == 0, block[:, :8], block[:, 8:])
            lane = lax.broadcasted_iota(jnp.int32, (P_SIZE, 128), 1)
            total = jnp.zeros((P_SIZE, 128), jnp.float32)
            for r in range(BLK):
                line = jnp.where((lane >= at_lane) & (lane < at_lane + BLK), block[:, r], 0.0)
                shift = (128 + j % 2 * 64 + r * BLK - at_lane) & 127
                total = total + pltpu.roll(line, shift, 1)
            total = total.astype(jnp.bfloat16)
            for n in range(4):
                at = 128 * (j // 2 * 4 + n)
                out[:, at : at + 128] += total[16 * n : 16 * n + 16]


def own_blocks(me, offsets, amplitudes, rows):
    return pl.pallas_call(
        blocks_kernel,
        out_shape=jax.ShapeDtypeStruct((16, 1024), jnp.bfloat16),
        in_specs=[SMEM, SMEM, HBM, HBM],
        out_specs=VMEM,
        scratch_shapes=[
            pltpu.VMEM((P_SIZE, 16, 128), jnp.bfloat16),
            pltpu.SemaphoreType.DMA(()),
        ],
        compiler_params=pltpu.CompilerParams(vmem_limit_bytes=4 << 20),
        name="blocks",
    )(me, offsets, amplitudes, rows)


def one_hot(to, dtype):
    lane = lax.broadcasted_iota(jnp.int32, (128, 128), 0)
    return jnp.where(to(lane) == lax.broadcasted_iota(jnp.int32, (128, 128), 1), 1.0, 0.0).astype(
        dtype
    )


def ladder_kernel(me, offdiag, swap, a_in, *refs):
    b_in = refs[0:4]
    keep, give = refs[4:6]
    a_all, b_all, m_all, tail, sems = refs[6:]
    x, y, z, c = coords(me[0])
    copies = []
    for j in range(8):
        at = (((j // 2 - (z >> 1)) & 3) * 2 + j % 2) * 64
        copies.append(
            pltpu.make_async_copy(
                a_in.at[pl.ds(64 * j, 64), :],
                a_all.at[pl.ds(pl.multiple_of(at, 64), 64), :],
                sems.at[j],
            )
        )
    for d in range(BLK):
        for j in range(4):
            copies.append(
                pltpu.make_async_copy(
                    b_in[j].at[pl.ds(32 * d, 32), :],
                    b_all.at[d, pl.ds(32 * j, 32), :],
                    sems.at[8 + d * 4 + j],
                )
            )
    for j in range(4):
        copies.append(
            pltpu.make_async_copy(
                b_in[j].at[pl.ds(256, 16), pl.ds(0, 1024)], tail.at[j], sems.at[40 + j]
            )
        )
    for copy in copies:
        copy.start()
    for copy in copies[:8]:
        copy.wait()
    for d in range(0, BLK, 2):
        for copy in copies[8 + 4 * d : 16 + 4 * d]:
            copy.wait()
        cols = b_all[d : d + 2].reshape(256, DEPTH)
        m = lax.dot_general(
            a_all[...], cols, (((1,), (1,)), ((), ())), preferred_element_type=jnp.float32
        )
        m_all[:, d] = m[:, :128].reshape(64, BLK, 128)
        m_all[:, d + 1] = m[:, 128:].reshape(64, BLK, 128)
    for copy in copies[40:]:
        copy.wait()
    t = tail[...].astype(jnp.float32)
    t = t[0] + t[1] + t[2] + t[3]
    parts = []
    for n in range(4):
        parts.append(
            jnp.where(c == 0, t[:, 128 * n : 128 * n + 128], t[:, 128 * n + 512 : 128 * n + 640])
        )
    t = jnp.concatenate(parts).astype(jnp.bfloat16)
    t = jnp.dot(t, swap[...], preferred_element_type=jnp.float32)
    forward, mirror = t[:, :64], t[:, 64:]
    plus = 0.5 * (forward + mirror)
    minus = 0.5 * (forward - mirror) * offdiag[:, :64]
    u = jnp.concatenate([plus + minus, plus - minus])
    hi = u.astype(jnp.bfloat16)
    lo = (u - hi.astype(jnp.float32)).astype(jnp.bfloat16)
    left = jnp.concatenate([hi, hi, lo], axis=1)

    def target(lane):
        near, far = lane >> 3 & 3, lane >> 5
        src_x = (x - jnp.where(c == 0, near, far)) & 3
        src_y = (y - jnp.where(c == 0, far, near)) & 3
        return (
            (src_y >> 1) * 64
            + ((src_y ^ y) & 1) * 32
            + ((lane >> 2 ^ c) & 1) * 16
            + src_x * 4
            + (lane & 3)
        )

    order = one_hot(target, jnp.bfloat16)
    for g in range(32):
        w = m_all[2 * g : 2 * g + 2].reshape(128, 128)
        hi = w.astype(jnp.bfloat16)
        lo = (w - hi.astype(jnp.float32)).astype(jnp.bfloat16)
        both = jnp.dot(
            jnp.concatenate([hi, lo]), order, preferred_element_type=jnp.float32
        ).astype(jnp.bfloat16)
        parts = []
        for n in range(2):
            hi, lo = both[64 * n : 64 * n + 64], both[128 + 64 * n : 192 + 64 * n]
            parts.append(jnp.concatenate([hi, lo, hi]))
        res = jnp.dot(left, jnp.concatenate(parts, axis=1), preferred_element_type=jnp.float32)
        kz, zl, ec, i = g // 8, g // 4 % 2, g // 2 % 2, g % 2 * 2
        at = 8 * ((1 - c) if ec else c) + 4 * zl + i
        x0, x1 = res[64:, :128], res[64:, 128:]
        top = jnp.concatenate([x0[:, :64], x1[:, :64]], axis=1)
        bottom = jnp.concatenate([x0[:, 64:], x1[:, 64:]], axis=1)
        turned = jnp.concatenate([top, bottom]).T
        kx = (kz + (z >> 1) - x) & 3
        for n in range(2):
            one = res[:64, 128 * n : 128 * n + 128].reshape(4, 16, 128)
            two = turned[64 * n : 64 * n + 64].reshape(4, 16, 128)
            keep[jnp.where(c == 0, kz, kx), at + n] = jnp.where(c == 0, one, two)
            give[jnp.where(c == 0, kx, kz), at + n] = jnp.where(c == 0, two, one)


def ladder(me, offdiag, swap, rows, cols):
    f32, bf16 = jnp.float32, jnp.bfloat16
    return pl.pallas_call(
        ladder_kernel,
        out_shape=[jax.ShapeDtypeStruct((4, 16, 4, 16, 128), f32)] * 2,
        in_specs=[SMEM, VMEM, VMEM] + [HBM] * 5,
        out_specs=[VMEM] * 2,
        scratch_shapes=[
            pltpu.VMEM((512, DEPTH), bf16),
            pltpu.VMEM((BLK, 128, DEPTH), bf16),
            pltpu.VMEM((64, BLK, BLK, 128), f32),
            pltpu.VMEM((4, 16, 1024), bf16),
            pltpu.SemaphoreType.DMA((44,)),
        ],
        compiler_params=pltpu.CompilerParams(vmem_limit_bytes=20 << 20),
        name="ladder",
    )(me, offdiag, swap, rows, *cols)


def route_kernel(me, *refs):
    got, out = refs[:4], refs[4:8]
    x, _, z, c = coords(me[0])
    for shift in range(4):

        @pl.when((c == 0) & ((((z >> 1) - x) & 3) == shift))
        def _(shift=shift):
            for j in range(4):
                out[j][...] = got[(shift - j) % 4][...]

    @pl.when(c == 1)
    def _():
        for e in range(2):
            for k in range(4):
                at = 2 * (k % 2)
                out[2 * e + k // 2][:, at : at + 2] = got[k][:, 2 * e : 2 * e + 2]


def route(me, got):
    return pl.pallas_call(
        route_kernel,
        out_shape=[jax.ShapeDtypeStruct(got[0].shape, got[0].dtype)] * 4,
        in_specs=[SMEM] + [VMEM] * 4,
        out_specs=[VMEM] * 4,
        compiler_params=pltpu.CompilerParams(vmem_limit_bytes=10 << 20),
        name="route",
    )(me, *got)


def split_kernel(me, *refs):
    own, out = refs[:4], refs[4]
    c = coords(me[0])[3]

    @pl.when(c == 0)
    def _():
        for j in range(4):
            out[j] = own[j][8:]

    @pl.when(c == 1)
    def _():
        for j in range(4):
            for a5 in range(2):
                for k in range(2):
                    out[j, :, 2 * a5 + k] = own[j][8 * a5 : 8 * a5 + 8, 2 * k]


def split(me, own):
    return pl.pallas_call(
        split_kernel,
        out_shape=jax.ShapeDtypeStruct((4, 8, 4, 16, 128), own[0].dtype),
        in_specs=[SMEM] + [VMEM] * 4,
        out_specs=VMEM,
        compiler_params=pltpu.CompilerParams(vmem_limit_bytes=10 << 20),
        name="split",
    )(me, *own)


def finish_kernel(me, *refs):
    own, other, out = refs[:4], refs[4], refs[5]
    r1, r2 = refs[6:]
    x, y, _, c = coords(me[0])

    def fetch(core):
        for j in range(4):
            r1[(x - j) & 3] = other[j] if core else own[j][:8]
            for a5 in range(2):
                for k in range(2):
                    if core:
                        block = own[j][8 * a5 : 8 * a5 + 8, 2 * k + 1]
                    else:
                        block = other[j, :, 2 * a5 + k]
                    r2[(y & 1) ^ (j // 2), a5, (x - 2 * (j % 2) - k) & 3] = block

    for core in range(2):

        @pl.when(c == core)
        def _(core=core):
            fetch(core)

    order = one_hot(
        lambda lane: ((lane >> 5 ^ y) & 1) * 64
        + (lane >> 4 & 1) * 32
        + (lane >> 2 & 3) * 8
        + (lane >> 6) * 4
        + (lane & 3),
        jnp.float32,
    )
    for g in range(4):
        t = jnp.dot(
            r1[g].reshape(8 * P_SIZE, 128),
            order,
            preferred_element_type=jnp.float32,
            precision=lax.Precision.HIGHEST,
        )
        for n in range(8):
            out[:, 8 * g + n, :] = t[64 * n : 64 * n + 64]
    for r in range(16):
        t = r2[:, :, :, :, r, :].reshape(128, 128).T
        for b2 in range(2):
            row = r // 4 * 8 + b2 * 4 + r % 4
            out[:, row, :] = out[:, row, :] + t[64 * b2 : 64 * b2 + 64]


def finish(me, own, other):
    f32 = jnp.float32
    return pl.pallas_call(
        finish_kernel,
        out_shape=jax.ShapeDtypeStruct((P_SIZE, 32, 128), f32),
        in_specs=[SMEM] + [VMEM] * 5,
        out_specs=VMEM,
        scratch_shapes=[
            pltpu.VMEM((4, 8, 4, 16, 128), f32),
            pltpu.VMEM((2, 2, 4, 8, 16, 128), f32),
        ],
        compiler_params=pltpu.CompilerParams(vmem_limit_bytes=16 << 20),
        name="finish",
    )(me, *own, other)


def transposed_forward():
    m = np.zeros((128, 128), np.float32)
    for c in range(BLK):
        for d in range(BLK):
            m[c * BLK + d, d * BLK + c] = 1
            m[64 + d * BLK + c, 64 + d * BLK + c] = 1
    return m


def on_device(pairs, offsets, amplitudes, slabs):
    me = lax.axis_index(AXES)
    c = me >> 3 & 1
    core = lambda x, y, z, c: (x, y, z, c + 1)
    slabs = slabs.reshape(STEPS, 2, OWN * BLK, DEPTH)
    mine = lax.dynamic_index_in_dim(slabs, c, 0, keepdims=False)
    yours = lax.dynamic_index_in_dim(slabs, 1 - c, 0, keepdims=False)
    swapped = send(yours[0], core)
    mixed = jnp.concatenate([mine[0], swapped])
    groups = [
        [flat(x, y, z, k) for z in range(Z)]
        for x in range(X)
        for y in range(Y)
        for k in range(CORES)
    ]
    rows = lax.all_gather(mixed, AXES, axis_index_groups=groups, axis=0, tiled=True)
    cols = [
        send(mine[1], rehome),
        send(yours[1], lambda x, y, z, c: rehome(x, y, z, c + 1)),
    ]
    me = me[None]
    t = own_blocks(me, offsets, amplitudes, mixed)
    t = (
        t
        + send(t, core)
        + send(t, lambda x, y, z, c: (x, y, z ^ 1, c))
        + send(t, lambda x, y, z, c: (x, y, z ^ 1, c + 1))
    )

    def near(n):
        return lambda x, y, z, c: (x + n * (1 - c), y + n * c, z, c)

    def far(n):
        return lambda x, y, z, c: (x + n * c, y + n * (1 - c), z, c)

    first = [jnp.concatenate(cols)]
    first += [send(first[0], near(n)) for n in range(1, 4)]
    t = t + cols[0][:16, :1024] * 0 + cols[1][:16, :1024] * 0
    t = t + sum(send(t, lambda x, y, z, c, n=n: (x, y, z ^ n, c)) for n in (2, 4, 6))
    t = t + sum(send(t, near(n)) for n in range(1, 4))
    t = jnp.pad(t, ((0, 0), (0, DEPTH - 1024)))
    cols = jnp.stack([m.reshape(8, BLK, DEPTH) for m in first])
    cols = jnp.transpose(cols, (2, 0, 1, 3)).reshape(256, DEPTH)
    second = [jnp.concatenate([cols, t])]
    second += [send(second[0], far(n)) for n in range(1, 4)]
    offdiag = (pairs[:, 0] != pairs[:, 1]).astype(jnp.float32)
    offdiag = jnp.broadcast_to(offdiag[:, None], (P_SIZE, 128))
    swap = jnp.asarray(transposed_forward(), jnp.bfloat16)
    keep, give = ladder(me, offdiag, swap, rows, second)

    taken = send(give, core)
    got = [keep[0] + taken[0]]
    for k in range(1, 4):
        got.append(
            send(
                keep[k] + taken[k],
                lambda x, y, z, c, k=k: (x + k * c, y, z + 2 * k * (1 - c), c),
            )
        )

    def onward(j):
        def where(x, y, z, c):
            if c == 0:
                return x + j, y, z, c
            x, y, z, c = rehome(x, y, z, c)
            return x, y ^ (j // 2), z, c

        return where

    own = [send(piece, onward(j)) for j, piece in enumerate(route(me, got))]
    return finish(me, own, send(split(me, own), core))


def solution(mesh):
    in_specs = (P(), P(), P(None, "vrow", "vcol"), P(None, None, ("vrow", "vcol"), None, None))
    out_specs = P(None, "vrow", "vcol")
    return jax.shard_map(
        on_device, mesh=mesh, in_specs=in_specs, out_specs=out_specs, check_vma=False
    )
```

time: 348 us -> 180 us (0.52)
  blocking collectives: 106 us -> 0 us
  waiting for transfers between devices: 167 us -> 89.3 us
  starting transfers between devices: 0.12 us -> 44.2 us
  local copies, waits for them, and re-layouts: 30 us -> 8.84 us
  Pallas kernels: 0 us -> 20.4 us
  matrix products: 16.4 us -> 0 us
  between operations: 23.6 us -> 13.6 us
    all_gather x4 -> x1, waiting for transfers between devices: 165 us -> 0.01 us  [on_device(): lax.all_gather(mixed, AXES, axis_index_groups=groups, axis=0, tiled=True)]
    ppermute x0 -> x27, waiting for transfers between devices: none -> 89.3 us  [send(): return lax.ppermute(block, AXES, pairs)]
    psum x1 -> x0, blocking collectives: 87 us -> none  [broadcast(): return lax.psum(block, axis)]
    ppermute x0 -> x27, starting transfers between devices: none -> 44.2 us  [send(): return lax.ppermute(block, AXES, pairs)]
    pallas_call x0 -> x5, Pallas kernels: none -> 20.4 us  [the longest x1 15.2 us: ladder(): pl.pallas_call(ladder_kernel, out_shape=[jax.ShapeDtypeStruct((4, 16, 4,...]
    slice x4 -> x0, local copies, waits for them, and re-layouts: 18.8 us -> none  [the longest x2 16.2 us: ladder_part(): piece_d = piece[0, 1].reshape(count_b * BLK, depth)]
    all_to_all x1 -> x0, blocking collectives: 18.6 us -> none  [on_device(): lax.all_to_all(shaped, 'vcol', split_axis=2, concat_axis=4, tiled=True)]
    dot_general x8 -> x0, matrix products: 16.4 us -> none  [the longest x2 8.84 us: ladder_part(): lax.dot_general(rows_d, piece_c, (((1,), (1,)), ((), ())), preferred_elem...]
  transfers between devices with their start and end apart: 4 -> 28, of which waited for: 3 -> 16; matrix products, arithmetic and copies ran while one was open for 8% -> 0% of each run, Pallas kernels for 0% -> 0%
where the time goes in v1:
time: 180 us; the launch traced here: 178 us
  waiting for transfers between devices  89.3 us (50%)
  starting transfers between devices  44.2 us (25%)
  Pallas kernels  20.4 us (11%)
  between operations  13.6 us (8%)
  local copies, waits for them, and re-layouts  8.84 us (5%)
    ppermute x27, waiting for transfers between devices, send(): return lax.ppermute(block, AXES, pairs)  89.3 us
    ppermute x27, starting transfers between devices, send(): return lax.ppermute(block, AXES, pairs)  44.2 us
    pallas_call x1, Pallas kernels, ladder(): pl.pallas_call(ladder_kernel, out_shape=[jax.ShapeDtypeStruct((4, 16, 4,...  15.2 us
    unnamed x21, local copies, waits for them, and re-layouts  7.34 us
    pallas_call x1, Pallas kernels, finish(): pl.pallas_call(finish_kernel, out_shape=jax.ShapeDtypeStruct((P_SIZE, 32,...  4.46 us
  transfers between devices with their start and end apart: 28, of which 16 were waited for; matrix products, arithmetic and copies ran while one was open for 0% of the time, Pallas kernels for 0%

profile of v1, /device:TPU:33, one launch (start us, length us, event | category | flops | bytes accessed | tf_op | source)
XLA Modules:
  0.0 177.7 jit_solution(1818307422424258325)
XLA Ops:
  6.5 1.2 dynamic-slice_bitcast_fusion.1
  7.8 0.8 collective-permute-start
  8.5 1.0 collective-permute-done
  9.5 0.7 pad_maximum_fusion._
  10.3 0.0 all-gather.2.cloned.1.call-update
  10.3 4.4 %collective-permute-start.1 = (bf16[32,2304]{1,0:T(8,128)(2,1)S(1)}, bf16[32,2304]{1,0:T(8,128)(2,1)S(1)}, u32[]{:S(2)}, u32[]{:S(2)}) collective-permute-start(bf16[32,2304]{1,0:T(8,128)(2,1)S(1)} %get-tuple-element.21), channel_id=1, source_target_pairs={{0,0},{1,32},{2,2},{3,34},{4,4},{5,36},{6,6},{7,38},{8,8},{9,40},{... | collective-permute-start | bytes 442376 | tf_op jit(solution)/shard_map/ppermute | solution.py:36
  14.7 2.0 %collective-permute-start.2 = (bf16[32,2304]{1,0:T(8,128)(2,1)S(1)}, bf16[32,2304]{1,0:T(8,128)(2,1)S(1)}, u32[]{:S(2)}, u32[]{:S(2)}) collective-permute-start(bf16[32,2304]{1,0:T(8,128)(2,1)S(1)} %get-tuple-element.24), channel_id=1, source_target_pairs={{0,8},{1,40},{2,10},{3,42},{4,12},{5,44},{6,14},{7,46},{8,0},{9,32... | collective-permute-start | bytes 442376 | tf_op jit(solution)/shard_map/ppermute | solution.py:36
  16.7 1.0 copy-done
  17.7 0.6 blocks.1
  18.3 0.1 collective-permute-start.8
  18.4 1.2 collective-permute-start.7
  19.6 0.9 collective-permute-start.6
  20.5 3.1 %collective-permute-done.2 = bf16[32,2304]{1,0:T(8,128)(2,1)S(1)} collective-permute-done((bf16[32,2304]{1,0:T(8,128)(2,1)S(1)}, bf16[32,2304]{1,0:T(8,128)(2,1)S(1)}, u32[]{:S(2)}, u32[]{:S(2)}) %collective-permute-start.2) | collective-permute-done | bytes 147488 | tf_op jit(solution)/shard_map/ppermute | solution.py:36
  23.6 6.0 %collective-permute-start.11 = (bf16[16,1024]{1,0:T(8,128)(2,1)S(1)}, bf16[16,1024]{1,0:T(8,128)(2,1)S(1)}, u32[]{:S(2)}, u32[]{:S(2)}) collective-permute-start(bf16[16,1024]{1,0:T(8,128)(2,1)S(1)} %fusion.6), channel_id=1, source_target_pairs={{0,192},{1,193},{2,194},{3,195},{4,196},{5,197},{6,198},{7,199},{8... | collective-permute-start | bytes 98312 | tf_op jit(solution)/shard_map/ppermute | solution.py:36
  29.6 1.0 collective-permute-start.10
  30.6 1.2 collective-permute-start.9
  31.8 1.7 collective-permute-start.5
  33.5 0.7 collective-permute-start.4
  34.2 0.2 collective-permute-start.3
  34.4 2.6 %collective-permute-done.10 = bf16[16,1024]{1,0:T(8,128)(2,1)S(1)} collective-permute-done((bf16[16,1024]{1,0:T(8,128)(2,1)S(1)}, bf16[16,1024]{1,0:T(8,128)(2,1)S(1)}, u32[]{:S(2)}, u32[]{:S(2)}) %collective-permute-start.10) | collective-permute-done | bytes 32800 | tf_op jit(solution)/shard_map/ppermute | solution.py:36
  37.0 1.7 collective-permute-start.14
  38.7 0.4 collective-permute-start.13
  39.1 2.3 %collective-permute-done.14 = bf16[16,1024]{1,0:T(8,128)(2,1)S(1)} collective-permute-done((bf16[16,1024]{1,0:T(8,128)(2,1)S(1)}, bf16[16,1024]{1,0:T(8,128)(2,1)S(1)}, u32[]{:S(2)}, u32[]{:S(2)}) %collective-permute-start.14) | collective-permute-done | bytes 32800 | tf_op jit(solution)/shard_map/ppermute | solution.py:36
  41.5 1.0 collective-permute-start.12
  42.4 2.0 %collective-permute-done.13 = bf16[16,1024]{1,0:T(8,128)(2,1)S(1)} collective-permute-done((bf16[16,1024]{1,0:T(8,128)(2,1)S(1)}, bf16[16,1024]{1,0:T(8,128)(2,1)S(1)}, u32[]{:S(2)}, u32[]{:S(2)}) %collective-permute-start.13) | collective-permute-done | bytes 32800 | tf_op jit(solution)/shard_map/ppermute | solution.py:36
  44.4 1.6 collective-permute-done.12
  46.1 0.2 maximum_bitcast_fusion
  46.2 0.2 copy.6
  46.4 0.0 copy-start.9
  46.5 0.0 copy-start.7
  46.5 0.1 fusion.1.refs_0_
  46.6 2.4 %collective-permute-start.17 = (bf16[272,2304]{1,0:T(8,128)(2,1)S(1)}, bf16[272,2304]{1,0:T(8,128)(2,1)S(1)}, u32[]{:S(2)}, u32[]{:S(2)}) collective-permute-start(bf16[272,2304]{1,0:T(8,128)(2,1)S(1)} %fusion.1.refs_0_), channel_id=1, source_target_pairs={{0,48},{1,49},{2,50},{3,51},{4,52},{5,53},{6,54},{7,55},{8,14},{9,... | collective-permute-start | bytes 3760136 | tf_op jit(solution)/shard_map/ppermute | solution.py:36
  48.9 0.3 collective-permute-start.16
  49.2 0.4 collective-permute-start.15
  49.6 26.7 %collective-permute-done.17.refs_3_ = bf16[272,2304]{1,0:T(8,128)(2,1)S(1)} collective-permute-done((bf16[272,2304]{1,0:T(8,128)(2,1)S(1)}, bf16[272,2304]{1,0:T(8,128)(2,1)S(1)}, u32[]{:S(2)}, u32[]{:S(2)}) %collective-permute-start.17) | collective-permute-done | bytes 1253408 | tf_op jit(solution)/shard_map/ppermute | solution.py:36
  76.3 1.0 copy-done.2
  77.3 2.6 %collective-permute-done.15.refs_1_ = bf16[272,2304]{1,0:T(8,128)(2,1)S(1)} collective-permute-done((bf16[272,2304]{1,0:T(8,128)(2,1)S(1)}, bf16[272,2304]{1,0:T(8,128)(2,1)S(1)}, u32[]{:S(2)}, u32[]{:S(2)}) %collective-permute-start.15) | collective-permute-done | bytes 1253408 | tf_op jit(solution)/shard_map/ppermute | solution.py:36
  80.0 1.0 copy-done.4
  81.0 0.1 broadcast_in_dim.17.offdiag
  81.1 1.7 copy-done.1
  82.8 1.3 copy-done.3
  84.1 1.3 copy-done.5
  85.4 15.2 %ladder.1 = (f32[4,16,4,16,128]{4,3,2,1,0:T(8,128)S(1)}, f32[4,16,4,16,128]{4,3,2,1,0:T(8,128)S(1)}) custom-call(s32[1]{0:T(128)} %bitcast.me, f32[64,128]{1,0:T(8,128)S(1)} %broadcast_in_dim.17.offdiag, bf16[128,128]{1,0:T(8,128)(2,1)S(1)} %copy-done.7, bf16[512,2304]{1,0:T(8,128)(2,1)S(1)} %copy-done.1, bf16[272,2304]{1,0:T(8,128)(2,1)S(1)} %fusion.1.refs_0_, ...), custom_call_target="tpu_custom_call" | custom-call | tf_op jit(solution)/shard_map/ladder/pallas_call | solution.py:194
  100.5 3.6 %collective-permute-start.18 = (f32[4,16,4,16,128]{4,3,2,1,0:T(8,128)S(1)}, f32[4,16,4,16,128]{4,3,2,1,0:T(8,128)S(1)}, u32[]{:S(2)}, u32[]{:S(2)}) collective-permute-start(f32[4,16,4,16,128]{4,3,2,1,0:T(8,128)S(1)} %get-tuple-element.12), channel_id=1, source_target_pairs={{0,8},{1,9},{2,10},{3,11},{4,12},{5,13},{6,14},{7,15},{8,0},{9,1},... | collective-permute-start | bytes 6291464 | tf_op jit(solution)/shard_map/ppermute | solution.py:36
  104.2 3.8 %collective-permute-done.18 = f32[4,16,4,16,128]{4,3,2,1,0:T(8,128)S(1)} collective-permute-done((f32[4,16,4,16,128]{4,3,2,1,0:T(8,128)S(1)}, f32[4,16,4,16,128]{4,3,2,1,0:T(8,128)S(1)}, u32[]{:S(2)}, u32[]{:S(2)}) %collective-permute-start.18) | collective-permute-done | bytes 2097184 | tf_op jit(solution)/shard_map/ppermute | solution.py:36
  107.9 0.4 fusion.2
  108.3 1.8 %collective-permute-start.21 = (f32[16,4,16,128]{3,2,1,0:T(8,128)S(1)}, f32[16,4,16,128]{3,2,1,0:T(8,128)S(1)}, u32[]{:S(2)}, u32[]{:S(2)}) collective-permute-start(f32[16,4,16,128]{3,2,1,0:T(8,128)S(1)} %get-tuple-element.17), channel_id=1, source_target_pairs={{0,192},{1,193},{2,194},{3,195},{4,196},{5,197},{6,198},{7,199},{8... | collective-permute-start | bytes 1572872 | tf_op jit(solution)/shard_map/ppermute | solution.py:36
  110.2 0.2 collective-permute-start.20
  110.4 0.5 collective-permute-start.19
  110.8 11.1 %collective-permute-done.21.refs_3_ = f32[16,4,16,128]{3,2,1,0:T(8,128)S(1)} collective-permute-done((f32[16,4,16,128]{3,2,1,0:T(8,128)S(1)}, f32[16,4,16,128]{3,2,1,0:T(8,128)S(1)}, u32[]{:S(2)}, u32[]{:S(2)}) %collective-permute-start.21) | collective-permute-done | bytes 524320 | tf_op jit(solution)/shard_map/ppermute | solution.py:36
  121.9 3.6 %collective-permute-done.19.refs_1_ = f32[16,4,16,128]{3,2,1,0:T(8,128)S(1)} collective-permute-done((f32[16,4,16,128]{3,2,1,0:T(8,128)S(1)}, f32[16,4,16,128]{3,2,1,0:T(8,128)S(1)}, u32[]{:S(2)}, u32[]{:S(2)}) %collective-permute-start.19) | collective-permute-done | bytes 524320 | tf_op jit(solution)/shard_map/ppermute | solution.py:36
  125.5 0.1 route.1
  125.7 5.4 %collective-permute-start.22 = (f32[16,4,16,128]{3,2,1,0:T(8,128)S(1)}, f32[16,4,16,128]{3,2,1,0:T(8,128)S(1)}, u32[]{:S(2)}, u32[]{:S(2)}) collective-permute-start(f32[16,4,16,128]{3,2,1,0:T(8,128)S(1)} %get-tuple-element.13), channel_id=1, source_target_pairs={{0,0},{1,1},{2,2},{3,3},{4,4},{5,5},{6,6},{7,7},{8,8},{9,40},{10,1... | collective-permute-start | bytes 1572872 | tf_op jit(solution)/shard_map/ppermute | solution.py:36
  131.1 2.3 %collective-permute-start.23 = (f32[16,4,16,128]{3,2,1,0:T(8,128)S(1)}, f32[16,4,16,128]{3,2,1,0:T(8,128)S(1)}, u32[]{:S(2)}, u32[]{:S(2)}) collective-permute-start(f32[16,4,16,128]{3,2,1,0:T(8,128)S(1)} %get-tuple-element.14), channel_id=1, source_target_pairs={{0,2},{1,3},{2,4},{3,5},{4,6},{5,7},{6,0},{7,1},{8,8},{9,40},{10,1... | collective-permute-start | bytes 1572872 | tf_op jit(solution)/shard_map/ppermute | solution.py:36
  133.4 3.8 %collective-permute-start.24 = (f32[16,4,16,128]{3,2,1,0:T(8,128)S(1)}, f32[16,4,16,128]{3,2,1,0:T(8,128)S(1)}, u32[]{:S(2)}, u32[]{:S(2)}) collective-permute-start(f32[16,4,16,128]{3,2,1,0:T(8,128)S(1)} %get-tuple-element.15), channel_id=1, source_target_pairs={{0,4},{1,5},{2,6},{3,7},{4,0},{5,1},{6,2},{7,3},{8,24},{9,56},{10,... | collective-permute-start | bytes 1572872 | tf_op jit(solution)/shard_map/ppermute | solution.py:36
  137.2 0.1 collective-permute-start.25
  137.3 7.8 %collective-permute-done.22.refs_0_ = f32[16,4,16,128]{3,2,1,0:T(8,128)S(1)} collective-permute-done((f32[16,4,16,128]{3,2,1,0:T(8,128)S(1)}, f32[16,4,16,128]{3,2,1,0:T(8,128)S(1)}, u32[]{:S(2)}, u32[]{:S(2)}) %collective-permute-start.22) | collective-permute-done | bytes 524320 | tf_op jit(solution)/shard_map/ppermute | solution.py:36
  145.1 6.6 %collective-permute-done.23.refs_1_ = f32[16,4,16,128]{3,2,1,0:T(8,128)S(1)} collective-permute-done((f32[16,4,16,128]{3,2,1,0:T(8,128)S(1)}, f32[16,4,16,128]{3,2,1,0:T(8,128)S(1)}, u32[]{:S(2)}, u32[]{:S(2)}) %collective-permute-start.23) | collective-permute-done | bytes 524320 | tf_op jit(solution)/shard_map/ppermute | solution.py:36
  151.7 6.6 %collective-permute-done.24.refs_2_ = f32[16,4,16,128]{3,2,1,0:T(8,128)S(1)} collective-permute-done((f32[16,4,16,128]{3,2,1,0:T(8,128)S(1)}, f32[16,4,16,128]{3,2,1,0:T(8,128)S(1)}, u32[]{:S(2)}, u32[]{:S(2)}) %collective-permute-start.24) | collective-permute-done | bytes 524320 | tf_op jit(solution)/shard_map/ppermute | solution.py:36
  158.2 5.3 %collective-permute-done.25.refs_3_ = f32[16,4,16,128]{3,2,1,0:T(8,128)S(1)} collective-permute-done((f32[16,4,16,128]{3,2,1,0:T(8,128)S(1)}, f32[16,4,16,128]{3,2,1,0:T(8,128)S(1)}, u32[]{:S(2)}, u32[]{:S(2)}) %collective-permute-start.25) | collective-permute-done | bytes 524320 | tf_op jit(solution)/shard_map/ppermute | solution.py:36
  163.6 0.1 split.1
  163.6 0.1 collective-permute-start.26
  163.7 2.6 %collective-permute-done.26.refs_4_ = f32[4,8,4,16,128]{4,3,2,1,0:T(8,128)S(1)} collective-permute-done((f32[4,8,4,16,128]{4,3,2,1,0:T(8,128)S(1)}, f32[4,8,4,16,128]{4,3,2,1,0:T(8,128)S(1)}, u32[]{:S(2)}, u32[]{:S(2)}) %collective-permute-start.26) | collective-permute-done | bytes 1048608 | tf_op jit(solution)/shard_map/ppermute | solution.py:36
  166.4 4.5 %finish.1 = f32[64,32,128]{2,1,0:T(8,128)} custom-call(s32[1]{0:T(128)} %bitcast.me, f32[16,4,16,128]{3,2,1,0:T(8,128)S(1)} %collective-permute-done.22.refs_0_, f32[16,4,16,128]{3,2,1,0:T(8,128)S(1)} %collective-permute-done.23.refs_1_, f32[16,4,16,128]{3,2,1,0:T(8,128)S(1)} %collective-permute-done.24.refs_2_, ...), custom_call_target="tpu_custom_call" | custom-call | tf_op jit(solution)/shard_map/finish/pallas_call | solution.py:316
  (31 shorter events, 0.1 us)
Async XLA Ops:
  6.5 10.2 %copy-start.6 = (bf16[64,32,128]{2,1,0:T(8,128)(2,1)S(1)}, bf16[64,32,128]{2,1,0:T(8,128)(2,1)}, u32[]{:S(2)}) copy-start(bf16[64,32,128]{2,1,0:T(8,128)(2,1)} %amplitudes.1) | copy-start | bytes 1572868
  6.5 10.2 %copy-start.8 = (s32[2,2]{1,0:T(2,128)S(1)}, s32[2,2]{1,0:T(2,128)}, u32[]{:S(2)}) copy-start(s32[2,2]{1,0:T(2,128)} %offsets.1) | copy-start | bytes 52
  6.5 74.5 %all-gather.2.cloned.1.call-start = ((), (), s32[]{:S(2)}) async-start(), calls=%async_computation | async-start | bytes 2654208 | tf_op jit(solution)/shard_map/all_gather | solution.py:354
  7.8 1.8 collective-permute-start
  10.3 10.2 %collective-permute-start.1 = (bf16[32,2304]{1,0:T(8,128)(2,1)S(1)}, bf16[32,2304]{1,0:T(8,128)(2,1)S(1)}, u32[]{:S(2)}, u32[]{:S(2)}) collective-permute-start(bf16[32,2304]{1,0:T(8,128)(2,1)S(1)} %get-tuple-element.21), channel_id=1, source_target_pairs={{0,0},{1,32},{2,2},{3,34},{4,4},{5,36},{6,6},{7,38},{8,8},{9,40},{... | collective-permute-start | bytes 442376 | tf_op jit(solution)/shard_map/ppermute | solution.py:36
  14.7 8.9 %collective-permute-start.2 = (bf16[32,2304]{1,0:T(8,128)(2,1)S(1)}, bf16[32,2304]{1,0:T(8,128)(2,1)S(1)}, u32[]{:S(2)}, u32[]{:S(2)}) collective-permute-start(bf16[32,2304]{1,0:T(8,128)(2,1)S(1)} %get-tuple-element.24), channel_id=1, source_target_pairs={{0,8},{1,40},{2,10},{3,42},{4,12},{5,44},{6,14},{7,46},{8,0},{9,32... | collective-permute-start | bytes 442376 | tf_op jit(solution)/shard_map/ppermute | solution.py:36
  16.7 1.0 copy-start
  18.3 5.3 %collective-permute-start.8 = (bf16[16,1024]{1,0:T(8,128)(2,1)S(1)}, bf16[16,1024]{1,0:T(8,128)(2,1)S(1)}, u32[]{:S(2)}, u32[]{:S(2)}) collective-permute-start(bf16[16,1024]{1,0:T(8,128)(2,1)S(1)} %blocks.1), channel_id=1, source_target_pairs={{0,9},{1,8},{2,11},{3,10},{4,13},{5,12},{6,15},{7,14},{8,1},{9,0},... | collective-permute-start | bytes 98312 | tf_op jit(solution)/shard_map/ppermute | solution.py:36
  18.4 5.3 %collective-permute-start.7 = (bf16[16,1024]{1,0:T(8,128)(2,1)S(1)}, bf16[16,1024]{1,0:T(8,128)(2,1)S(1)}, u32[]{:S(2)}, u32[]{:S(2)}) collective-permute-start(bf16[16,1024]{1,0:T(8,128)(2,1)S(1)} %blocks.1), channel_id=1, source_target_pairs={{0,1},{1,0},{2,3},{3,2},{4,5},{5,4},{6,7},{7,6},{8,9},{9,8},{10,11... | collective-permute-start | bytes 98312 | tf_op jit(solution)/shard_map/ppermute | solution.py:36
  19.6 4.1 %collective-permute-start.6 = (bf16[16,1024]{1,0:T(8,128)(2,1)S(1)}, bf16[16,1024]{1,0:T(8,128)(2,1)S(1)}, u32[]{:S(2)}, u32[]{:S(2)}) collective-permute-start(bf16[16,1024]{1,0:T(8,128)(2,1)S(1)} %blocks.1), channel_id=1, source_target_pairs={{0,8},{1,9},{2,10},{3,11},{4,12},{5,13},{6,14},{7,15},{8,0},{9,1},... | collective-permute-start | bytes 98312 | tf_op jit(solution)/shard_map/ppermute | solution.py:36
  23.6 10.6 %collective-permute-start.11 = (bf16[16,1024]{1,0:T(8,128)(2,1)S(1)}, bf16[16,1024]{1,0:T(8,128)(2,1)S(1)}, u32[]{:S(2)}, u32[]{:S(2)}) collective-permute-start(bf16[16,1024]{1,0:T(8,128)(2,1)S(1)} %fusion.6), channel_id=1, source_target_pairs={{0,192},{1,193},{2,194},{3,195},{4,196},{5,197},{6,198},{7,199},{8... | collective-permute-start | bytes 98312 | tf_op jit(solution)/shard_map/ppermute | solution.py:36
  29.6 7.3 %collective-permute-start.10 = (bf16[16,1024]{1,0:T(8,128)(2,1)S(1)}, bf16[16,1024]{1,0:T(8,128)(2,1)S(1)}, u32[]{:S(2)}, u32[]{:S(2)}) collective-permute-start(bf16[16,1024]{1,0:T(8,128)(2,1)S(1)} %fusion.6), channel_id=1, source_target_pairs={{0,128},{1,129},{2,130},{3,131},{4,132},{5,133},{6,134},{7,135},{8... | collective-permute-start | bytes 98312 | tf_op jit(solution)/shard_map/ppermute | solution.py:36
  30.6 6.4 %collective-permute-start.9 = (bf16[16,1024]{1,0:T(8,128)(2,1)S(1)}, bf16[16,1024]{1,0:T(8,128)(2,1)S(1)}, u32[]{:S(2)}, u32[]{:S(2)}) collective-permute-start(bf16[16,1024]{1,0:T(8,128)(2,1)S(1)} %fusion.6), channel_id=1, source_target_pairs={{0,64},{1,65},{2,66},{3,67},{4,68},{5,69},{6,70},{7,71},{8,72},{9,... | collective-permute-start | bytes 98312 | tf_op jit(solution)/shard_map/ppermute | solution.py:36
  31.8 14.2 %collective-permute-start.5 = (bf16[64,2304]{1,0:T(8,128)(2,1)S(1)}, bf16[64,2304]{1,0:T(8,128)(2,1)S(1)}, u32[]{:S(2)}, u32[]{:S(2)}) collective-permute-start(bf16[64,2304]{1,0:T(8,128)(2,1)S(1)} %constant_dynamic-update-slice_fusion), channel_id=1, source_target_pairs={{0,6},{1,7},{2,0},{3,1},{4,2},{5,3},{6,4},{7,5},{8,56},{9,57},{10,... | collective-permute-start | bytes 884744 | tf_op jit(solution)/shard_map/ppermute | solution.py:36
  33.5 12.6 %collective-permute-start.4 = (bf16[64,2304]{1,0:T(8,128)(2,1)S(1)}, bf16[64,2304]{1,0:T(8,128)(2,1)S(1)}, u32[]{:S(2)}, u32[]{:S(2)}) collective-permute-start(bf16[64,2304]{1,0:T(8,128)(2,1)S(1)} %constant_dynamic-update-slice_fusion), channel_id=1, source_target_pairs={{0,4},{1,5},{2,6},{3,7},{4,0},{5,1},{6,2},{7,3},{8,40},{9,41},{10,... | collective-permute-start | bytes 884744 | tf_op jit(solution)/shard_map/ppermute | solution.py:36
  34.2 11.9 %collective-permute-start.3 = (bf16[64,2304]{1,0:T(8,128)(2,1)S(1)}, bf16[64,2304]{1,0:T(8,128)(2,1)S(1)}, u32[]{:S(2)}, u32[]{:S(2)}) collective-permute-start(bf16[64,2304]{1,0:T(8,128)(2,1)S(1)} %constant_dynamic-update-slice_fusion), channel_id=1, source_target_pairs={{0,2},{1,3},{2,4},{3,5},{4,6},{5,7},{6,0},{7,1},{8,24},{9,25},{10,... | collective-permute-start | bytes 884744 | tf_op jit(solution)/shard_map/ppermute | solution.py:36
  37.0 4.4 %collective-permute-start.14 = (bf16[16,1024]{1,0:T(8,128)(2,1)S(1)}, bf16[16,1024]{1,0:T(8,128)(2,1)S(1)}, u32[]{:S(2)}, u32[]{:S(2)}) collective-permute-start(bf16[16,1024]{1,0:T(8,128)(2,1)S(1)} %add_add_fusion.1), channel_id=1, source_target_pairs={{0,6},{1,7},{2,0},{3,1},{4,2},{5,3},{6,4},{7,5},{8,56},{9,57},{10,... | collective-permute-start | bytes 98312 | tf_op jit(solution)/shard_map/ppermute | solution.py:36
  38.7 5.7 %collective-permute-start.13 = (bf16[16,1024]{1,0:T(8,128)(2,1)S(1)}, bf16[16,1024]{1,0:T(8,128)(2,1)S(1)}, u32[]{:S(2)}, u32[]{:S(2)}) collective-permute-start(bf16[16,1024]{1,0:T(8,128)(2,1)S(1)} %add_add_fusion.1), channel_id=1, source_target_pairs={{0,4},{1,5},{2,6},{3,7},{4,0},{5,1},{6,2},{7,3},{8,40},{9,41},{10,... | collective-permute-start | bytes 98312 | tf_op jit(solution)/shard_map/ppermute | solution.py:36
  41.5 4.6 %collective-permute-start.12 = (bf16[16,1024]{1,0:T(8,128)(2,1)S(1)}, bf16[16,1024]{1,0:T(8,128)(2,1)S(1)}, u32[]{:S(2)}, u32[]{:S(2)}) collective-permute-start(bf16[16,1024]{1,0:T(8,128)(2,1)S(1)} %add_add_fusion.1), channel_id=1, source_target_pairs={{0,2},{1,3},{2,4},{3,5},{4,6},{5,7},{6,0},{7,1},{8,24},{9,25},{10,... | collective-permute-start | bytes 98312 | tf_op jit(solution)/shard_map/ppermute | solution.py:36
  46.4 3.2 %copy-start.9 = (s32[64,2]{0,1:T(2,128)S(1)}, s32[64,2]{0,1:T(2,128)}, u32[]{:S(2)}) copy-start(s32[64,2]{0,1:T(2,128)} %param.5) | copy-start | bytes 1540
  46.5 34.6 %copy-start.7 = (bf16[128,128]{1,0:T(8,128)(2,1)S(1)}, bf16[128,128]{1,0:T(8,128)(2,1)}, u32[]{:S(2)}) copy-start(bf16[128,128]{1,0:T(8,128)(2,1)} %constant.30.clone.swap) | copy-start | bytes 98308
  46.6 29.7 %collective-permute-start.17 = (bf16[272,2304]{1,0:T(8,128)(2,1)S(1)}, bf16[272,2304]{1,0:T(8,128)(2,1)S(1)}, u32[]{:S(2)}, u32[]{:S(2)}) collective-permute-start(bf16[272,2304]{1,0:T(8,128)(2,1)S(1)} %fusion.1.refs_0_), channel_id=1, source_target_pairs={{0,48},{1,49},{2,50},{3,51},{4,52},{5,53},{6,54},{7,55},{8,14},{9,... | collective-permute-start | bytes 3760136 | tf_op jit(solution)/shard_map/ppermute | solution.py:36
  48.9 27.4 %collective-permute-start.16 = (bf16[272,2304]{1,0:T(8,128)(2,1)S(1)}, bf16[272,2304]{1,0:T(8,128)(2,1)S(1)}, u32[]{:S(2)}, u32[]{:S(2)}) collective-permute-start(bf16[272,2304]{1,0:T(8,128)(2,1)S(1)} %fusion.1.refs_0_), channel_id=1, source_target_pairs={{0,32},{1,33},{2,34},{3,35},{4,36},{5,37},{6,38},{7,39},{8,12},{9,... | collective-permute-start | bytes 3760136 | tf_op jit(solution)/shard_map/ppermute | solution.py:36
  49.2 30.8 %collective-permute-start.15 = (bf16[272,2304]{1,0:T(8,128)(2,1)S(1)}, bf16[272,2304]{1,0:T(8,128)(2,1)S(1)}, u32[]{:S(2)}, u32[]{:S(2)}) collective-permute-start(bf16[272,2304]{1,0:T(8,128)(2,1)S(1)} %fusion.1.refs_0_), channel_id=1, source_target_pairs={{0,16},{1,17},{2,18},{3,19},{4,20},{5,21},{6,22},{7,23},{8,10},{9,... | collective-permute-start | bytes 3760136 | tf_op jit(solution)/shard_map/ppermute | solution.py:36
  76.3 1.0 copy-start.2
  80.0 1.0 copy-start.4
  81.1 1.7 copy-start.1
  82.8 1.3 copy-start.3
  84.1 1.3 copy-start.5
  100.5 7.4 %collective-permute-start.18 = (f32[4,16,4,16,128]{4,3,2,1,0:T(8,128)S(1)}, f32[4,16,4,16,128]{4,3,2,1,0:T(8,128)S(1)}, u32[]{:S(2)}, u32[]{:S(2)}) collective-permute-start(f32[4,16,4,16,128]{4,3,2,1,0:T(8,128)S(1)} %get-tuple-element.12), channel_id=1, source_target_pairs={{0,8},{1,9},{2,10},{3,11},{4,12},{5,13},{6,14},{7,15},{8,0},{9,1},... | collective-permute-start | bytes 6291464 | tf_op jit(solution)/shard_map/ppermute | solution.py:36
  108.3 13.6 %collective-permute-start.21 = (f32[16,4,16,128]{3,2,1,0:T(8,128)S(1)}, f32[16,4,16,128]{3,2,1,0:T(8,128)S(1)}, u32[]{:S(2)}, u32[]{:S(2)}) collective-permute-start(f32[16,4,16,128]{3,2,1,0:T(8,128)S(1)} %get-tuple-element.17), channel_id=1, source_target_pairs={{0,192},{1,193},{2,194},{3,195},{4,196},{5,197},{6,198},{7,199},{8... | collective-permute-start | bytes 1572872 | tf_op jit(solution)/shard_map/ppermute | solution.py:36
  110.2 11.7 %collective-permute-start.20 = (f32[16,4,16,128]{3,2,1,0:T(8,128)S(1)}, f32[16,4,16,128]{3,2,1,0:T(8,128)S(1)}, u32[]{:S(2)}, u32[]{:S(2)}) collective-permute-start(f32[16,4,16,128]{3,2,1,0:T(8,128)S(1)} %get-tuple-element.18), channel_id=1, source_target_pairs={{0,128},{1,129},{2,130},{3,131},{4,132},{5,133},{6,134},{7,135},{8... | collective-permute-start | bytes 1572872 | tf_op jit(solution)/shard_map/ppermute | solution.py:36
  110.4 15.2 %collective-permute-start.19 = (f32[16,4,16,128]{3,2,1,0:T(8,128)S(1)}, f32[16,4,16,128]{3,2,1,0:T(8,128)S(1)}, u32[]{:S(2)}, u32[]{:S(2)}) collective-permute-start(f32[16,4,16,128]{3,2,1,0:T(8,128)S(1)} %get-tuple-element.19), channel_id=1, source_target_pairs={{0,64},{1,65},{2,66},{3,67},{4,68},{5,69},{6,70},{7,71},{8,10},{9,... | collective-permute-start | bytes 1572872 | tf_op jit(solution)/shard_map/ppermute | solution.py:36
  125.7 19.4 %collective-permute-start.22 = (f32[16,4,16,128]{3,2,1,0:T(8,128)S(1)}, f32[16,4,16,128]{3,2,1,0:T(8,128)S(1)}, u32[]{:S(2)}, u32[]{:S(2)}) collective-permute-start(f32[16,4,16,128]{3,2,1,0:T(8,128)S(1)} %get-tuple-element.13), channel_id=1, source_target_pairs={{0,0},{1,1},{2,2},{3,3},{4,4},{5,5},{6,6},{7,7},{8,8},{9,40},{10,1... | collective-permute-start | bytes 1572872 | tf_op jit(solution)/shard_map/ppermute | solution.py:36
  131.1 20.6 %collective-permute-start.23 = (f32[16,4,16,128]{3,2,1,0:T(8,128)S(1)}, f32[16,4,16,128]{3,2,1,0:T(8,128)S(1)}, u32[]{:S(2)}, u32[]{:S(2)}) collective-permute-start(f32[16,4,16,128]{3,2,1,0:T(8,128)S(1)} %get-tuple-element.14), channel_id=1, source_target_pairs={{0,2},{1,3},{2,4},{3,5},{4,6},{5,7},{6,0},{7,1},{8,8},{9,40},{10,1... | collective-permute-start | bytes 1572872 | tf_op jit(solution)/shard_map/ppermute | solution.py:36
  133.4 24.9 %collective-permute-start.24 = (f32[16,4,16,128]{3,2,1,0:T(8,128)S(1)}, f32[16,4,16,128]{3,2,1,0:T(8,128)S(1)}, u32[]{:S(2)}, u32[]{:S(2)}) collective-permute-start(f32[16,4,16,128]{3,2,1,0:T(8,128)S(1)} %get-tuple-element.15), channel_id=1, source_target_pairs={{0,4},{1,5},{2,6},{3,7},{4,0},{5,1},{6,2},{7,3},{8,24},{9,56},{10,... | collective-permute-start | bytes 1572872 | tf_op jit(solution)/shard_map/ppermute | solution.py:36
  137.2 26.4 %collective-permute-start.25 = (f32[16,4,16,128]{3,2,1,0:T(8,128)S(1)}, f32[16,4,16,128]{3,2,1,0:T(8,128)S(1)}, u32[]{:S(2)}, u32[]{:S(2)}) collective-permute-start(f32[16,4,16,128]{3,2,1,0:T(8,128)S(1)} %get-tuple-element.16), channel_id=1, source_target_pairs={{0,6},{1,7},{2,0},{3,1},{4,2},{5,3},{6,4},{7,5},{8,24},{9,56},{10,... | collective-permute-start | bytes 1572872 | tf_op jit(solution)/shard_map/ppermute | solution.py:36
  163.6 2.7 %collective-permute-start.26 = (f32[4,8,4,16,128]{4,3,2,1,0:T(8,128)S(1)}, f32[4,8,4,16,128]{4,3,2,1,0:T(8,128)S(1)}, u32[]{:S(2)}, u32[]{:S(2)}) collective-permute-start(f32[4,8,4,16,128]{4,3,2,1,0:T(8,128)S(1)} %split.1), channel_id=1, source_target_pairs={{0,8},{1,9},{2,10},{3,11},{4,12},{5,13},{6,14},{7,15},{8,0},{9,1},... | collective-permute-start | bytes 3145736 | tf_op jit(solution)/shard_map/ppermute | solution.py:36
Sparse Core Ops, SparseCore 0:
  10.4 43.3 all-gather.1

commit v2 on v1

--- a/solution.py
+++ b/solution.py
@@ -203,38 +203,32 @@
             pltpu.VMEM((4, 16, 1024), bf16),
             pltpu.SemaphoreType.DMA((44,)),
         ],
-        compiler_params=pltpu.CompilerParams(vmem_limit_bytes=20 << 20),
+        compiler_params=pltpu.CompilerParams(vmem_limit_bytes=56 << 20),
         name="ladder",
     )(me, offdiag, swap, rows, *cols)
 
 
-def route_kernel(me, *refs):
-    got, out = refs[:4], refs[4:8]
-    x, _, z, c = coords(me[0])
-    for shift in range(4):
-
-        @pl.when((c == 0) & ((((z >> 1) - x) & 3) == shift))
-        def _(shift=shift):
-            for j in range(4):
-                out[j][...] = got[(shift - j) % 4][...]
-
-    @pl.when(c == 1)
-    def _():
-        for e in range(2):
-            for k in range(4):
-                at = 2 * (k % 2)
-                out[2 * e + k // 2][:, at : at + 2] = got[k][:, 2 * e : 2 * e + 2]
+def pack(block):
+    top = jnp.max(jnp.abs(block), axis=0, keepdims=True)
+    power = jnp.clip(jnp.floor(jnp.log2(top)), -100.0, 100.0)
+    return jnp.concatenate([block * jnp.exp2(14.0 - power), power]).astype(jnp.float16)
+
+
+def unpack(block):
+    block = block.astype(jnp.float32)
+    return block[:16] * jnp.exp2(block[16:] - 14.0)
 
 
 def route(me, got):
-    return pl.pallas_call(
-        route_kernel,
-        out_shape=[jax.ShapeDtypeStruct(got[0].shape, got[0].dtype)] * 4,
-        in_specs=[SMEM] + [VMEM] * 4,
-        out_specs=[VMEM] * 4,
-        compiler_params=pltpu.CompilerParams(vmem_limit_bytes=10 << 20),
-        name="route",
-    )(me, *got)
+    x, _, z, c = coords(me)
+    every = jnp.stack(got)
+    out = []
+    for j in range(4):
+        whole = lax.dynamic_index_in_dim(every, ((z >> 1) - x - j) & 3, 0, keepdims=False)
+        e, k = j // 2, j % 2 * 2
+        rows = [got[k + n][:, 2 * e : 2 * e + 2] for n in range(2)]
+        out.append(jnp.where(c == 0, whole, jnp.concatenate(rows, axis=1)))
+    return out
 
 
 def split_kernel(me, *refs):
@@ -373,7 +367,6 @@
 
     first = [jnp.concatenate(cols)]
     first += [send(first[0], near(n)) for n in range(1, 4)]
-    t = t + cols[0][:16, :1024] * 0 + cols[1][:16, :1024] * 0
     t = t + sum(send(t, lambda x, y, z, c, n=n: (x, y, z ^ n, c)) for n in (2, 4, 6))
     t = t + sum(send(t, near(n)) for n in range(1, 4))
     t = jnp.pad(t, ((0, 0), (0, DEPTH - 1024)))
@@ -387,11 +380,11 @@
     keep, give = ladder(me, offdiag, swap, rows, second)
 
     taken = send(give, core)
-    got = [keep[0] + taken[0]]
+    got = [pack(keep[0] + taken[0])]
     for k in range(1, 4):
         got.append(
             send(
-                keep[k] + taken[k],
+                pack(keep[k] + taken[k]),
                 lambda x, y, z, c, k=k: (x + k * c, y, z + 2 * k * (1 - c), c),
             )
         )
@@ -405,7 +398,7 @@
 
         return where
 
-    own = [send(piece, onward(j)) for j, piece in enumerate(route(me, got))]
+    own = [unpack(send(piece, onward(j))) for j, piece in enumerate(route(me[0], got))]
     return finish(me, own, send(split(me, own), core))
 
 

time: 180 us -> 157 us (0.87)
  waiting for transfers between devices: 89.3 us -> 58.1 us
  starting transfers between devices: 44.2 us -> 54.5 us
  local copies, waits for them, and re-layouts: 8.84 us -> 4.39 us
  other arithmetic: 1.4 us -> 5.34 us
  Pallas kernels: 20.4 us -> 18.1 us
    ppermute x27, waiting for transfers between devices: 89.3 us -> 58 us  [send(): return lax.ppermute(block, AXES, pairs)]
    ppermute x27, starting transfers between devices: 44.2 us -> 54.5 us  [send(): return lax.ppermute(block, AXES, pairs)]
    unnamed x21 -> x17, local copies, waits for them, and re-layouts: 7.34 us -> 2.08 us
    reduce_max x0 -> x1, other arithmetic: none -> 2.1 us  [pack(): top = jnp.max(jnp.abs(block), axis=0, keepdims=True)]
    pallas_call x1, Pallas kernels: 15.2 us -> 13.2 us  [ladder(): pl.pallas_call(ladder_kernel, out_shape=[jax.ShapeDtypeStruct((4, 16, 4,...]
  transfers between devices with their start and end apart: 28 -> 28, of which waited for: 16 -> 14; matrix products, arithmetic and copies ran while one was open for 0% -> 1% of each run, Pallas kernels for 0% -> 0%
where the time goes in v2:
time: 157 us; the launch traced here: 154 us
  waiting for transfers between devices  58.1 us (37%)
  starting transfers between devices  54.5 us (35%)
  Pallas kernels  18.1 us (12%)
  between operations  13.8 us (9%)
  other arithmetic  5.34 us (3%)
  local copies, waits for them, and re-layouts  4.39 us (3%)
    ppermute x27, waiting for transfers between devices, send(): return lax.ppermute(block, AXES, pairs)  58 us
    ppermute x27, starting transfers between devices, send(): return lax.ppermute(block, AXES, pairs)  54.5 us
    pallas_call x1, Pallas kernels, ladder(): pl.pallas_call(ladder_kernel, out_shape=[jax.ShapeDtypeStruct((4, 16, 4,...  13.2 us
    pallas_call x1, Pallas kernels, finish(): pl.pallas_call(finish_kernel, out_shape=jax.ShapeDtypeStruct((P_SIZE, 32,...  4.24 us
  transfers between devices with their start and end apart: 28, of which 14 were waited for; matrix products, arithmetic and copies ran while one was open for 1% of the time, Pallas kernels for 0%

profile of v2, /device:TPU:33, one launch (start us, length us, event | category | flops | bytes accessed | tf_op | source)
XLA Modules:
  0.0 154.3 jit_solution(7320790349959043510)
XLA Ops:
  6.5 1.2 dynamic-slice_bitcast_fusion
  7.8 0.8 collective-permute-start
  8.5 1.0 collective-permute-done
  9.5 0.7 pad_maximum_fusion.2._
  10.3 4.4 %collective-permute-start.1 = (bf16[32,2304]{1,0:T(8,128)(2,1)S(1)}, bf16[32,2304]{1,0:T(8,128)(2,1)S(1)}, u32[]{:S(2)}, u32[]{:S(2)}) collective-permute-start(bf16[32,2304]{1,0:T(8,128)(2,1)S(1)} %get-tuple-element.24), channel_id=1, source_target_pairs={{0,0},{1,32},{2,2},{3,34},{4,4},{5,36},{6,6},{7,38},{8,8},{9,40},{... | collective-permute-start | bytes 442376 | tf_op jit(solution)/shard_map/ppermute | solution.py:36
  14.7 2.0 %collective-permute-start.2 = (bf16[32,2304]{1,0:T(8,128)(2,1)S(1)}, bf16[32,2304]{1,0:T(8,128)(2,1)S(1)}, u32[]{:S(2)}, u32[]{:S(2)}) collective-permute-start(bf16[32,2304]{1,0:T(8,128)(2,1)S(1)} %get-tuple-element.21), channel_id=1, source_target_pairs={{0,8},{1,40},{2,10},{3,42},{4,12},{5,44},{6,14},{7,46},{8,0},{9,32... | collective-permute-start | bytes 442376 | tf_op jit(solution)/shard_map/ppermute | solution.py:36
  16.7 1.0 copy-done
  17.7 0.6 blocks.1
  18.3 0.1 collective-permute-start.6
  18.4 0.1 collective-permute-start.7
  18.5 2.0 %collective-permute-start.8 = (bf16[16,1024]{1,0:T(8,128)(2,1)S(1)}, bf16[16,1024]{1,0:T(8,128)(2,1)S(1)}, u32[]{:S(2)}, u32[]{:S(2)}) collective-permute-start(bf16[16,1024]{1,0:T(8,128)(2,1)S(1)} %blocks.1), channel_id=1, source_target_pairs={{0,9},{1,8},{2,11},{3,10},{4,13},{5,12},{6,15},{7,14},{8,1},{9,0},... | collective-permute-start | bytes 98312 | tf_op jit(solution)/shard_map/ppermute | solution.py:36
  20.5 1.0 collective-permute-done.7
  21.5 1.2 collective-permute-done.8
  22.7 6.3 %collective-permute-start.10 = (bf16[16,1024]{1,0:T(8,128)(2,1)S(1)}, bf16[16,1024]{1,0:T(8,128)(2,1)S(1)}, u32[]{:S(2)}, u32[]{:S(2)}) collective-permute-start(bf16[16,1024]{1,0:T(8,128)(2,1)S(1)} %add_add_fusion.2), channel_id=1, source_target_pairs={{0,128},{1,129},{2,130},{3,131},{4,132},{5,133},{6,134},{7,135},{8... | collective-permute-start | bytes 98312 | tf_op jit(solution)/shard_map/ppermute | solution.py:36
  29.1 0.1 collective-permute-start.11
  29.2 2.0 %collective-permute-start.9 = (bf16[16,1024]{1,0:T(8,128)(2,1)S(1)}, bf16[16,1024]{1,0:T(8,128)(2,1)S(1)}, u32[]{:S(2)}, u32[]{:S(2)}) collective-permute-start(bf16[16,1024]{1,0:T(8,128)(2,1)S(1)} %add_add_fusion.2), channel_id=1, source_target_pairs={{0,64},{1,65},{2,66},{3,67},{4,68},{5,69},{6,70},{7,71},{8,72},{9,... | collective-permute-start | bytes 98312 | tf_op jit(solution)/shard_map/ppermute | solution.py:36
  31.2 0.3 collective-permute-start.3
  31.5 3.3 %collective-permute-start.4 = (bf16[64,2304]{1,0:T(8,128)(2,1)S(1)}, bf16[64,2304]{1,0:T(8,128)(2,1)S(1)}, u32[]{:S(2)}, u32[]{:S(2)}) collective-permute-start(bf16[64,2304]{1,0:T(8,128)(2,1)S(1)} %constant_dynamic-update-slice_fusion), channel_id=1, source_target_pairs={{0,4},{1,5},{2,6},{3,7},{4,0},{5,1},{6,2},{7,3},{8,40},{9,41},{10,... | collective-permute-start | bytes 884744 | tf_op jit(solution)/shard_map/ppermute | solution.py:36
  34.8 0.9 collective-permute-start.5
  35.7 0.6 collective-permute-start.12
  36.4 2.6 %collective-permute-start.13 = (bf16[16,1024]{1,0:T(8,128)(2,1)S(1)}, bf16[16,1024]{1,0:T(8,128)(2,1)S(1)}, u32[]{:S(2)}, u32[]{:S(2)}) collective-permute-start(bf16[16,1024]{1,0:T(8,128)(2,1)S(1)} %add_add_fusion.1), channel_id=1, source_target_pairs={{0,4},{1,5},{2,6},{3,7},{4,0},{5,1},{6,2},{7,3},{8,40},{9,41},{10,... | collective-permute-start | bytes 98312 | tf_op jit(solution)/shard_map/ppermute | solution.py:36
  39.0 3.6 %collective-permute-done.12 = bf16[16,1024]{1,0:T(8,128)(2,1)S(1)} collective-permute-done((bf16[16,1024]{1,0:T(8,128)(2,1)S(1)}, bf16[16,1024]{1,0:T(8,128)(2,1)S(1)}, u32[]{:S(2)}, u32[]{:S(2)}) %collective-permute-start.12) | collective-permute-done | bytes 32800 | tf_op jit(solution)/shard_map/ppermute | solution.py:36
  42.5 0.6 collective-permute-start.14
  43.2 2.5 %collective-permute-done.14 = bf16[16,1024]{1,0:T(8,128)(2,1)S(1)} collective-permute-done((bf16[16,1024]{1,0:T(8,128)(2,1)S(1)}, bf16[16,1024]{1,0:T(8,128)(2,1)S(1)}, u32[]{:S(2)}, u32[]{:S(2)}) %collective-permute-start.14) | collective-permute-done | bytes 32800 | tf_op jit(solution)/shard_map/ppermute | solution.py:36
  45.8 0.1 copy.8
  45.9 0.1 pad_maximum_fusion
  46.1 0.1 fusion.1.refs_0_
  46.2 1.2 collective-permute-start.15
  47.4 2.5 %collective-permute-start.16 = (bf16[272,2304]{1,0:T(8,128)(2,1)S(1)}, bf16[272,2304]{1,0:T(8,128)(2,1)S(1)}, u32[]{:S(2)}, u32[]{:S(2)}) collective-permute-start(bf16[272,2304]{1,0:T(8,128)(2,1)S(1)} %fusion.1.refs_0_), channel_id=1, source_target_pairs={{0,32},{1,33},{2,34},{3,35},{4,36},{5,37},{6,38},{7,39},{8,12},{9,... | collective-permute-start | bytes 3760136 | tf_op jit(solution)/shard_map/ppermute | solution.py:36
  49.9 1.1 collective-permute-start.17
  51.0 12.6 %collective-permute-done.15.refs_1_ = bf16[272,2304]{1,0:T(8,128)(2,1)S(1)} collective-permute-done((bf16[272,2304]{1,0:T(8,128)(2,1)S(1)}, bf16[272,2304]{1,0:T(8,128)(2,1)S(1)}, u32[]{:S(2)}, u32[]{:S(2)}) %collective-permute-start.15) | collective-permute-done | bytes 1253408 | tf_op jit(solution)/shard_map/ppermute | solution.py:36
  63.6 14.4 %collective-permute-done.16.refs_2_ = bf16[272,2304]{1,0:T(8,128)(2,1)S(1)} collective-permute-done((bf16[272,2304]{1,0:T(8,128)(2,1)S(1)}, bf16[272,2304]{1,0:T(8,128)(2,1)S(1)}, u32[]{:S(2)}, u32[]{:S(2)}) %collective-permute-start.16) | collective-permute-done | bytes 1253408 | tf_op jit(solution)/shard_map/ppermute | solution.py:36
  78.0 1.1 copy-done.6
  79.1 0.7 broadcast_in_dim.21.offdiag
  79.8 13.2 %ladder.1 = (f32[4,16,4,16,128]{4,3,2,1,0:T(8,128)}, f32[4,16,4,16,128]{4,3,2,1,0:T(8,128)}) custom-call(s32[1]{0:T(128)} %bitcast.me, f32[64,128]{1,0:T(8,128)} %broadcast_in_dim.21.offdiag, bf16[128,128]{1,0:T(8,128)(2,1)} %constant.66.clone.swap, bf16[512,2304]{1,0:T(8,128)(2,1)} %all-gather.2.cloned.1.call-done.a_in, bf16[272,2304]{1,0:T(8,128)(2,1)} %copy-done.4, ...), custom_call_target="tpu_custom_call" | custom-call | tf_op jit(solution)/shard_map/ladder/pallas_call | solution.py:194
  93.0 5.9 %collective-permute-start.18 = (f32[4,16,4,16,128]{4,3,2,1,0:T(8,128)}, f32[4,16,4,16,128]{4,3,2,1,0:T(8,128)S(1)}, u32[]{:S(2)}, u32[]{:S(2)}) collective-permute-start(f32[4,16,4,16,128]{4,3,2,1,0:T(8,128)} %get-tuple-element.8), channel_id=1, source_target_pairs={{0,8},{1,9},{2,10},{3,11},{4,12},{5,13},{6,14},{7,15},{8,0},{9,1},... | collective-permute-start | bytes 6291464 | tf_op jit(solution)/shard_map/ppermute | solution.py:36
  99.0 4.0 %collective-permute-done.18 = f32[4,16,4,16,128]{4,3,2,1,0:T(8,128)S(1)} collective-permute-done((f32[4,16,4,16,128]{4,3,2,1,0:T(8,128)}, f32[4,16,4,16,128]{4,3,2,1,0:T(8,128)S(1)}, u32[]{:S(2)}, u32[]{:S(2)}) %collective-permute-start.18) | collective-permute-done | bytes 2097184 | tf_op jit(solution)/shard_map/ppermute | solution.py:36
  103.0 2.1 %abs_reduce_fusion.1 = (f32[4,16,128]{2,1,0:T(8,128)S(1)}, f32[4,16,128]{2,1,0:T(8,128)S(1)}, f32[4,16,128]{2,1,0:T(8,128)S(1)}, f32[4,16,128]{2,1,0:T(8,128)S(1)}) fusion(f32[4,16,4,16,128]{4,3,2,1,0:T(8,128)S(1)} %collective-permute-done.18, f32[4,16,4,16,128]{4,3,2,1,0:T(8,128)} %get-tuple-element.7), kind=kLoop, calls=%fused_computation.23 | loop fusion | flops 1540096 | bytes 4325376 | tf_op jit(solution)/shard_map/reduce_max | solution.py:212
  105.2 0.5 multiply_convert_fusion.1
  105.7 0.1 pad_maximum_fusion.4
  105.8 0.1 collective-permute-start.19
  105.9 0.1 pad_maximum_fusion.5
  106.0 2.5 %collective-permute-start.20 = (f16[17,4,16,128]{3,2,1,0:T(8,128)(2,1)S(1)}, f16[17,4,16,128]{3,2,1,0:T(8,128)(2,1)S(1)}, u32[]{:S(2)}, u32[]{:S(2)}) collective-permute-start(f16[17,4,16,128]{3,2,1,0:T(8,128)(2,1)S(1)} %pad_maximum_fusion.5), channel_id=1, source_target_pairs={{0,128},{1,129},{2,130},{3,131},{4,132},{5,133},{6,134},{7,135},{8... | collective-permute-start | bytes 835592 | tf_op jit(solution)/shard_map/ppermute | solution.py:36
  108.5 0.1 pad_maximum_fusion.6
  108.6 0.3 collective-permute-start.21
  108.9 0.1 multiply_convert_fusion.3
  109.0 6.7 %collective-permute-done.19 = f16[17,4,16,128]{3,2,1,0:T(8,128)(2,1)S(1)} collective-permute-done((f16[17,4,16,128]{3,2,1,0:T(8,128)(2,1)S(1)}, f16[17,4,16,128]{3,2,1,0:T(8,128)(2,1)S(1)}, u32[]{:S(2)}, u32[]{:S(2)}) %collective-permute-start.19) | collective-permute-done | bytes 278560 | tf_op jit(solution)/shard_map/ppermute | solution.py:36
  115.7 0.8 collective-permute-done.21
  116.5 0.4 pad_maximum_fusion.1
  117.0 0.1 fusion.34
  117.0 0.1 fusion.32
  117.1 0.1 fusion.33
  117.1 0.5 maximum_select_fusion.2
  117.6 2.5 %collective-permute-start.25 = (f16[17,4,16,128]{3,2,1,0:T(8,128)(2,1)S(1)}, f16[17,4,16,128]{3,2,1,0:T(8,128)(2,1)S(1)}, u32[]{:S(2)}, u32[]{:S(2)}) collective-permute-start(f16[17,4,16,128]{3,2,1,0:T(8,128)(2,1)S(1)} %get-tuple-element.17), channel_id=1, source_target_pairs={{0,6},{1,7},{2,0},{3,1},{4,2},{5,3},{6,4},{7,5},{8,24},{9,56},{10,... | collective-permute-start | bytes 835592 | tf_op jit(solution)/shard_map/ppermute | solution.py:36
  120.1 1.2 collective-permute-start.24
  121.3 1.9 %collective-permute-start.23 = (f16[17,4,16,128]{3,2,1,0:T(8,128)(2,1)S(1)}, f16[17,4,16,128]{3,2,1,0:T(8,128)(2,1)S(1)}, u32[]{:S(2)}, u32[]{:S(2)}) collective-permute-start(f16[17,4,16,128]{3,2,1,0:T(8,128)(2,1)S(1)} %get-tuple-element.19), channel_id=1, source_target_pairs={{0,2},{1,3},{2,4},{3,5},{4,6},{5,7},{6,0},{7,1},{8,8},{9,40},{10,1... | collective-permute-start | bytes 835592 | tf_op jit(solution)/shard_map/ppermute | solution.py:36
  123.2 5.8 %collective-permute-start.22 = (f16[17,4,16,128]{3,2,1,0:T(8,128)(2,1)S(1)}, f16[17,4,16,128]{3,2,1,0:T(8,128)(2,1)S(1)}, u32[]{:S(2)}, u32[]{:S(2)}) collective-permute-start(f16[17,4,16,128]{3,2,1,0:T(8,128)(2,1)S(1)} %get-tuple-element.20), channel_id=1, source_target_pairs={{0,0},{1,1},{2,2},{3,3},{4,4},{5,5},{6,6},{7,7},{8,8},{9,40},{10,1... | collective-permute-start | bytes 835592 | tf_op jit(solution)/shard_map/ppermute | solution.py:36
  129.1 2.9 %collective-permute-done.24 = f16[17,4,16,128]{3,2,1,0:T(8,128)(2,1)S(1)} collective-permute-done((f16[17,4,16,128]{3,2,1,0:T(8,128)(2,1)S(1)}, f16[17,4,16,128]{3,2,1,0:T(8,128)(2,1)S(1)}, u32[]{:S(2)}, u32[]{:S(2)}) %collective-permute-start.24) | collective-permute-done | bytes 278560 | tf_op jit(solution)/shard_map/ppermute | solution.py:36
  132.1 2.3 %collective-permute-done.23 = f16[17,4,16,128]{3,2,1,0:T(8,128)(2,1)S(1)} collective-permute-done((f16[17,4,16,128]{3,2,1,0:T(8,128)(2,1)S(1)}, f16[17,4,16,128]{3,2,1,0:T(8,128)(2,1)S(1)}, u32[]{:S(2)}, u32[]{:S(2)}) %collective-permute-start.23) | collective-permute-done | bytes 278560 | tf_op jit(solution)/shard_map/ppermute | solution.py:36
  134.5 2.9 %collective-permute-done.22 = f16[17,4,16,128]{3,2,1,0:T(8,128)(2,1)S(1)} collective-permute-done((f16[17,4,16,128]{3,2,1,0:T(8,128)(2,1)S(1)}, f16[17,4,16,128]{3,2,1,0:T(8,128)(2,1)S(1)}, u32[]{:S(2)}, u32[]{:S(2)}) %collective-permute-start.22) | collective-permute-done | bytes 278560 | tf_op jit(solution)/shard_map/ppermute | solution.py:36
  137.5 0.1 split.1
  137.6 3.3 %collective-permute-start.26 = (f32[4,8,4,16,128]{4,3,2,1,0:T(8,128)S(1)}, f32[4,8,4,16,128]{4,3,2,1,0:T(8,128)S(1)}, u32[]{:S(2)}, u32[]{:S(2)}) collective-permute-start(f32[4,8,4,16,128]{4,3,2,1,0:T(8,128)S(1)} %split.1), channel_id=1, source_target_pairs={{0,8},{1,9},{2,10},{3,11},{4,12},{5,13},{6,14},{7,15},{8,0},{9,1},... | collective-permute-start | bytes 3145736 | tf_op jit(solution)/shard_map/ppermute | solution.py:36
  140.9 2.3 %collective-permute-done.26.refs_4_ = f32[4,8,4,16,128]{4,3,2,1,0:T(8,128)S(1)} collective-permute-done((f32[4,8,4,16,128]{4,3,2,1,0:T(8,128)S(1)}, f32[4,8,4,16,128]{4,3,2,1,0:T(8,128)S(1)}, u32[]{:S(2)}, u32[]{:S(2)}) %collective-permute-start.26) | collective-permute-done | bytes 1048608 | tf_op jit(solution)/shard_map/ppermute | solution.py:36
  143.2 4.2 %finish.1 = f32[64,32,128]{2,1,0:T(8,128)} custom-call(s32[1]{0:T(128)} %bitcast.me, f32[16,4,16,128]{3,2,1,0:T(8,128)S(1)} %slice_multiply_fusion.3.refs_0_, f32[16,4,16,128]{3,2,1,0:T(8,128)S(1)} %slice_multiply_fusion.2.refs_1_, f32[16,4,16,128]{3,2,1,0:T(8,128)S(1)} %slice_multiply_fusion.1.refs_2_, f32[16,4,16,128]{3,2,1,0:T(8,128)S(1)} %slice_multiply_fusion.refs_3_, ...), custom_call_target="tpu_custom_call" | custom-call | tf_op jit(solution)/shard_map/finish/pallas_call | solution.py:310
  (54 shorter events, 0.8 us)
Async XLA Ops:
  6.5 10.2 %copy-start.2 = (s32[2,2]{1,0:T(2,128)S(1)}, s32[2,2]{1,0:T(2,128)}, u32[]{:S(2)}) copy-start(s32[2,2]{1,0:T(2,128)} %offsets.1) | copy-start | bytes 52
  6.5 10.2 %copy-start.1 = (bf16[64,32,128]{2,1,0:T(8,128)(2,1)S(1)}, bf16[64,32,128]{2,1,0:T(8,128)(2,1)}, u32[]{:S(2)}) copy-start(bf16[64,32,128]{2,1,0:T(8,128)(2,1)} %amplitudes.1) | copy-start | bytes 1572868
  6.5 72.5 %all-gather.2.cloned.1.call-start = ((), (), s32[]{:S(2)}) async-start(), calls=%async_computation | async-start | bytes 2654208 | tf_op jit(solution)/shard_map/all_gather | solution.py:348
  7.8 1.8 %collective-permute-start = (bf16[32,2304]{1,0:T(8,128)(2,1)S(1)}, bf16[32,2304]{1,0:T(8,128)(2,1)S(1)}, u32[]{:S(2)}, u32[]{:S(2)}) collective-permute-start(bf16[32,2304]{1,0:T(8,128)(2,1)S(1)} %get-tuple-element.22), channel_id=1, source_target_pairs={{0,8},{1,9},{2,10},{3,11},{4,12},{5,13},{6,14},{7,15},{8,0},{9,1},... | collective-permute-start | bytes 442376 | tf_op jit(solution)/shard_map/ppermute | solution.py:36
  10.3 10.2 %collective-permute-start.1 = (bf16[32,2304]{1,0:T(8,128)(2,1)S(1)}, bf16[32,2304]{1,0:T(8,128)(2,1)S(1)}, u32[]{:S(2)}, u32[]{:S(2)}) collective-permute-start(bf16[32,2304]{1,0:T(8,128)(2,1)S(1)} %get-tuple-element.24), channel_id=1, source_target_pairs={{0,0},{1,32},{2,2},{3,34},{4,4},{5,36},{6,6},{7,38},{8,8},{9,40},{... | collective-permute-start | bytes 442376 | tf_op jit(solution)/shard_map/ppermute | solution.py:36
  14.7 16.5 %collective-permute-start.2 = (bf16[32,2304]{1,0:T(8,128)(2,1)S(1)}, bf16[32,2304]{1,0:T(8,128)(2,1)S(1)}, u32[]{:S(2)}, u32[]{:S(2)}) collective-permute-start(bf16[32,2304]{1,0:T(8,128)(2,1)S(1)} %get-tuple-element.21), channel_id=1, source_target_pairs={{0,8},{1,40},{2,10},{3,42},{4,12},{5,44},{6,14},{7,46},{8,0},{9,32... | collective-permute-start | bytes 442376 | tf_op jit(solution)/shard_map/ppermute | solution.py:36
  16.7 1.0 copy-start
  18.3 2.2 %collective-permute-start.6 = (bf16[16,1024]{1,0:T(8,128)(2,1)S(1)}, bf16[16,1024]{1,0:T(8,128)(2,1)S(1)}, u32[]{:S(2)}, u32[]{:S(2)}) collective-permute-start(bf16[16,1024]{1,0:T(8,128)(2,1)S(1)} %blocks.1), channel_id=1, source_target_pairs={{0,8},{1,9},{2,10},{3,11},{4,12},{5,13},{6,14},{7,15},{8,0},{9,1},... | collective-permute-start | bytes 98312 | tf_op jit(solution)/shard_map/ppermute | solution.py:36
  18.4 3.1 %collective-permute-start.7 = (bf16[16,1024]{1,0:T(8,128)(2,1)S(1)}, bf16[16,1024]{1,0:T(8,128)(2,1)S(1)}, u32[]{:S(2)}, u32[]{:S(2)}) collective-permute-start(bf16[16,1024]{1,0:T(8,128)(2,1)S(1)} %blocks.1), channel_id=1, source_target_pairs={{0,1},{1,0},{2,3},{3,2},{4,5},{5,4},{6,7},{7,6},{8,9},{9,8},{10,11... | collective-permute-start | bytes 98312 | tf_op jit(solution)/shard_map/ppermute | solution.py:36
  18.5 4.3 %collective-permute-start.8 = (bf16[16,1024]{1,0:T(8,128)(2,1)S(1)}, bf16[16,1024]{1,0:T(8,128)(2,1)S(1)}, u32[]{:S(2)}, u32[]{:S(2)}) collective-permute-start(bf16[16,1024]{1,0:T(8,128)(2,1)S(1)} %blocks.1), channel_id=1, source_target_pairs={{0,9},{1,8},{2,11},{3,10},{4,13},{5,12},{6,15},{7,14},{8,1},{9,0},... | collective-permute-start | bytes 98312 | tf_op jit(solution)/shard_map/ppermute | solution.py:36
  22.7 12.1 %collective-permute-start.10 = (bf16[16,1024]{1,0:T(8,128)(2,1)S(1)}, bf16[16,1024]{1,0:T(8,128)(2,1)S(1)}, u32[]{:S(2)}, u32[]{:S(2)}) collective-permute-start(bf16[16,1024]{1,0:T(8,128)(2,1)S(1)} %add_add_fusion.2), channel_id=1, source_target_pairs={{0,128},{1,129},{2,130},{3,131},{4,132},{5,133},{6,134},{7,135},{8... | collective-permute-start | bytes 98312 | tf_op jit(solution)/shard_map/ppermute | solution.py:36
  29.1 6.6 %collective-permute-start.11 = (bf16[16,1024]{1,0:T(8,128)(2,1)S(1)}, bf16[16,1024]{1,0:T(8,128)(2,1)S(1)}, u32[]{:S(2)}, u32[]{:S(2)}) collective-permute-start(bf16[16,1024]{1,0:T(8,128)(2,1)S(1)} %add_add_fusion.2), channel_id=1, source_target_pairs={{0,192},{1,193},{2,194},{3,195},{4,196},{5,197},{6,198},{7,199},{8... | collective-permute-start | bytes 98312 | tf_op jit(solution)/shard_map/ppermute | solution.py:36
  29.2 6.5 %collective-permute-start.9 = (bf16[16,1024]{1,0:T(8,128)(2,1)S(1)}, bf16[16,1024]{1,0:T(8,128)(2,1)S(1)}, u32[]{:S(2)}, u32[]{:S(2)}) collective-permute-start(bf16[16,1024]{1,0:T(8,128)(2,1)S(1)} %add_add_fusion.2), channel_id=1, source_target_pairs={{0,64},{1,65},{2,66},{3,67},{4,68},{5,69},{6,70},{7,71},{8,72},{9,... | collective-permute-start | bytes 98312 | tf_op jit(solution)/shard_map/ppermute | solution.py:36
  31.2 14.5 %collective-permute-start.3 = (bf16[64,2304]{1,0:T(8,128)(2,1)S(1)}, bf16[64,2304]{1,0:T(8,128)(2,1)S(1)}, u32[]{:S(2)}, u32[]{:S(2)}) collective-permute-start(bf16[64,2304]{1,0:T(8,128)(2,1)S(1)} %constant_dynamic-update-slice_fusion), channel_id=1, source_target_pairs={{0,2},{1,3},{2,4},{3,5},{4,6},{5,7},{6,0},{7,1},{8,24},{9,25},{10,... | collective-permute-start | bytes 884744 | tf_op jit(solution)/shard_map/ppermute | solution.py:36
  31.5 14.2 %collective-permute-start.4 = (bf16[64,2304]{1,0:T(8,128)(2,1)S(1)}, bf16[64,2304]{1,0:T(8,128)(2,1)S(1)}, u32[]{:S(2)}, u32[]{:S(2)}) collective-permute-start(bf16[64,2304]{1,0:T(8,128)(2,1)S(1)} %constant_dynamic-update-slice_fusion), channel_id=1, source_target_pairs={{0,4},{1,5},{2,6},{3,7},{4,0},{5,1},{6,2},{7,3},{8,40},{9,41},{10,... | collective-permute-start | bytes 884744 | tf_op jit(solution)/shard_map/ppermute | solution.py:36
  34.8 11.0 %collective-permute-start.5 = (bf16[64,2304]{1,0:T(8,128)(2,1)S(1)}, bf16[64,2304]{1,0:T(8,128)(2,1)S(1)}, u32[]{:S(2)}, u32[]{:S(2)}) collective-permute-start(bf16[64,2304]{1,0:T(8,128)(2,1)S(1)} %constant_dynamic-update-slice_fusion), channel_id=1, source_target_pairs={{0,6},{1,7},{2,0},{3,1},{4,2},{5,3},{6,4},{7,5},{8,56},{9,57},{10,... | collective-permute-start | bytes 884744 | tf_op jit(solution)/shard_map/ppermute | solution.py:36
  35.7 6.8 %collective-permute-start.12 = (bf16[16,1024]{1,0:T(8,128)(2,1)S(1)}, bf16[16,1024]{1,0:T(8,128)(2,1)S(1)}, u32[]{:S(2)}, u32[]{:S(2)}) collective-permute-start(bf16[16,1024]{1,0:T(8,128)(2,1)S(1)} %add_add_fusion.1), channel_id=1, source_target_pairs={{0,2},{1,3},{2,4},{3,5},{4,6},{5,7},{6,0},{7,1},{8,24},{9,25},{10,... | collective-permute-start | bytes 98312 | tf_op jit(solution)/shard_map/ppermute | solution.py:36
  36.4 6.8 %collective-permute-start.13 = (bf16[16,1024]{1,0:T(8,128)(2,1)S(1)}, bf16[16,1024]{1,0:T(8,128)(2,1)S(1)}, u32[]{:S(2)}, u32[]{:S(2)}) collective-permute-start(bf16[16,1024]{1,0:T(8,128)(2,1)S(1)} %add_add_fusion.1), channel_id=1, source_target_pairs={{0,4},{1,5},{2,6},{3,7},{4,0},{5,1},{6,2},{7,3},{8,40},{9,41},{10,... | collective-permute-start | bytes 98312 | tf_op jit(solution)/shard_map/ppermute | solution.py:36
  42.5 3.2 %collective-permute-start.14 = (bf16[16,1024]{1,0:T(8,128)(2,1)S(1)}, bf16[16,1024]{1,0:T(8,128)(2,1)S(1)}, u32[]{:S(2)}, u32[]{:S(2)}) collective-permute-start(bf16[16,1024]{1,0:T(8,128)(2,1)S(1)} %add_add_fusion.1), channel_id=1, source_target_pairs={{0,6},{1,7},{2,0},{3,1},{4,2},{5,3},{6,4},{7,5},{8,56},{9,57},{10,... | collective-permute-start | bytes 98312 | tf_op jit(solution)/shard_map/ppermute | solution.py:36
  46.1 5.0 %copy-start.7 = (s32[64,2]{0,1:T(2,128)S(1)}, s32[64,2]{0,1:T(2,128)}, u32[]{:S(2)}) copy-start(s32[64,2]{0,1:T(2,128)} %param.5) | copy-start | bytes 1540
  46.2 33.6 %copy-start.4 = (bf16[272,2304]{1,0:T(8,128)(2,1)}, bf16[272,2304]{1,0:T(8,128)(2,1)S(1)}, u32[]{:S(2)}) copy-start(bf16[272,2304]{1,0:T(8,128)(2,1)S(1)} %fusion.1.refs_0_) | copy-start | bytes 3760132
  46.2 17.4 %collective-permute-start.15 = (bf16[272,2304]{1,0:T(8,128)(2,1)S(1)}, bf16[272,2304]{1,0:T(8,128)(2,1)S(1)}, u32[]{:S(2)}, u32[]{:S(2)}) collective-permute-start(bf16[272,2304]{1,0:T(8,128)(2,1)S(1)} %fusion.1.refs_0_), channel_id=1, source_target_pairs={{0,16},{1,17},{2,18},{3,19},{4,20},{5,21},{6,22},{7,23},{8,10},{9,... | collective-permute-start | bytes 3760136 | tf_op jit(solution)/shard_map/ppermute | solution.py:36
  47.4 30.6 %collective-permute-start.16 = (bf16[272,2304]{1,0:T(8,128)(2,1)S(1)}, bf16[272,2304]{1,0:T(8,128)(2,1)S(1)}, u32[]{:S(2)}, u32[]{:S(2)}) collective-permute-start(bf16[272,2304]{1,0:T(8,128)(2,1)S(1)} %fusion.1.refs_0_), channel_id=1, source_target_pairs={{0,32},{1,33},{2,34},{3,35},{4,36},{5,37},{6,38},{7,39},{8,12},{9,... | collective-permute-start | bytes 3760136 | tf_op jit(solution)/shard_map/ppermute | solution.py:36
  49.9 29.2 %collective-permute-start.17 = (bf16[272,2304]{1,0:T(8,128)(2,1)S(1)}, bf16[272,2304]{1,0:T(8,128)(2,1)}, u32[]{:S(2)}, u32[]{:S(2)}) collective-permute-start(bf16[272,2304]{1,0:T(8,128)(2,1)S(1)} %fusion.1.refs_0_), channel_id=1, source_target_pairs={{0,48},{1,49},{2,50},{3,51},{4,52},{5,53},{6,54},{7,55},{8,14},{9,... | collective-permute-start | bytes 3760136 | tf_op jit(solution)/shard_map/ppermute | solution.py:36
  63.6 16.2 %copy-start.5 = (bf16[272,2304]{1,0:T(8,128)(2,1)}, bf16[272,2304]{1,0:T(8,128)(2,1)S(1)}, u32[]{:S(2)}) copy-start(bf16[272,2304]{1,0:T(8,128)(2,1)S(1)} %collective-permute-done.15.refs_1_) | copy-start | bytes 3760132
  78.0 1.1 copy-start.6
  93.0 9.9 %collective-permute-start.18 = (f32[4,16,4,16,128]{4,3,2,1,0:T(8,128)}, f32[4,16,4,16,128]{4,3,2,1,0:T(8,128)S(1)}, u32[]{:S(2)}, u32[]{:S(2)}) collective-permute-start(f32[4,16,4,16,128]{4,3,2,1,0:T(8,128)} %get-tuple-element.8), channel_id=1, source_target_pairs={{0,8},{1,9},{2,10},{3,11},{4,12},{5,13},{6,14},{7,15},{8,0},{9,1},... | collective-permute-start | bytes 6291464 | tf_op jit(solution)/shard_map/ppermute | solution.py:36
  103.0 2.2 %copy-start.3 = (f32[4,16,4,16,128]{4,3,2,1,0:T(8,128)S(1)}, f32[4,16,4,16,128]{4,3,2,1,0:T(8,128)}, u32[]{:S(2)}) copy-start(f32[4,16,4,16,128]{4,3,2,1,0:T(8,128)} %get-tuple-element.7) | copy-start | bytes 6291460
  105.8 10.0 %collective-permute-start.19 = (f16[17,4,16,128]{3,2,1,0:T(8,128)(2,1)S(1)}, f16[17,4,16,128]{3,2,1,0:T(8,128)(2,1)S(1)}, u32[]{:S(2)}, u32[]{:S(2)}) collective-permute-start(f16[17,4,16,128]{3,2,1,0:T(8,128)(2,1)S(1)} %pad_maximum_fusion.4), channel_id=1, source_target_pairs={{0,64},{1,65},{2,66},{3,67},{4,68},{5,69},{6,70},{7,71},{8,10},{9,... | collective-permute-start | bytes 835592 | tf_op jit(solution)/shard_map/ppermute | solution.py:36
  106.0 9.8 %collective-permute-start.20 = (f16[17,4,16,128]{3,2,1,0:T(8,128)(2,1)S(1)}, f16[17,4,16,128]{3,2,1,0:T(8,128)(2,1)S(1)}, u32[]{:S(2)}, u32[]{:S(2)}) collective-permute-start(f16[17,4,16,128]{3,2,1,0:T(8,128)(2,1)S(1)} %pad_maximum_fusion.5), channel_id=1, source_target_pairs={{0,128},{1,129},{2,130},{3,131},{4,132},{5,133},{6,134},{7,135},{8... | collective-permute-start | bytes 835592 | tf_op jit(solution)/shard_map/ppermute | solution.py:36
  108.6 8.0 %collective-permute-start.21 = (f16[17,4,16,128]{3,2,1,0:T(8,128)(2,1)S(1)}, f16[17,4,16,128]{3,2,1,0:T(8,128)(2,1)S(1)}, u32[]{:S(2)}, u32[]{:S(2)}) collective-permute-start(f16[17,4,16,128]{3,2,1,0:T(8,128)(2,1)S(1)} %pad_maximum_fusion.6), channel_id=1, source_target_pairs={{0,192},{1,193},{2,194},{3,195},{4,196},{5,197},{6,198},{7,199},{8... | collective-permute-start | bytes 835592 | tf_op jit(solution)/shard_map/ppermute | solution.py:36
  117.6 11.3 %collective-permute-start.25 = (f16[17,4,16,128]{3,2,1,0:T(8,128)(2,1)S(1)}, f16[17,4,16,128]{3,2,1,0:T(8,128)(2,1)S(1)}, u32[]{:S(2)}, u32[]{:S(2)}) collective-permute-start(f16[17,4,16,128]{3,2,1,0:T(8,128)(2,1)S(1)} %get-tuple-element.17), channel_id=1, source_target_pairs={{0,6},{1,7},{2,0},{3,1},{4,2},{5,3},{6,4},{7,5},{8,24},{9,56},{10,... | collective-permute-start | bytes 835592 | tf_op jit(solution)/shard_map/ppermute | solution.py:36
  120.1 11.9 %collective-permute-start.24 = (f16[17,4,16,128]{3,2,1,0:T(8,128)(2,1)S(1)}, f16[17,4,16,128]{3,2,1,0:T(8,128)(2,1)S(1)}, u32[]{:S(2)}, u32[]{:S(2)}) collective-permute-start(f16[17,4,16,128]{3,2,1,0:T(8,128)(2,1)S(1)} %get-tuple-element.18), channel_id=1, source_target_pairs={{0,4},{1,5},{2,6},{3,7},{4,0},{5,1},{6,2},{7,3},{8,24},{9,56},{10,... | collective-permute-start | bytes 835592 | tf_op jit(solution)/shard_map/ppermute | solution.py:36
  121.3 13.1 %collective-permute-start.23 = (f16[17,4,16,128]{3,2,1,0:T(8,128)(2,1)S(1)}, f16[17,4,16,128]{3,2,1,0:T(8,128)(2,1)S(1)}, u32[]{:S(2)}, u32[]{:S(2)}) collective-permute-start(f16[17,4,16,128]{3,2,1,0:T(8,128)(2,1)S(1)} %get-tuple-element.19), channel_id=1, source_target_pairs={{0,2},{1,3},{2,4},{3,5},{4,6},{5,7},{6,0},{7,1},{8,8},{9,40},{10,1... | collective-permute-start | bytes 835592 | tf_op jit(solution)/shard_map/ppermute | solution.py:36
  123.2 14.1 %collective-permute-start.22 = (f16[17,4,16,128]{3,2,1,0:T(8,128)(2,1)S(1)}, f16[17,4,16,128]{3,2,1,0:T(8,128)(2,1)S(1)}, u32[]{:S(2)}, u32[]{:S(2)}) collective-permute-start(f16[17,4,16,128]{3,2,1,0:T(8,128)(2,1)S(1)} %get-tuple-element.20), channel_id=1, source_target_pairs={{0,0},{1,1},{2,2},{3,3},{4,4},{5,5},{6,6},{7,7},{8,8},{9,40},{10,1... | collective-permute-start | bytes 835592 | tf_op jit(solution)/shard_map/ppermute | solution.py:36
  137.6 5.6 %collective-permute-start.26 = (f32[4,8,4,16,128]{4,3,2,1,0:T(8,128)S(1)}, f32[4,8,4,16,128]{4,3,2,1,0:T(8,128)S(1)}, u32[]{:S(2)}, u32[]{:S(2)}) collective-permute-start(f32[4,8,4,16,128]{4,3,2,1,0:T(8,128)S(1)} %split.1), channel_id=1, source_target_pairs={{0,8},{1,9},{2,10},{3,11},{4,12},{5,13},{6,14},{7,15},{8,0},{9,1},... | collective-permute-start | bytes 3145736 | tf_op jit(solution)/shard_map/ppermute | solution.py:36
Sparse Core Ops, SparseCore 0:
  10.4 43.8 all-gather.1

commit v3 on v2

--- a/solution.py
+++ b/solution.py
@@ -88,10 +88,10 @@
     )
 
 
-def ladder_kernel(me, offdiag, swap, a_in, *refs):
+def ladder_kernel(me, offdiag, swap, blocks, a_in, *refs):
     b_in = refs[0:4]
-    keep, give = refs[4:6]
-    a_all, b_all, m_all, tail, sems = refs[6:]
+    keep, give = refs[4], refs[5:9]
+    a_all, b_all, m_all, mine, other, sems = refs[9:]
     x, y, z, c = coords(me[0])
     copies = []
     for j in range(8):
@@ -112,12 +112,6 @@
                     sems.at[8 + d * 4 + j],
                 )
             )
-    for j in range(4):
-        copies.append(
-            pltpu.make_async_copy(
-                b_in[j].at[pl.ds(256, 16), pl.ds(0, 1024)], tail.at[j], sems.at[40 + j]
-            )
-        )
     for copy in copies:
         copy.start()
     for copy in copies[:8]:
@@ -131,15 +125,10 @@
         )
         m_all[:, d] = m[:, :128].reshape(64, BLK, 128)
         m_all[:, d + 1] = m[:, 128:].reshape(64, BLK, 128)
-    for copy in copies[40:]:
-        copy.wait()
-    t = tail[...].astype(jnp.float32)
-    t = t[0] + t[1] + t[2] + t[3]
     parts = []
     for n in range(4):
-        parts.append(
-            jnp.where(c == 0, t[:, 128 * n : 128 * n + 128], t[:, 128 * n + 512 : 128 * n + 640])
-        )
+        one, two = (blocks[:, at : at + 128] for at in (128 * n, 128 * n + 512))
+        parts.append(jnp.where(c == 0, one.astype(jnp.float32), two.astype(jnp.float32)))
     t = jnp.concatenate(parts).astype(jnp.bfloat16)
     t = jnp.dot(t, swap[...], preferred_element_type=jnp.float32)
     forward, mirror = t[:, :64], t[:, 64:]
@@ -185,27 +174,41 @@
         for n in range(2):
             one = res[:64, 128 * n : 128 * n + 128].reshape(4, 16, 128)
             two = turned[64 * n : 64 * n + 64].reshape(4, 16, 128)
-            keep[jnp.where(c == 0, kz, kx), at + n] = jnp.where(c == 0, one, two)
-            give[jnp.where(c == 0, kx, kz), at + n] = jnp.where(c == 0, two, one)
-
-
-def ladder(me, offdiag, swap, rows, cols):
+            mine[kz, at + n] = jnp.where(c == 0, one, two)
+            other[kz, at + n] = jnp.where(c == 0, two, one)
+        if g % 8 == 7:
+            to = keep.at[jnp.where(c == 0, kz, kx)]
+            pltpu.make_async_copy(mine.at[kz], to, sems.at[kz]).start()
+            for k in range(4):
+
+                @pl.when(jnp.where(c == 0, kx, kz) == k)
+                def _(kz=kz, k=k):
+                    pltpu.make_async_copy(other.at[kz], give[k], sems.at[4 + kz]).start()
+
+    for kz in range(4):
+        pltpu.make_async_copy(mine.at[kz], keep.at[kz], sems.at[kz]).wait()
+        pltpu.make_async_copy(other.at[kz], give[kz], sems.at[4 + kz]).wait()
+
+
+def ladder(me, offdiag, swap, blocks, rows, cols):
     f32, bf16 = jnp.float32, jnp.bfloat16
     return pl.pallas_call(
         ladder_kernel,
-        out_shape=[jax.ShapeDtypeStruct((4, 16, 4, 16, 128), f32)] * 2,
-        in_specs=[SMEM, VMEM, VMEM] + [HBM] * 5,
-        out_specs=[VMEM] * 2,
+        out_shape=[jax.ShapeDtypeStruct((4, 16, 4, 16, 128), f32)]
+        + [jax.ShapeDtypeStruct((16, 4, 16, 128), f32)] * 4,
+        in_specs=[SMEM, VMEM, VMEM, VMEM] + [HBM] * 5,
+        out_specs=[HBM] * 5,
         scratch_shapes=[
             pltpu.VMEM((512, DEPTH), bf16),
             pltpu.VMEM((BLK, 128, DEPTH), bf16),
             pltpu.VMEM((64, BLK, BLK, 128), f32),
-            pltpu.VMEM((4, 16, 1024), bf16),
-            pltpu.SemaphoreType.DMA((44,)),
+            pltpu.VMEM((4, 16, 4, 16, 128), f32),
+            pltpu.VMEM((4, 16, 4, 16, 128), f32),
+            pltpu.SemaphoreType.DMA((40,)),
         ],
         compiler_params=pltpu.CompilerParams(vmem_limit_bytes=56 << 20),
         name="ladder",
-    )(me, offdiag, swap, rows, *cols)
+    )(me, offdiag, swap, blocks, rows, *cols)
 
 
 def pack(block):
@@ -287,14 +290,14 @@
         + (lane >> 2 & 3) * 8
         + (lane >> 6) * 4
         + (lane & 3),
-        jnp.float32,
+        jnp.bfloat16,
     )
     for g in range(4):
-        t = jnp.dot(
-            r1[g].reshape(8 * P_SIZE, 128),
-            order,
-            preferred_element_type=jnp.float32,
-            precision=lax.Precision.HIGHEST,
+        t = r1[g].reshape(8 * P_SIZE, 128)
+        hi = t.astype(jnp.bfloat16)
+        lo = (t - hi.astype(jnp.float32)).astype(jnp.bfloat16)
+        t = jnp.dot(hi, order, preferred_element_type=jnp.float32) + jnp.dot(
+            lo, order, preferred_element_type=jnp.float32
         )
         for n in range(8):
             out[:, 8 * g + n, :] = t[64 * n : 64 * n + 64]
@@ -365,29 +368,24 @@
     def far(n):
         return lambda x, y, z, c: (x + n * c, y + n * (1 - c), z, c)
 
-    first = [jnp.concatenate(cols)]
+    t = jnp.pad(t, ((0, 0), (0, DEPTH - 1024)))
+    first = [jnp.concatenate(cols + [t])]
     first += [send(first[0], near(n)) for n in range(1, 4)]
+    cols = jnp.stack([m[:64].reshape(8, BLK, DEPTH) for m in first])
+    cols = jnp.transpose(cols, (2, 0, 1, 3)).reshape(256, DEPTH)
+    second = [cols] + [send(cols, far(n)) for n in range(1, 4)]
+    t = sum(m[64:, :1024] for m in first[1:]) + first[0][64:, :1024]
+    t = t + cols[:16, :1024] * 0
     t = t + sum(send(t, lambda x, y, z, c, n=n: (x, y, z ^ n, c)) for n in (2, 4, 6))
-    t = t + sum(send(t, near(n)) for n in range(1, 4))
-    t = jnp.pad(t, ((0, 0), (0, DEPTH - 1024)))
-    cols = jnp.stack([m.reshape(8, BLK, DEPTH) for m in first])
-    cols = jnp.transpose(cols, (2, 0, 1, 3)).reshape(256, DEPTH)
-    second = [jnp.concatenate([cols, t])]
-    second += [send(second[0], far(n)) for n in range(1, 4)]
+    t = t + sum(send(t, far(n)) for n in range(1, 4))
     offdiag = (pairs[:, 0] != pairs[:, 1]).astype(jnp.float32)
     offdiag = jnp.broadcast_to(offdiag[:, None], (P_SIZE, 128))
     swap = jnp.asarray(transposed_forward(), jnp.bfloat16)
-    keep, give = ladder(me, offdiag, swap, rows, second)
-
-    taken = send(give, core)
-    got = [pack(keep[0] + taken[0])]
+    keep, *give = ladder(me, offdiag, swap, t, rows, second)
+
+    got = [pack(keep[k] + send(give[k], core)) for k in range(4)]
     for k in range(1, 4):
-        got.append(
-            send(
-                pack(keep[k] + taken[k]),
-                lambda x, y, z, c, k=k: (x + k * c, y, z + 2 * k * (1 - c), c),
-            )
-        )
+        got[k] = send(got[k], lambda x, y, z, c, k=k: (x + k * c, y, z + 2 * k * (1 - c), c))
 
     def onward(j):
         def where(x, y, z, c):

time: 157 us -> 149 us (0.949); the launches traced: 154 us -> 149 us
  waiting for transfers between devices: 58.1 us -> 55.6 us
    ppermute x27 -> x30, waiting for transfers between devices: 58 us -> 55.6 us  [send(): return lax.ppermute(block, AXES, pairs)]
    ppermute x27 -> x30, starting transfers between devices: 54.5 us -> 54.2 us  [send(): return lax.ppermute(block, AXES, pairs)]
  transfers between devices with their start and end apart: 28 -> 31, of which waited for: 14 -> 21; matrix products, arithmetic and copies ran while one was open for 1% -> 1% of each run, Pallas kernels for 0% -> 0%
where the time goes in v3:
time: 149 us
  waiting for transfers between devices  55.6 us (37%)
  starting transfers between devices  54.2 us (36%)
  Pallas kernels  16.8 us (11%)
  between operations  13.8 us (9%)
  other arithmetic  5.13 us (3%)
  local copies, waits for them, and re-layouts  3.07 us (2%)
    ppermute x30, waiting for transfers between devices, send(): return lax.ppermute(block, AXES, pairs)  55.6 us
    ppermute x30, starting transfers between devices, send(): return lax.ppermute(block, AXES, pairs)  54.2 us
    pallas_call x1, Pallas kernels, ladder(): pl.pallas_call(ladder_kernel, out_shape=[jax.ShapeDtypeStruct((4, 16, 4,...  12.2 us
    pallas_call x1, Pallas kernels, finish(): pl.pallas_call(finish_kernel, out_shape=jax.ShapeDtypeStruct((P_SIZE, 32,...  3.99 us
  transfers between devices with their start and end apart: 31, of which 21 were waited for; matrix products, arithmetic and copies ran while one was open for 1% of the time, Pallas kernels for 0%

profile of v3, /device:TPU:33, one launch (start us, length us, event | category | flops | bytes accessed | tf_op | source)
XLA Modules:
  0.0 148.7 jit_solution(3592553392292201079)
XLA Ops:
  6.5 1.2 dynamic-slice_bitcast_fusion.3
  7.8 0.8 collective-permute-start.2
  8.5 1.0 collective-permute-done.2
  9.6 0.6 blocks.1
  10.2 0.5 collective-permute-start.3
  10.7 1.6 %collective-permute-start.4 = (bf16[16,1024]{1,0:T(8,128)(2,1)S(1)}, bf16[16,1024]{1,0:T(8,128)(2,1)S(1)}, u32[]{:S(2)}, u32[]{:S(2)}) collective-permute-start(bf16[16,1024]{1,0:T(8,128)(2,1)S(1)} %blocks.1), channel_id=1, source_target_pairs={{0,1},{1,0},{2,3},{3,2},{4,5},{5,4},{6,7},{7,6},{8,9},{9,8},{10,11... | collective-permute-start | bytes 98312 | tf_op jit(solution)/shard_map/ppermute | solution.py:36
  12.2 0.2 collective-permute-start.5
  12.4 4.4 %collective-permute-start = (bf16[32,2304]{1,0:T(8,128)(2,1)S(1)}, bf16[32,2304]{1,0:T(8,128)(2,1)S(1)}, u32[]{:S(2)}, u32[]{:S(2)}) collective-permute-start(bf16[32,2304]{1,0:T(8,128)(2,1)S(1)} %get-tuple-element.27), channel_id=1, source_target_pairs={{0,0},{1,32},{2,2},{3,34},{4,4},{5,36},{6,6},{7,38},{8,8},{9,40},{... | collective-permute-start | bytes 442376 | tf_op jit(solution)/shard_map/ppermute | solution.py:36
  16.8 1.9 %collective-permute-start.1 = (bf16[32,2304]{1,0:T(8,128)(2,1)S(1)}, bf16[32,2304]{1,0:T(8,128)(2,1)S(1)}, u32[]{:S(2)}, u32[]{:S(2)}) collective-permute-start(bf16[32,2304]{1,0:T(8,128)(2,1)S(1)} %get-tuple-element.28), channel_id=1, source_target_pairs={{0,8},{1,40},{2,10},{3,42},{4,12},{5,44},{6,14},{7,46},{8,0},{9,32... | collective-permute-start | bytes 442376 | tf_op jit(solution)/shard_map/ppermute | solution.py:36
  18.8 3.2 %collective-permute-done = bf16[32,2304]{1,0:T(8,128)(2,1)S(1)} collective-permute-done((bf16[32,2304]{1,0:T(8,128)(2,1)S(1)}, bf16[32,2304]{1,0:T(8,128)(2,1)S(1)}, u32[]{:S(2)}, u32[]{:S(2)}) %collective-permute-start) | collective-permute-done | bytes 147488 | tf_op jit(solution)/shard_map/ppermute | solution.py:36
  22.0 3.7 %collective-permute-done.1 = bf16[32,2304]{1,0:T(8,128)(2,1)S(1)} collective-permute-done((bf16[32,2304]{1,0:T(8,128)(2,1)S(1)}, bf16[32,2304]{1,0:T(8,128)(2,1)S(1)}, u32[]{:S(2)}, u32[]{:S(2)}) %collective-permute-start.1) | collective-permute-done | bytes 147488 | tf_op jit(solution)/shard_map/ppermute | solution.py:36
  25.7 1.2 collective-permute-start.6
  27.0 0.1 collective-permute-start.7
  27.1 2.4 %collective-permute-start.8 = (bf16[80,2304]{1,0:T(8,128)(2,1)S(1)}, bf16[80,2304]{1,0:T(8,128)(2,1)S(1)}, u32[]{:S(2)}, u32[]{:S(2)}) collective-permute-start(bf16[80,2304]{1,0:T(8,128)(2,1)S(1)} %fusion.1), channel_id=1, source_target_pairs={{0,6},{1,7},{2,0},{3,1},{4,2},{5,3},{6,4},{7,5},{8,56},{9,57},{10,... | collective-permute-start | bytes 1105928 | tf_op jit(solution)/shard_map/ppermute | solution.py:36
  29.5 8.2 %collective-permute-done.6 = bf16[80,2304]{1,0:T(8,128)(2,1)S(1)} collective-permute-done((bf16[80,2304]{1,0:T(8,128)(2,1)S(1)}, bf16[80,2304]{1,0:T(8,128)(2,1)S(1)}, u32[]{:S(2)}, u32[]{:S(2)}) %collective-permute-start.6) | collective-permute-done | bytes 368672 | tf_op jit(solution)/shard_map/ppermute | solution.py:36
  37.8 0.6 collective-permute-done.8
  38.5 0.1 pad_maximum_fusion
  38.7 1.3 collective-permute-start.15
  40.0 2.5 %collective-permute-start.16 = (bf16[256,2304]{1,0:T(8,128)(2,1)S(1)}, bf16[256,2304]{1,0:T(8,128)(2,1)S(1)}, u32[]{:S(2)}, u32[]{:S(2)}) collective-permute-start(bf16[256,2304]{1,0:T(8,128)(2,1)S(1)} %bitcast.78), channel_id=1, source_target_pairs={{0,32},{1,33},{2,34},{3,35},{4,36},{5,37},{6,38},{7,39},{8,12},{9,... | collective-permute-start | bytes 3538952 | tf_op jit(solution)/shard_map/ppermute | solution.py:36
  42.4 1.2 collective-permute-start.17
  43.6 6.6 %collective-permute-start.10 = (bf16[16,1024]{1,0:T(8,128)(2,1)S(1)}, bf16[16,1024]{1,0:T(8,128)(2,1)S(1)}, u32[]{:S(2)}, u32[]{:S(2)}) collective-permute-start(bf16[16,1024]{1,0:T(8,128)(2,1)S(1)} %fusion.17), channel_id=1, source_target_pairs={{0,128},{1,129},{2,130},{3,131},{4,132},{5,133},{6,134},{7,135},{8... | collective-permute-start | bytes 98312 | tf_op jit(solution)/shard_map/ppermute | solution.py:36
  50.2 2.2 %collective-permute-done.10 = bf16[16,1024]{1,0:T(8,128)(2,1)S(1)} collective-permute-done((bf16[16,1024]{1,0:T(8,128)(2,1)S(1)}, bf16[16,1024]{1,0:T(8,128)(2,1)S(1)}, u32[]{:S(2)}, u32[]{:S(2)}) %collective-permute-start.10) | collective-permute-done | bytes 32800 | tf_op jit(solution)/shard_map/ppermute | solution.py:36
  52.4 1.4 collective-permute-start.9
  53.7 2.7 %collective-permute-done.11 = bf16[16,1024]{1,0:T(8,128)(2,1)S(1)} collective-permute-done((bf16[16,1024]{1,0:T(8,128)(2,1)S(1)}, bf16[16,1024]{1,0:T(8,128)(2,1)S(1)}, u32[]{:S(2)}, u32[]{:S(2)}) %collective-permute-start.11) | collective-permute-done | bytes 32800 | tf_op jit(solution)/shard_map/ppermute | solution.py:36
  56.4 0.6 collective-permute-done.9
  57.0 0.2 collective-permute-start.12
  57.2 1.1 collective-permute-start.13
  58.3 11.0 %collective-permute-done.12 = bf16[16,1024]{1,0:T(8,128)(2,1)S(1)} collective-permute-done((bf16[16,1024]{1,0:T(8,128)(2,1)S(1)}, bf16[16,1024]{1,0:T(8,128)(2,1)S(1)}, u32[]{:S(2)}, u32[]{:S(2)}) %collective-permute-start.12) | collective-permute-done | bytes 32800 | tf_op jit(solution)/shard_map/ppermute | solution.py:36
  69.3 0.4 collective-permute-start.14
  69.7 2.3 %collective-permute-done.14 = bf16[16,1024]{1,0:T(8,128)(2,1)S(1)} collective-permute-done((bf16[16,1024]{1,0:T(8,128)(2,1)S(1)}, bf16[16,1024]{1,0:T(8,128)(2,1)S(1)}, u32[]{:S(2)}, u32[]{:S(2)}) %collective-permute-start.14) | collective-permute-done | bytes 32800 | tf_op jit(solution)/shard_map/ppermute | solution.py:36
  72.0 0.6 add_add_fusion.blocks
  72.7 0.8 broadcast_in_dim.21.offdiag
  73.6 0.2 copy-done.5
  73.7 0.4 copy-done.6
  74.1 12.2 %ladder.1 = (f32[4,16,4,16,128]{4,3,2,1,0:T(8,128)}, f32[16,4,16,128]{3,2,1,0:T(8,128)}, f32[16,4,16,128]{3,2,1,0:T(8,128)}, f32[16,4,16,128]{3,2,1,0:T(8,128)}, f32[16,4,16,128]{3,2,1,0:T(8,128)}) custom-call(s32[1]{0:T(128)} %bitcast.me, f32[64,128]{1,0:T(8,128)} %broadcast_in_dim.21.offdiag, bf16[128,128]{1,0:T(8,128)(2,1)} %constant.67.clone.swap, ...), custom_call_target="tpu_custom_call" | custom-call | tf_op jit(solution)/shard_map/ladder/pallas_call | solution.py:195
  86.3 3.1 %collective-permute-start.18 = (f32[16,4,16,128]{3,2,1,0:T(8,128)}, f32[16,4,16,128]{3,2,1,0:T(8,128)S(1)}, u32[]{:S(2)}, u32[]{:S(2)}) collective-permute-start(f32[16,4,16,128]{3,2,1,0:T(8,128)} %get-tuple-element.11), channel_id=1, source_target_pairs={{0,8},{1,9},{2,10},{3,11},{4,12},{5,13},{6,14},{7,15},{8,0},{9,1},... | collective-permute-start | bytes 1572872 | tf_op jit(solution)/shard_map/ppermute | solution.py:36
  89.3 0.1 collective-permute-start.19
  89.4 0.4 collective-permute-start.21
  89.8 0.1 collective-permute-start.23
  89.9 1.1 collective-permute-done.18
  91.1 0.7 collective-permute-done.19
  91.8 0.7 collective-permute-done.21
  92.6 0.7 collective-permute-done.23
  93.3 2.1 %abs_reduce_fusion.1 = (f32[4,16,128]{2,1,0:T(8,128)S(1)}, f32[4,16,128]{2,1,0:T(8,128)S(1)}, f32[4,16,128]{2,1,0:T(8,128)S(1)}, f32[4,16,128]{2,1,0:T(8,128)S(1)}) fusion(f32[16,4,16,128]{3,2,1,0:T(8,128)S(1)} %collective-permute-done.21, f32[4,16,4,16,128]{4,3,2,1,0:T(8,128)} %get-tuple-element.10, f32[16,4,16,128]{3,2,1,0:T(8,128)S(1)} %collective-permute-done.23, ...), kind=kLoop, calls=%fused_computation.15 | loop fusion | flops 1540096 | bytes 4325376 | tf_op jit(solution)/shard_map/reduce_max | solution.py:215
  95.6 0.5 multiply_convert_fusion.1
  96.1 0.1 pad_maximum_fusion.4
  96.2 1.8 %collective-permute-start.20 = (f16[17,4,16,128]{3,2,1,0:T(8,128)(2,1)S(1)}, f16[17,4,16,128]{3,2,1,0:T(8,128)(2,1)S(1)}, u32[]{:S(2)}, u32[]{:S(2)}) collective-permute-start(f16[17,4,16,128]{3,2,1,0:T(8,128)(2,1)S(1)} %pad_maximum_fusion.4), channel_id=1, source_target_pairs={{0,64},{1,65},{2,66},{3,67},{4,68},{5,69},{6,70},{7,71},{8,10},{9,... | collective-permute-start | bytes 835592 | tf_op jit(solution)/shard_map/ppermute | solution.py:36
  98.1 1.9 %collective-permute-start.22 = (f16[17,4,16,128]{3,2,1,0:T(8,128)(2,1)S(1)}, f16[17,4,16,128]{3,2,1,0:T(8,128)(2,1)S(1)}, u32[]{:S(2)}, u32[]{:S(2)}) collective-permute-start(f16[17,4,16,128]{3,2,1,0:T(8,128)(2,1)S(1)} %pad_maximum_fusion.5), channel_id=1, source_target_pairs={{0,128},{1,129},{2,130},{3,131},{4,132},{5,133},{6,134},{7,135},{8... | collective-permute-start | bytes 835592 | tf_op jit(solution)/shard_map/ppermute | solution.py:36
  100.0 1.4 collective-permute-start.24
  101.5 1.4 collective-permute-done.20
  102.9 4.1 %collective-permute-done.22 = f16[17,4,16,128]{3,2,1,0:T(8,128)(2,1)S(1)} collective-permute-done((f16[17,4,16,128]{3,2,1,0:T(8,128)(2,1)S(1)}, f16[17,4,16,128]{3,2,1,0:T(8,128)(2,1)S(1)}, u32[]{:S(2)}, u32[]{:S(2)}) %collective-permute-start.22) | collective-permute-done | bytes 278560 | tf_op jit(solution)/shard_map/ppermute | solution.py:36
  107.0 0.4 pad_maximum_fusion.1
  107.6 0.5 maximum_select_fusion.2
  108.1 1.8 %collective-permute-start.28 = (f16[17,4,16,128]{3,2,1,0:T(8,128)(2,1)S(1)}, f16[17,4,16,128]{3,2,1,0:T(8,128)(2,1)S(1)}, u32[]{:S(2)}, u32[]{:S(2)}) collective-permute-start(f16[17,4,16,128]{3,2,1,0:T(8,128)(2,1)S(1)} %get-tuple-element.23), channel_id=1, source_target_pairs={{0,6},{1,7},{2,0},{3,1},{4,2},{5,3},{6,4},{7,5},{8,24},{9,56},{10,... | collective-permute-start | bytes 835592 | tf_op jit(solution)/shard_map/ppermute | solution.py:36
  109.9 2.0 %collective-permute-start.27 = (f16[17,4,16,128]{3,2,1,0:T(8,128)(2,1)S(1)}, f16[17,4,16,128]{3,2,1,0:T(8,128)(2,1)S(1)}, u32[]{:S(2)}, u32[]{:S(2)}) collective-permute-start(f16[17,4,16,128]{3,2,1,0:T(8,128)(2,1)S(1)} %get-tuple-element.24), channel_id=1, source_target_pairs={{0,4},{1,5},{2,6},{3,7},{4,0},{5,1},{6,2},{7,3},{8,24},{9,56},{10,... | collective-permute-start | bytes 835592 | tf_op jit(solution)/shard_map/ppermute | solution.py:36
  111.9 1.9 %collective-permute-start.26 = (f16[17,4,16,128]{3,2,1,0:T(8,128)(2,1)S(1)}, f16[17,4,16,128]{3,2,1,0:T(8,128)(2,1)S(1)}, u32[]{:S(2)}, u32[]{:S(2)}) collective-permute-start(f16[17,4,16,128]{3,2,1,0:T(8,128)(2,1)S(1)} %get-tuple-element.25), channel_id=1, source_target_pairs={{0,2},{1,3},{2,4},{3,5},{4,6},{5,7},{6,0},{7,1},{8,8},{9,40},{10,1... | collective-permute-start | bytes 835592 | tf_op jit(solution)/shard_map/ppermute | solution.py:36
  113.9 5.8 %collective-permute-start.25 = (f16[17,4,16,128]{3,2,1,0:T(8,128)(2,1)S(1)}, f16[17,4,16,128]{3,2,1,0:T(8,128)(2,1)S(1)}, u32[]{:S(2)}, u32[]{:S(2)}) collective-permute-start(f16[17,4,16,128]{3,2,1,0:T(8,128)(2,1)S(1)} %get-tuple-element.26), channel_id=1, source_target_pairs={{0,0},{1,1},{2,2},{3,3},{4,4},{5,5},{6,6},{7,7},{8,8},{9,40},{10,1... | collective-permute-start | bytes 835592 | tf_op jit(solution)/shard_map/ppermute | solution.py:36
  119.6 0.3 collective-permute-done.28
  120.1 2.8 %collective-permute-done.27 = f16[17,4,16,128]{3,2,1,0:T(8,128)(2,1)S(1)} collective-permute-done((f16[17,4,16,128]{3,2,1,0:T(8,128)(2,1)S(1)}, f16[17,4,16,128]{3,2,1,0:T(8,128)(2,1)S(1)}, u32[]{:S(2)}, u32[]{:S(2)}) %collective-permute-start.27) | collective-permute-done | bytes 278560 | tf_op jit(solution)/shard_map/ppermute | solution.py:36
  123.0 2.9 %collective-permute-done.26 = f16[17,4,16,128]{3,2,1,0:T(8,128)(2,1)S(1)} collective-permute-done((f16[17,4,16,128]{3,2,1,0:T(8,128)(2,1)S(1)}, f16[17,4,16,128]{3,2,1,0:T(8,128)(2,1)S(1)}, u32[]{:S(2)}, u32[]{:S(2)}) %collective-permute-start.26) | collective-permute-done | bytes 278560 | tf_op jit(solution)/shard_map/ppermute | solution.py:36
  126.0 2.9 %collective-permute-done.25 = f16[17,4,16,128]{3,2,1,0:T(8,128)(2,1)S(1)} collective-permute-done((f16[17,4,16,128]{3,2,1,0:T(8,128)(2,1)S(1)}, f16[17,4,16,128]{3,2,1,0:T(8,128)(2,1)S(1)}, u32[]{:S(2)}, u32[]{:S(2)}) %collective-permute-start.25) | collective-permute-done | bytes 278560 | tf_op jit(solution)/shard_map/ppermute | solution.py:36
  129.1 6.5 %collective-permute-start.29 = (f32[4,8,4,16,128]{4,3,2,1,0:T(8,128)S(1)}, f32[4,8,4,16,128]{4,3,2,1,0:T(8,128)S(1)}, u32[]{:S(2)}, u32[]{:S(2)}) collective-permute-start(f32[4,8,4,16,128]{4,3,2,1,0:T(8,128)S(1)} %split.1), channel_id=1, source_target_pairs={{0,8},{1,9},{2,10},{3,11},{4,12},{5,13},{6,14},{7,15},{8,0},{9,1},... | collective-permute-start | bytes 3145736 | tf_op jit(solution)/shard_map/ppermute | solution.py:36
  135.6 2.3 %collective-permute-done.29.refs_4_ = f32[4,8,4,16,128]{4,3,2,1,0:T(8,128)S(1)} collective-permute-done((f32[4,8,4,16,128]{4,3,2,1,0:T(8,128)S(1)}, f32[4,8,4,16,128]{4,3,2,1,0:T(8,128)S(1)}, u32[]{:S(2)}, u32[]{:S(2)}) %collective-permute-start.29) | collective-permute-done | bytes 1048608 | tf_op jit(solution)/shard_map/ppermute | solution.py:36
  137.9 4.0 %finish.1 = f32[64,32,128]{2,1,0:T(8,128)} custom-call(s32[1]{0:T(128)} %bitcast.me, f32[16,4,16,128]{3,2,1,0:T(8,128)S(1)} %slice_multiply_fusion.3.refs_0_, f32[16,4,16,128]{3,2,1,0:T(8,128)S(1)} %slice_multiply_fusion.2.refs_1_, f32[16,4,16,128]{3,2,1,0:T(8,128)S(1)} %slice_multiply_fusion.1.refs_2_, f32[16,4,16,128]{3,2,1,0:T(8,128)S(1)} %slice_multiply_fusion.refs_3_, ...), custom_call_target="tpu_custom_call" | custom-call | tf_op jit(solution)/shard_map/finish/pallas_call | solution.py:313
  (62 shorter events, 1.4 us)
Async XLA Ops:
  6.5 3.0 %copy-start.2 = (s32[2,2]{1,0:T(2,128)S(1)}, s32[2,2]{1,0:T(2,128)}, u32[]{:S(2)}) copy-start(s32[2,2]{1,0:T(2,128)} %offsets.1) | copy-start | bytes 52
  6.5 3.0 %copy-start.1 = (bf16[64,32,128]{2,1,0:T(8,128)(2,1)S(1)}, bf16[64,32,128]{2,1,0:T(8,128)(2,1)}, u32[]{:S(2)}) copy-start(bf16[64,32,128]{2,1,0:T(8,128)(2,1)} %amplitudes.1) | copy-start | bytes 1572868
  6.5 66.2 %all-gather.2.cloned.1.call-start = ((), (), s32[]{:S(2)}) async-start(), calls=%async_computation | async-start | bytes 2654208 | tf_op jit(solution)/shard_map/all_gather | solution.py:351
  7.8 1.8 %collective-permute-start.2 = (bf16[32,2304]{1,0:T(8,128)(2,1)S(1)}, bf16[32,2304]{1,0:T(8,128)(2,1)S(1)}, u32[]{:S(2)}, u32[]{:S(2)}) collective-permute-start(bf16[32,2304]{1,0:T(8,128)(2,1)S(1)} %get-tuple-element.29), channel_id=1, source_target_pairs={{0,8},{1,9},{2,10},{3,11},{4,12},{5,13},{6,14},{7,15},{8,0},{9,1},... | collective-permute-start | bytes 442376 | tf_op jit(solution)/shard_map/ppermute | solution.py:36
  9.6 9.1 %copy-start = (bf16[64,2304]{1,0:T(8,128)(2,1)}, bf16[64,2304]{1,0:T(8,128)(2,1)S(1)}, u32[]{:S(2)}) copy-start(bf16[64,2304]{1,0:T(8,128)(2,1)S(1)} %pad_maximum_fusion.2._) | copy-start | bytes 884740
  10.2 8.5 %collective-permute-start.3 = (bf16[16,1024]{1,0:T(8,128)(2,1)S(1)}, bf16[16,1024]{1,0:T(8,128)(2,1)S(1)}, u32[]{:S(2)}, u32[]{:S(2)}) collective-permute-start(bf16[16,1024]{1,0:T(8,128)(2,1)S(1)} %blocks.1), channel_id=1, source_target_pairs={{0,8},{1,9},{2,10},{3,11},{4,12},{5,13},{6,14},{7,15},{8,0},{9,1},... | collective-permute-start | bytes 98312 | tf_op jit(solution)/shard_map/ppermute | solution.py:36
  10.7 8.1 %collective-permute-start.4 = (bf16[16,1024]{1,0:T(8,128)(2,1)S(1)}, bf16[16,1024]{1,0:T(8,128)(2,1)S(1)}, u32[]{:S(2)}, u32[]{:S(2)}) collective-permute-start(bf16[16,1024]{1,0:T(8,128)(2,1)S(1)} %blocks.1), channel_id=1, source_target_pairs={{0,1},{1,0},{2,3},{3,2},{4,5},{5,4},{6,7},{7,6},{8,9},{9,8},{10,11... | collective-permute-start | bytes 98312 | tf_op jit(solution)/shard_map/ppermute | solution.py:36
  12.2 6.5 %collective-permute-start.5 = (bf16[16,1024]{1,0:T(8,128)(2,1)S(1)}, bf16[16,1024]{1,0:T(8,128)(2,1)S(1)}, u32[]{:S(2)}, u32[]{:S(2)}) collective-permute-start(bf16[16,1024]{1,0:T(8,128)(2,1)S(1)} %blocks.1), channel_id=1, source_target_pairs={{0,9},{1,8},{2,11},{3,10},{4,13},{5,12},{6,15},{7,14},{8,1},{9,0},... | collective-permute-start | bytes 98312 | tf_op jit(solution)/shard_map/ppermute | solution.py:36
  12.4 9.6 %collective-permute-start = (bf16[32,2304]{1,0:T(8,128)(2,1)S(1)}, bf16[32,2304]{1,0:T(8,128)(2,1)S(1)}, u32[]{:S(2)}, u32[]{:S(2)}) collective-permute-start(bf16[32,2304]{1,0:T(8,128)(2,1)S(1)} %get-tuple-element.27), channel_id=1, source_target_pairs={{0,0},{1,32},{2,2},{3,34},{4,4},{5,36},{6,6},{7,38},{8,8},{9,40},{... | collective-permute-start | bytes 442376 | tf_op jit(solution)/shard_map/ppermute | solution.py:36
  16.8 8.9 %collective-permute-start.1 = (bf16[32,2304]{1,0:T(8,128)(2,1)S(1)}, bf16[32,2304]{1,0:T(8,128)(2,1)S(1)}, u32[]{:S(2)}, u32[]{:S(2)}) collective-permute-start(bf16[32,2304]{1,0:T(8,128)(2,1)S(1)} %get-tuple-element.28), channel_id=1, source_target_pairs={{0,8},{1,40},{2,10},{3,42},{4,12},{5,44},{6,14},{7,46},{8,0},{9,32... | collective-permute-start | bytes 442376 | tf_op jit(solution)/shard_map/ppermute | solution.py:36
  25.7 11.9 %collective-permute-start.6 = (bf16[80,2304]{1,0:T(8,128)(2,1)S(1)}, bf16[80,2304]{1,0:T(8,128)(2,1)S(1)}, u32[]{:S(2)}, u32[]{:S(2)}) collective-permute-start(bf16[80,2304]{1,0:T(8,128)(2,1)S(1)} %fusion.1), channel_id=1, source_target_pairs={{0,2},{1,3},{2,4},{3,5},{4,6},{5,7},{6,0},{7,1},{8,24},{9,25},{10,... | collective-permute-start | bytes 1105928 | tf_op jit(solution)/shard_map/ppermute | solution.py:36
  27.0 10.7 %collective-permute-start.7 = (bf16[80,2304]{1,0:T(8,128)(2,1)S(1)}, bf16[80,2304]{1,0:T(8,128)(2,1)S(1)}, u32[]{:S(2)}, u32[]{:S(2)}) collective-permute-start(bf16[80,2304]{1,0:T(8,128)(2,1)S(1)} %fusion.1), channel_id=1, source_target_pairs={{0,4},{1,5},{2,6},{3,7},{4,0},{5,1},{6,2},{7,3},{8,40},{9,41},{10,... | collective-permute-start | bytes 1105928 | tf_op jit(solution)/shard_map/ppermute | solution.py:36
  27.1 11.4 %collective-permute-start.8 = (bf16[80,2304]{1,0:T(8,128)(2,1)S(1)}, bf16[80,2304]{1,0:T(8,128)(2,1)S(1)}, u32[]{:S(2)}, u32[]{:S(2)}) collective-permute-start(bf16[80,2304]{1,0:T(8,128)(2,1)S(1)} %fusion.1), channel_id=1, source_target_pairs={{0,6},{1,7},{2,0},{3,1},{4,2},{5,3},{6,4},{7,5},{8,56},{9,57},{10,... | collective-permute-start | bytes 1105928 | tf_op jit(solution)/shard_map/ppermute | solution.py:36
  38.5 31.2 %copy-start.7 = (s32[64,2]{0,1:T(2,128)S(1)}, s32[64,2]{0,1:T(2,128)}, u32[]{:S(2)}) copy-start(s32[64,2]{0,1:T(2,128)} %param.5) | copy-start | bytes 1540
  38.7 34.9 %copy-start.4 = (bf16[4,8,8,2304]{3,1,0,2:T(8,128)(2,1)}, bf16[4,8,8,2304]{3,1,0,2:T(8,128)(2,1)S(1)}, u32[]{:S(2)}) copy-start(bf16[4,8,8,2304]{3,1,0,2:T(8,128)(2,1)S(1)} %pad_maximum_fusion) | copy-start | bytes 3538948
  38.7 34.0 %collective-permute-start.15 = (bf16[256,2304]{1,0:T(8,128)(2,1)S(1)}, bf16[256,2304]{1,0:T(8,128)(2,1)S(1)}, u32[]{:S(2)}, u32[]{:S(2)}) collective-permute-start(bf16[256,2304]{1,0:T(8,128)(2,1)S(1)} %bitcast.77), channel_id=1, source_target_pairs={{0,16},{1,17},{2,18},{3,19},{4,20},{5,21},{6,22},{7,23},{8,10},{9,... | collective-permute-start | bytes 3538952 | tf_op jit(solution)/shard_map/ppermute | solution.py:36
  40.0 32.7 %collective-permute-start.16 = (bf16[256,2304]{1,0:T(8,128)(2,1)S(1)}, bf16[256,2304]{1,0:T(8,128)(2,1)S(1)}, u32[]{:S(2)}, u32[]{:S(2)}) collective-permute-start(bf16[256,2304]{1,0:T(8,128)(2,1)S(1)} %bitcast.78), channel_id=1, source_target_pairs={{0,32},{1,33},{2,34},{3,35},{4,36},{5,37},{6,38},{7,39},{8,12},{9,... | collective-permute-start | bytes 3538952 | tf_op jit(solution)/shard_map/ppermute | solution.py:36
  42.4 30.3 %collective-permute-start.17 = (bf16[256,2304]{1,0:T(8,128)(2,1)S(1)}, bf16[256,2304]{1,0:T(8,128)(2,1)}, u32[]{:S(2)}, u32[]{:S(2)}) collective-permute-start(bf16[256,2304]{1,0:T(8,128)(2,1)S(1)} %bitcast.79), channel_id=1, source_target_pairs={{0,48},{1,49},{2,50},{3,51},{4,52},{5,53},{6,54},{7,55},{8,14},{9,... | collective-permute-start | bytes 3538952 | tf_op jit(solution)/shard_map/ppermute | solution.py:36
  43.6 8.8 %collective-permute-start.10 = (bf16[16,1024]{1,0:T(8,128)(2,1)S(1)}, bf16[16,1024]{1,0:T(8,128)(2,1)S(1)}, u32[]{:S(2)}, u32[]{:S(2)}) collective-permute-start(bf16[16,1024]{1,0:T(8,128)(2,1)S(1)} %fusion.17), channel_id=1, source_target_pairs={{0,128},{1,129},{2,130},{3,131},{4,132},{5,133},{6,134},{7,135},{8... | collective-permute-start | bytes 98312 | tf_op jit(solution)/shard_map/ppermute | solution.py:36
  50.2 6.3 %collective-permute-start.11 = (bf16[16,1024]{1,0:T(8,128)(2,1)S(1)}, bf16[16,1024]{1,0:T(8,128)(2,1)S(1)}, u32[]{:S(2)}, u32[]{:S(2)}) collective-permute-start(bf16[16,1024]{1,0:T(8,128)(2,1)S(1)} %fusion.17), channel_id=1, source_target_pairs={{0,192},{1,193},{2,194},{3,195},{4,196},{5,197},{6,198},{7,199},{8... | collective-permute-start | bytes 98312 | tf_op jit(solution)/shard_map/ppermute | solution.py:36
  52.4 4.7 %collective-permute-start.9 = (bf16[16,1024]{1,0:T(8,128)(2,1)S(1)}, bf16[16,1024]{1,0:T(8,128)(2,1)S(1)}, u32[]{:S(2)}, u32[]{:S(2)}) collective-permute-start(bf16[16,1024]{1,0:T(8,128)(2,1)S(1)} %fusion.17), channel_id=1, source_target_pairs={{0,64},{1,65},{2,66},{3,67},{4,68},{5,69},{6,70},{7,71},{8,72},{9,... | collective-permute-start | bytes 98312 | tf_op jit(solution)/shard_map/ppermute | solution.py:36
  57.0 12.3 %collective-permute-start.12 = (bf16[16,1024]{1,0:T(8,128)(2,1)S(1)}, bf16[16,1024]{1,0:T(8,128)(2,1)S(1)}, u32[]{:S(2)}, u32[]{:S(2)}) collective-permute-start(bf16[16,1024]{1,0:T(8,128)(2,1)S(1)} %add_add_fusion.1), channel_id=1, source_target_pairs={{0,16},{1,17},{2,18},{3,19},{4,20},{5,21},{6,22},{7,23},{8,10},{9,... | collective-permute-start | bytes 98312 | tf_op jit(solution)/shard_map/ppermute | solution.py:36
  57.2 12.5 %collective-permute-start.13 = (bf16[16,1024]{1,0:T(8,128)(2,1)S(1)}, bf16[16,1024]{1,0:T(8,128)(2,1)S(1)}, u32[]{:S(2)}, u32[]{:S(2)}) collective-permute-start(bf16[16,1024]{1,0:T(8,128)(2,1)S(1)} %add_add_fusion.1), channel_id=1, source_target_pairs={{0,32},{1,33},{2,34},{3,35},{4,36},{5,37},{6,38},{7,39},{8,12},{9,... | collective-permute-start | bytes 98312 | tf_op jit(solution)/shard_map/ppermute | solution.py:36
  69.3 2.8 %collective-permute-start.14 = (bf16[16,1024]{1,0:T(8,128)(2,1)S(1)}, bf16[16,1024]{1,0:T(8,128)(2,1)S(1)}, u32[]{:S(2)}, u32[]{:S(2)}) collective-permute-start(bf16[16,1024]{1,0:T(8,128)(2,1)S(1)} %add_add_fusion.1), channel_id=1, source_target_pairs={{0,48},{1,49},{2,50},{3,51},{4,52},{5,53},{6,54},{7,55},{8,14},{9,... | collective-permute-start | bytes 98312 | tf_op jit(solution)/shard_map/ppermute | solution.py:36
  72.7 1.1 copy-start.5
  72.7 1.4 copy-start.6
  86.3 4.8 %collective-permute-start.18 = (f32[16,4,16,128]{3,2,1,0:T(8,128)}, f32[16,4,16,128]{3,2,1,0:T(8,128)S(1)}, u32[]{:S(2)}, u32[]{:S(2)}) collective-permute-start(f32[16,4,16,128]{3,2,1,0:T(8,128)} %get-tuple-element.11), channel_id=1, source_target_pairs={{0,8},{1,9},{2,10},{3,11},{4,12},{5,13},{6,14},{7,15},{8,0},{9,1},... | collective-permute-start | bytes 1572872 | tf_op jit(solution)/shard_map/ppermute | solution.py:36
  89.3 2.5 %collective-permute-start.19 = (f32[16,4,16,128]{3,2,1,0:T(8,128)}, f32[16,4,16,128]{3,2,1,0:T(8,128)S(1)}, u32[]{:S(2)}, u32[]{:S(2)}) collective-permute-start(f32[16,4,16,128]{3,2,1,0:T(8,128)} %get-tuple-element.12), channel_id=1, source_target_pairs={{0,8},{1,9},{2,10},{3,11},{4,12},{5,13},{6,14},{7,15},{8,0},{9,1},... | collective-permute-start | bytes 1572872 | tf_op jit(solution)/shard_map/ppermute | solution.py:36
  89.4 3.1 %collective-permute-start.21 = (f32[16,4,16,128]{3,2,1,0:T(8,128)}, f32[16,4,16,128]{3,2,1,0:T(8,128)S(1)}, u32[]{:S(2)}, u32[]{:S(2)}) collective-permute-start(f32[16,4,16,128]{3,2,1,0:T(8,128)} %get-tuple-element.13), channel_id=1, source_target_pairs={{0,8},{1,9},{2,10},{3,11},{4,12},{5,13},{6,14},{7,15},{8,0},{9,1},... | collective-permute-start | bytes 1572872 | tf_op jit(solution)/shard_map/ppermute | solution.py:36
  89.8 3.5 %collective-permute-start.23 = (f32[16,4,16,128]{3,2,1,0:T(8,128)}, f32[16,4,16,128]{3,2,1,0:T(8,128)S(1)}, u32[]{:S(2)}, u32[]{:S(2)}) collective-permute-start(f32[16,4,16,128]{3,2,1,0:T(8,128)} %get-tuple-element.14), channel_id=1, source_target_pairs={{0,8},{1,9},{2,10},{3,11},{4,12},{5,13},{6,14},{7,15},{8,0},{9,1},... | collective-permute-start | bytes 1572872 | tf_op jit(solution)/shard_map/ppermute | solution.py:36
  93.3 2.2 %copy-start.3 = (f32[4,16,4,16,128]{4,3,2,1,0:T(8,128)S(1)}, f32[4,16,4,16,128]{4,3,2,1,0:T(8,128)}, u32[]{:S(2)}) copy-start(f32[4,16,4,16,128]{4,3,2,1,0:T(8,128)} %get-tuple-element.10) | copy-start | bytes 6291460
  96.2 6.7 %collective-permute-start.20 = (f16[17,4,16,128]{3,2,1,0:T(8,128)(2,1)S(1)}, f16[17,4,16,128]{3,2,1,0:T(8,128)(2,1)S(1)}, u32[]{:S(2)}, u32[]{:S(2)}) collective-permute-start(f16[17,4,16,128]{3,2,1,0:T(8,128)(2,1)S(1)} %pad_maximum_fusion.4), channel_id=1, source_target_pairs={{0,64},{1,65},{2,66},{3,67},{4,68},{5,69},{6,70},{7,71},{8,10},{9,... | collective-permute-start | bytes 835592 | tf_op jit(solution)/shard_map/ppermute | solution.py:36
  98.1 8.9 %collective-permute-start.22 = (f16[17,4,16,128]{3,2,1,0:T(8,128)(2,1)S(1)}, f16[17,4,16,128]{3,2,1,0:T(8,128)(2,1)S(1)}, u32[]{:S(2)}, u32[]{:S(2)}) collective-permute-start(f16[17,4,16,128]{3,2,1,0:T(8,128)(2,1)S(1)} %pad_maximum_fusion.5), channel_id=1, source_target_pairs={{0,128},{1,129},{2,130},{3,131},{4,132},{5,133},{6,134},{7,135},{8... | collective-permute-start | bytes 835592 | tf_op jit(solution)/shard_map/ppermute | solution.py:36
  100.0 6.9 %collective-permute-start.24 = (f16[17,4,16,128]{3,2,1,0:T(8,128)(2,1)S(1)}, f16[17,4,16,128]{3,2,1,0:T(8,128)(2,1)S(1)}, u32[]{:S(2)}, u32[]{:S(2)}) collective-permute-start(f16[17,4,16,128]{3,2,1,0:T(8,128)(2,1)S(1)} %pad_maximum_fusion.6), channel_id=1, source_target_pairs={{0,192},{1,193},{2,194},{3,195},{4,196},{5,197},{6,198},{7,199},{8... | collective-permute-start | bytes 835592 | tf_op jit(solution)/shard_map/ppermute | solution.py:36
  108.1 11.9 %collective-permute-start.28 = (f16[17,4,16,128]{3,2,1,0:T(8,128)(2,1)S(1)}, f16[17,4,16,128]{3,2,1,0:T(8,128)(2,1)S(1)}, u32[]{:S(2)}, u32[]{:S(2)}) collective-permute-start(f16[17,4,16,128]{3,2,1,0:T(8,128)(2,1)S(1)} %get-tuple-element.23), channel_id=1, source_target_pairs={{0,6},{1,7},{2,0},{3,1},{4,2},{5,3},{6,4},{7,5},{8,24},{9,56},{10,... | collective-permute-start | bytes 835592 | tf_op jit(solution)/shard_map/ppermute | solution.py:36
  109.9 13.0 %collective-permute-start.27 = (f16[17,4,16,128]{3,2,1,0:T(8,128)(2,1)S(1)}, f16[17,4,16,128]{3,2,1,0:T(8,128)(2,1)S(1)}, u32[]{:S(2)}, u32[]{:S(2)}) collective-permute-start(f16[17,4,16,128]{3,2,1,0:T(8,128)(2,1)S(1)} %get-tuple-element.24), channel_id=1, source_target_pairs={{0,4},{1,5},{2,6},{3,7},{4,0},{5,1},{6,2},{7,3},{8,24},{9,56},{10,... | collective-permute-start | bytes 835592 | tf_op jit(solution)/shard_map/ppermute | solution.py:36
  111.9 14.0 %collective-permute-start.26 = (f16[17,4,16,128]{3,2,1,0:T(8,128)(2,1)S(1)}, f16[17,4,16,128]{3,2,1,0:T(8,128)(2,1)S(1)}, u32[]{:S(2)}, u32[]{:S(2)}) collective-permute-start(f16[17,4,16,128]{3,2,1,0:T(8,128)(2,1)S(1)} %get-tuple-element.25), channel_id=1, source_target_pairs={{0,2},{1,3},{2,4},{3,5},{4,6},{5,7},{6,0},{7,1},{8,8},{9,40},{10,1... | collective-permute-start | bytes 835592 | tf_op jit(solution)/shard_map/ppermute | solution.py:36
  113.9 15.0 %collective-permute-start.25 = (f16[17,4,16,128]{3,2,1,0:T(8,128)(2,1)S(1)}, f16[17,4,16,128]{3,2,1,0:T(8,128)(2,1)S(1)}, u32[]{:S(2)}, u32[]{:S(2)}) collective-permute-start(f16[17,4,16,128]{3,2,1,0:T(8,128)(2,1)S(1)} %get-tuple-element.26), channel_id=1, source_target_pairs={{0,0},{1,1},{2,2},{3,3},{4,4},{5,5},{6,6},{7,7},{8,8},{9,40},{10,1... | collective-permute-start | bytes 835592 | tf_op jit(solution)/shard_map/ppermute | solution.py:36
  129.1 8.8 %collective-permute-start.29 = (f32[4,8,4,16,128]{4,3,2,1,0:T(8,128)S(1)}, f32[4,8,4,16,128]{4,3,2,1,0:T(8,128)S(1)}, u32[]{:S(2)}, u32[]{:S(2)}) collective-permute-start(f32[4,8,4,16,128]{4,3,2,1,0:T(8,128)S(1)} %split.1), channel_id=1, source_target_pairs={{0,8},{1,9},{2,10},{3,11},{4,12},{5,13},{6,14},{7,15},{8,0},{9,1},... | collective-permute-start | bytes 3145736 | tf_op jit(solution)/shard_map/ppermute | solution.py:36
Sparse Core Ops, SparseCore 0:
  18.8 42.4 all-gather.1

commit v4 on v3

--- a/solution.py
+++ b/solution.py
@@ -177,6 +177,8 @@
             mine[kz, at + n] = jnp.where(c == 0, one, two)
             other[kz, at + n] = jnp.where(c == 0, two, one)
         if g % 8 == 7:
+            mine[kz, 16] = jnp.max(jnp.abs(mine[kz, :16]), axis=0)
+            other[kz, 16] = jnp.max(jnp.abs(other[kz, :16]), axis=0)
             to = keep.at[jnp.where(c == 0, kz, kx)]
             pltpu.make_async_copy(mine.at[kz], to, sems.at[kz]).start()
             for k in range(4):
@@ -194,16 +196,16 @@
     f32, bf16 = jnp.float32, jnp.bfloat16
     return pl.pallas_call(
         ladder_kernel,
-        out_shape=[jax.ShapeDtypeStruct((4, 16, 4, 16, 128), f32)]
-        + [jax.ShapeDtypeStruct((16, 4, 16, 128), f32)] * 4,
+        out_shape=[jax.ShapeDtypeStruct((4, 17, 4, 16, 128), f32)]
+        + [jax.ShapeDtypeStruct((17, 4, 16, 128), f32)] * 4,
         in_specs=[SMEM, VMEM, VMEM, VMEM] + [HBM] * 5,
         out_specs=[HBM] * 5,
         scratch_shapes=[
             pltpu.VMEM((512, DEPTH), bf16),
             pltpu.VMEM((BLK, 128, DEPTH), bf16),
             pltpu.VMEM((64, BLK, BLK, 128), f32),
-            pltpu.VMEM((4, 16, 4, 16, 128), f32),
-            pltpu.VMEM((4, 16, 4, 16, 128), f32),
+            pltpu.VMEM((4, 17, 4, 16, 128), f32),
+            pltpu.VMEM((4, 17, 4, 16, 128), f32),
             pltpu.SemaphoreType.DMA((40,)),
         ],
         compiler_params=pltpu.CompilerParams(vmem_limit_bytes=56 << 20),
@@ -212,9 +214,8 @@
 
 
 def pack(block):
-    top = jnp.max(jnp.abs(block), axis=0, keepdims=True)
-    power = jnp.clip(jnp.floor(jnp.log2(top)), -100.0, 100.0)
-    return jnp.concatenate([block * jnp.exp2(14.0 - power), power]).astype(jnp.float16)
+    power = jnp.clip(jnp.floor(jnp.log2(block[16:])), -100.0, 100.0)
+    return jnp.concatenate([block[:16] * jnp.exp2(14.0 - power), power]).astype(jnp.float16)
 
 
 def unpack(block):
@@ -299,13 +300,13 @@
         t = jnp.dot(hi, order, preferred_element_type=jnp.float32) + jnp.dot(
             lo, order, preferred_element_type=jnp.float32
         )
-        for n in range(8):
-            out[:, 8 * g + n, :] = t[64 * n : 64 * n + 64]
+        r1[g] = t.reshape(8, 4, 16, 128)
     for r in range(16):
         t = r2[:, :, :, :, r, :].reshape(128, 128).T
         for b2 in range(2):
             row = r // 4 * 8 + b2 * 4 + r % 4
-            out[:, row, :] = out[:, row, :] + t[64 * b2 : 64 * b2 + 64]
+            one = r1[row // 8, row % 8].reshape(P_SIZE, 128)
+            out[:, row, :] = one + t[64 * b2 : 64 * b2 + 64]
 
 
 def finish(me, own, other):

time: 149 us -> 148 us (level)
    reduce_max x1 -> x0, other arithmetic: 2.14 us -> none  [pack(): top = jnp.max(jnp.abs(block), axis=0, keepdims=True)]
    add x0 -> x1, other arithmetic: none -> 1.98 us  [on_device(): got = [pack(keep[k] + send(give[k], core)) for k in range(4)]]
where the time goes in v4:
time: 148 us; the launch traced here: 147 us
  waiting for transfers between devices  55.6 us (38%)
  starting transfers between devices  54.2 us (37%)
  Pallas kernels  15.6 us (11%)
  between operations  13.9 us (9%)
  other arithmetic  4.85 us (3%)
  local copies, waits for them, and re-layouts  3.12 us (2%)
    ppermute x30, waiting for transfers between devices, send(): return lax.ppermute(block, AXES, pairs)  55.6 us
    ppermute x30, starting transfers between devices, send(): return lax.ppermute(block, AXES, pairs)  54.2 us
    pallas_call x1, Pallas kernels, ladder(): pl.pallas_call(ladder_kernel, out_shape=[jax.ShapeDtypeStruct((4, 17, 4,...  12.3 us
  transfers between devices with their start and end apart: 31, of which 21 were waited for; matrix products, arithmetic and copies ran while one was open for 1% of the time, Pallas kernels for 0%

profile of v4, /device:TPU:33, one launch (start us, length us, event | category | flops | bytes accessed | tf_op | source)
XLA Modules:
  0.0 147.3 jit_solution(4866919645833604221)
XLA Ops:
  6.5 1.2 dynamic-slice_bitcast_fusion.3
  7.8 0.8 collective-permute-start.2
  8.5 1.0 collective-permute-done.2
  9.6 0.6 blocks.1
  10.2 0.5 collective-permute-start.3
  10.7 1.6 %collective-permute-start.4 = (bf16[16,1024]{1,0:T(8,128)(2,1)S(1)}, bf16[16,1024]{1,0:T(8,128)(2,1)S(1)}, u32[]{:S(2)}, u32[]{:S(2)}) collective-permute-start(bf16[16,1024]{1,0:T(8,128)(2,1)S(1)} %blocks.1), channel_id=1, source_target_pairs={{0,1},{1,0},{2,3},{3,2},{4,5},{5,4},{6,7},{7,6},{8,9},{9,8},{10,11... | collective-permute-start | bytes 98312 | tf_op jit(solution)/shard_map/ppermute | solution.py:36
  12.2 0.2 collective-permute-start.5
  12.4 4.4 %collective-permute-start = (bf16[32,2304]{1,0:T(8,128)(2,1)S(1)}, bf16[32,2304]{1,0:T(8,128)(2,1)S(1)}, u32[]{:S(2)}, u32[]{:S(2)}) collective-permute-start(bf16[32,2304]{1,0:T(8,128)(2,1)S(1)} %get-tuple-element.23), channel_id=1, source_target_pairs={{0,0},{1,32},{2,2},{3,34},{4,4},{5,36},{6,6},{7,38},{8,8},{9,40},{... | collective-permute-start | bytes 442376 | tf_op jit(solution)/shard_map/ppermute | solution.py:36
  16.8 1.9 %collective-permute-start.1 = (bf16[32,2304]{1,0:T(8,128)(2,1)S(1)}, bf16[32,2304]{1,0:T(8,128)(2,1)S(1)}, u32[]{:S(2)}, u32[]{:S(2)}) collective-permute-start(bf16[32,2304]{1,0:T(8,128)(2,1)S(1)} %get-tuple-element.24), channel_id=1, source_target_pairs={{0,8},{1,40},{2,10},{3,42},{4,12},{5,44},{6,14},{7,46},{8,0},{9,32... | collective-permute-start | bytes 442376 | tf_op jit(solution)/shard_map/ppermute | solution.py:36
  18.8 3.2 %collective-permute-done = bf16[32,2304]{1,0:T(8,128)(2,1)S(1)} collective-permute-done((bf16[32,2304]{1,0:T(8,128)(2,1)S(1)}, bf16[32,2304]{1,0:T(8,128)(2,1)S(1)}, u32[]{:S(2)}, u32[]{:S(2)}) %collective-permute-start) | collective-permute-done | bytes 147488 | tf_op jit(solution)/shard_map/ppermute | solution.py:36
  22.0 3.7 %collective-permute-done.1 = bf16[32,2304]{1,0:T(8,128)(2,1)S(1)} collective-permute-done((bf16[32,2304]{1,0:T(8,128)(2,1)S(1)}, bf16[32,2304]{1,0:T(8,128)(2,1)S(1)}, u32[]{:S(2)}, u32[]{:S(2)}) %collective-permute-start.1) | collective-permute-done | bytes 147488 | tf_op jit(solution)/shard_map/ppermute | solution.py:36
  25.7 1.2 collective-permute-start.6
  27.0 0.1 collective-permute-start.7
  27.1 2.4 %collective-permute-start.8 = (bf16[80,2304]{1,0:T(8,128)(2,1)S(1)}, bf16[80,2304]{1,0:T(8,128)(2,1)S(1)}, u32[]{:S(2)}, u32[]{:S(2)}) collective-permute-start(bf16[80,2304]{1,0:T(8,128)(2,1)S(1)} %fusion.5), channel_id=1, source_target_pairs={{0,6},{1,7},{2,0},{3,1},{4,2},{5,3},{6,4},{7,5},{8,56},{9,57},{10,... | collective-permute-start | bytes 1105928 | tf_op jit(solution)/shard_map/ppermute | solution.py:36
  29.5 8.2 %collective-permute-done.6 = bf16[80,2304]{1,0:T(8,128)(2,1)S(1)} collective-permute-done((bf16[80,2304]{1,0:T(8,128)(2,1)S(1)}, bf16[80,2304]{1,0:T(8,128)(2,1)S(1)}, u32[]{:S(2)}, u32[]{:S(2)}) %collective-permute-start.6) | collective-permute-done | bytes 368672 | tf_op jit(solution)/shard_map/ppermute | solution.py:36
  37.8 0.6 collective-permute-done.8
  38.5 0.1 pad_maximum_fusion
  38.7 1.3 collective-permute-start.15
  40.0 2.5 %collective-permute-start.16 = (bf16[256,2304]{1,0:T(8,128)(2,1)S(1)}, bf16[256,2304]{1,0:T(8,128)(2,1)S(1)}, u32[]{:S(2)}, u32[]{:S(2)}) collective-permute-start(bf16[256,2304]{1,0:T(8,128)(2,1)S(1)} %bitcast.62), channel_id=1, source_target_pairs={{0,32},{1,33},{2,34},{3,35},{4,36},{5,37},{6,38},{7,39},{8,12},{9,... | collective-permute-start | bytes 3538952 | tf_op jit(solution)/shard_map/ppermute | solution.py:36
  42.4 1.2 collective-permute-start.17
  43.6 6.6 %collective-permute-start.10 = (bf16[16,1024]{1,0:T(8,128)(2,1)S(1)}, bf16[16,1024]{1,0:T(8,128)(2,1)S(1)}, u32[]{:S(2)}, u32[]{:S(2)}) collective-permute-start(bf16[16,1024]{1,0:T(8,128)(2,1)S(1)} %fusion.33), channel_id=1, source_target_pairs={{0,128},{1,129},{2,130},{3,131},{4,132},{5,133},{6,134},{7,135},{8... | collective-permute-start | bytes 98312 | tf_op jit(solution)/shard_map/ppermute | solution.py:36
  50.2 2.3 %collective-permute-done.10 = bf16[16,1024]{1,0:T(8,128)(2,1)S(1)} collective-permute-done((bf16[16,1024]{1,0:T(8,128)(2,1)S(1)}, bf16[16,1024]{1,0:T(8,128)(2,1)S(1)}, u32[]{:S(2)}, u32[]{:S(2)}) %collective-permute-start.10) | collective-permute-done | bytes 32800 | tf_op jit(solution)/shard_map/ppermute | solution.py:36
  52.4 1.3 collective-permute-start.9
  53.7 2.7 %collective-permute-done.11 = bf16[16,1024]{1,0:T(8,128)(2,1)S(1)} collective-permute-done((bf16[16,1024]{1,0:T(8,128)(2,1)S(1)}, bf16[16,1024]{1,0:T(8,128)(2,1)S(1)}, u32[]{:S(2)}, u32[]{:S(2)}) %collective-permute-start.11) | collective-permute-done | bytes 32800 | tf_op jit(solution)/shard_map/ppermute | solution.py:36
  56.4 0.6 collective-permute-done.9
  57.1 0.1 collective-permute-start.12
  57.2 1.1 collective-permute-start.13
  58.4 10.9 %collective-permute-done.12 = bf16[16,1024]{1,0:T(8,128)(2,1)S(1)} collective-permute-done((bf16[16,1024]{1,0:T(8,128)(2,1)S(1)}, bf16[16,1024]{1,0:T(8,128)(2,1)S(1)}, u32[]{:S(2)}, u32[]{:S(2)}) %collective-permute-start.12) | collective-permute-done | bytes 32800 | tf_op jit(solution)/shard_map/ppermute | solution.py:36
  69.3 0.4 collective-permute-start.14
  69.7 2.3 %collective-permute-done.14 = bf16[16,1024]{1,0:T(8,128)(2,1)S(1)} collective-permute-done((bf16[16,1024]{1,0:T(8,128)(2,1)S(1)}, bf16[16,1024]{1,0:T(8,128)(2,1)S(1)}, u32[]{:S(2)}, u32[]{:S(2)}) %collective-permute-start.14) | collective-permute-done | bytes 32800 | tf_op jit(solution)/shard_map/ppermute | solution.py:36
  72.0 0.6 add_add_fusion.blocks
  72.7 0.9 broadcast_in_dim.17.offdiag
  73.6 0.1 copy-done.4
  73.7 0.4 copy-done.5
  74.2 12.3 %ladder.1 = (f32[4,17,4,16,128]{4,3,2,1,0:T(8,128)}, f32[17,4,16,128]{3,2,1,0:T(8,128)}, f32[17,4,16,128]{3,2,1,0:T(8,128)}, f32[17,4,16,128]{3,2,1,0:T(8,128)}, f32[17,4,16,128]{3,2,1,0:T(8,128)}) custom-call(s32[1]{0:T(128)} %bitcast.me, f32[64,128]{1,0:T(8,128)} %broadcast_in_dim.17.offdiag, bf16[128,128]{1,0:T(8,128)(2,1)} %constant.65.clone.swap, ...), custom_call_target="tpu_custom_call" | custom-call | tf_op jit(solution)/shard_map/ladder/pallas_call | solution.py:197
  86.5 3.1 %collective-permute-start.18 = (f32[17,4,16,128]{3,2,1,0:T(8,128)}, f32[17,4,16,128]{3,2,1,0:T(8,128)S(1)}, u32[]{:S(2)}, u32[]{:S(2)}) collective-permute-start(f32[17,4,16,128]{3,2,1,0:T(8,128)} %get-tuple-element.11), channel_id=1, source_target_pairs={{0,8},{1,9},{2,10},{3,11},{4,12},{5,13},{6,14},{7,15},{8,0},{9,1},... | collective-permute-start | bytes 1671176 | tf_op jit(solution)/shard_map/ppermute | solution.py:36
  89.5 0.1 collective-permute-start.19
  89.6 0.4 collective-permute-start.21
  90.0 0.1 collective-permute-start.23
  90.1 1.2 collective-permute-done.18
  91.3 0.8 collective-permute-done.19
  92.1 0.8 collective-permute-done.21
  92.9 0.8 collective-permute-done.23
  93.7 2.0 %bitcast_add_fusion.1 = (f32[17,4,16,128]{3,2,1,0:T(8,128)S(1)}, f32[17,4,16,128]{3,2,1,0:T(8,128)S(1)}, f32[17,4,16,128]{3,2,1,0:T(8,128)S(1)}, f32[17,4,16,128]{3,2,1,0:T(8,128)S(1)}) fusion(f32[17,4,16,128]{3,2,1,0:T(8,128)S(1)} %collective-permute-done.21, f32[4,17,4,16,128]{4,3,2,1,0:T(8,128)} %get-tuple-element.10, ...), kind=kLoop, calls=%fused_computation.5 | loop fusion | flops 557056 | bytes 6684672 | tf_op jit(solution)/shard_map/add | solution.py:387
  95.9 0.1 pad_maximum_fusion.4
  96.0 1.8 %collective-permute-start.20 = (f16[17,4,16,128]{3,2,1,0:T(8,128)(2,1)S(1)}, f16[17,4,16,128]{3,2,1,0:T(8,128)(2,1)S(1)}, u32[]{:S(2)}, u32[]{:S(2)}) collective-permute-start(f16[17,4,16,128]{3,2,1,0:T(8,128)(2,1)S(1)} %pad_maximum_fusion.4), channel_id=1, source_target_pairs={{0,64},{1,65},{2,66},{3,67},{4,68},{5,69},{6,70},{7,71},{8,10},{9,... | collective-permute-start | bytes 835592 | tf_op jit(solution)/shard_map/ppermute | solution.py:36
  97.9 0.1 pad_maximum_fusion.5
  97.9 1.9 %collective-permute-start.22 = (f16[17,4,16,128]{3,2,1,0:T(8,128)(2,1)S(1)}, f16[17,4,16,128]{3,2,1,0:T(8,128)(2,1)S(1)}, u32[]{:S(2)}, u32[]{:S(2)}) collective-permute-start(f16[17,4,16,128]{3,2,1,0:T(8,128)(2,1)S(1)} %pad_maximum_fusion.5), channel_id=1, source_target_pairs={{0,128},{1,129},{2,130},{3,131},{4,132},{5,133},{6,134},{7,135},{8... | collective-permute-start | bytes 835592 | tf_op jit(solution)/shard_map/ppermute | solution.py:36
  100.1 1.4 collective-permute-start.24
  101.6 1.1 collective-permute-done.20
  102.7 4.1 %collective-permute-done.22 = f16[17,4,16,128]{3,2,1,0:T(8,128)(2,1)S(1)} collective-permute-done((f16[17,4,16,128]{3,2,1,0:T(8,128)(2,1)S(1)}, f16[17,4,16,128]{3,2,1,0:T(8,128)(2,1)S(1)}, u32[]{:S(2)}, u32[]{:S(2)}) %collective-permute-start.22) | collective-permute-done | bytes 278560 | tf_op jit(solution)/shard_map/ppermute | solution.py:36
  106.8 0.4 pad_maximum_fusion.1
  107.4 0.5 maximum_select_fusion.2
  107.9 1.8 %collective-permute-start.28 = (f16[17,4,16,128]{3,2,1,0:T(8,128)(2,1)S(1)}, f16[17,4,16,128]{3,2,1,0:T(8,128)(2,1)S(1)}, u32[]{:S(2)}, u32[]{:S(2)}) collective-permute-start(f16[17,4,16,128]{3,2,1,0:T(8,128)(2,1)S(1)} %get-tuple-element.19), channel_id=1, source_target_pairs={{0,6},{1,7},{2,0},{3,1},{4,2},{5,3},{6,4},{7,5},{8,24},{9,56},{10,... | collective-permute-start | bytes 835592 | tf_op jit(solution)/shard_map/ppermute | solution.py:36
  109.8 2.0 %collective-permute-start.27 = (f16[17,4,16,128]{3,2,1,0:T(8,128)(2,1)S(1)}, f16[17,4,16,128]{3,2,1,0:T(8,128)(2,1)S(1)}, u32[]{:S(2)}, u32[]{:S(2)}) collective-permute-start(f16[17,4,16,128]{3,2,1,0:T(8,128)(2,1)S(1)} %get-tuple-element.20), channel_id=1, source_target_pairs={{0,4},{1,5},{2,6},{3,7},{4,0},{5,1},{6,2},{7,3},{8,24},{9,56},{10,... | collective-permute-start | bytes 835592 | tf_op jit(solution)/shard_map/ppermute | solution.py:36
  111.8 1.9 %collective-permute-start.26 = (f16[17,4,16,128]{3,2,1,0:T(8,128)(2,1)S(1)}, f16[17,4,16,128]{3,2,1,0:T(8,128)(2,1)S(1)}, u32[]{:S(2)}, u32[]{:S(2)}) collective-permute-start(f16[17,4,16,128]{3,2,1,0:T(8,128)(2,1)S(1)} %get-tuple-element.21), channel_id=1, source_target_pairs={{0,2},{1,3},{2,4},{3,5},{4,6},{5,7},{6,0},{7,1},{8,8},{9,40},{10,1... | collective-permute-start | bytes 835592 | tf_op jit(solution)/shard_map/ppermute | solution.py:36
  113.7 5.8 %collective-permute-start.25 = (f16[17,4,16,128]{3,2,1,0:T(8,128)(2,1)S(1)}, f16[17,4,16,128]{3,2,1,0:T(8,128)(2,1)S(1)}, u32[]{:S(2)}, u32[]{:S(2)}) collective-permute-start(f16[17,4,16,128]{3,2,1,0:T(8,128)(2,1)S(1)} %get-tuple-element.22), channel_id=1, source_target_pairs={{0,0},{1,1},{2,2},{3,3},{4,4},{5,5},{6,6},{7,7},{8,8},{9,40},{10,1... | collective-permute-start | bytes 835592 | tf_op jit(solution)/shard_map/ppermute | solution.py:36
  119.5 0.4 collective-permute-done.28
  120.0 2.8 %collective-permute-done.27 = f16[17,4,16,128]{3,2,1,0:T(8,128)(2,1)S(1)} collective-permute-done((f16[17,4,16,128]{3,2,1,0:T(8,128)(2,1)S(1)}, f16[17,4,16,128]{3,2,1,0:T(8,128)(2,1)S(1)}, u32[]{:S(2)}, u32[]{:S(2)}) %collective-permute-start.27) | collective-permute-done | bytes 278560 | tf_op jit(solution)/shard_map/ppermute | solution.py:36
  122.9 2.9 %collective-permute-done.26 = f16[17,4,16,128]{3,2,1,0:T(8,128)(2,1)S(1)} collective-permute-done((f16[17,4,16,128]{3,2,1,0:T(8,128)(2,1)S(1)}, f16[17,4,16,128]{3,2,1,0:T(8,128)(2,1)S(1)}, u32[]{:S(2)}, u32[]{:S(2)}) %collective-permute-start.26) | collective-permute-done | bytes 278560 | tf_op jit(solution)/shard_map/ppermute | solution.py:36
  125.9 2.9 %collective-permute-done.25 = f16[17,4,16,128]{3,2,1,0:T(8,128)(2,1)S(1)} collective-permute-done((f16[17,4,16,128]{3,2,1,0:T(8,128)(2,1)S(1)}, f16[17,4,16,128]{3,2,1,0:T(8,128)(2,1)S(1)}, u32[]{:S(2)}, u32[]{:S(2)}) %collective-permute-start.25) | collective-permute-done | bytes 278560 | tf_op jit(solution)/shard_map/ppermute | solution.py:36
  129.0 6.6 %collective-permute-start.29 = (f32[4,8,4,16,128]{4,3,2,1,0:T(8,128)S(1)}, f32[4,8,4,16,128]{4,3,2,1,0:T(8,128)S(1)}, u32[]{:S(2)}, u32[]{:S(2)}) collective-permute-start(f32[4,8,4,16,128]{4,3,2,1,0:T(8,128)S(1)} %split.1), channel_id=1, source_target_pairs={{0,8},{1,9},{2,10},{3,11},{4,12},{5,13},{6,14},{7,15},{8,0},{9,1},... | collective-permute-start | bytes 3145736 | tf_op jit(solution)/shard_map/ppermute | solution.py:36
  135.6 2.3 %collective-permute-done.29.refs_4_ = f32[4,8,4,16,128]{4,3,2,1,0:T(8,128)S(1)} collective-permute-done((f32[4,8,4,16,128]{4,3,2,1,0:T(8,128)S(1)}, f32[4,8,4,16,128]{4,3,2,1,0:T(8,128)S(1)}, u32[]{:S(2)}, u32[]{:S(2)}) %collective-permute-start.29) | collective-permute-done | bytes 1048608 | tf_op jit(solution)/shard_map/ppermute | solution.py:36
  137.8 2.6 %finish.1 = f32[64,32,128]{2,1,0:T(8,128)} custom-call(s32[1]{0:T(128)} %bitcast.me, f32[16,4,16,128]{3,2,1,0:T(8,128)S(1)} %slice_multiply_fusion.3.refs_0_, f32[16,4,16,128]{3,2,1,0:T(8,128)S(1)} %slice_multiply_fusion.2.refs_1_, f32[16,4,16,128]{3,2,1,0:T(8,128)S(1)} %slice_multiply_fusion.1.refs_2_, f32[16,4,16,128]{3,2,1,0:T(8,128)S(1)} %slice_multiply_fusion.refs_3_, ...), custom_call_target="tpu_custom_call" | custom-call | tf_op jit(solution)/shard_map/finish/pallas_call | solution.py:314
  (66 shorter events, 1.7 us)
Async XLA Ops:
  6.5 3.0 %copy-start.2 = (s32[2,2]{1,0:T(2,128)S(1)}, s32[2,2]{1,0:T(2,128)}, u32[]{:S(2)}) copy-start(s32[2,2]{1,0:T(2,128)} %offsets.1) | copy-start | bytes 52
  6.5 3.0 %copy-start.1 = (bf16[64,32,128]{2,1,0:T(8,128)(2,1)S(1)}, bf16[64,32,128]{2,1,0:T(8,128)(2,1)}, u32[]{:S(2)}) copy-start(bf16[64,32,128]{2,1,0:T(8,128)(2,1)} %amplitudes.1) | copy-start | bytes 1572868
  6.5 66.2 %all-gather.2.cloned.1.call-start = ((), (), s32[]{:S(2)}) async-start(), calls=%async_computation | async-start | bytes 2654208 | tf_op jit(solution)/shard_map/all_gather | solution.py:352
  7.8 1.8 %collective-permute-start.2 = (bf16[32,2304]{1,0:T(8,128)(2,1)S(1)}, bf16[32,2304]{1,0:T(8,128)(2,1)S(1)}, u32[]{:S(2)}, u32[]{:S(2)}) collective-permute-start(bf16[32,2304]{1,0:T(8,128)(2,1)S(1)} %get-tuple-element.25), channel_id=1, source_target_pairs={{0,8},{1,9},{2,10},{3,11},{4,12},{5,13},{6,14},{7,15},{8,0},{9,1},... | collective-permute-start | bytes 442376 | tf_op jit(solution)/shard_map/ppermute | solution.py:36
  9.6 9.1 %copy-start = (bf16[64,2304]{1,0:T(8,128)(2,1)}, bf16[64,2304]{1,0:T(8,128)(2,1)S(1)}, u32[]{:S(2)}) copy-start(bf16[64,2304]{1,0:T(8,128)(2,1)S(1)} %pad_maximum_fusion.2._) | copy-start | bytes 884740
  10.2 8.5 %collective-permute-start.3 = (bf16[16,1024]{1,0:T(8,128)(2,1)S(1)}, bf16[16,1024]{1,0:T(8,128)(2,1)S(1)}, u32[]{:S(2)}, u32[]{:S(2)}) collective-permute-start(bf16[16,1024]{1,0:T(8,128)(2,1)S(1)} %blocks.1), channel_id=1, source_target_pairs={{0,8},{1,9},{2,10},{3,11},{4,12},{5,13},{6,14},{7,15},{8,0},{9,1},... | collective-permute-start | bytes 98312 | tf_op jit(solution)/shard_map/ppermute | solution.py:36
  10.7 8.1 %collective-permute-start.4 = (bf16[16,1024]{1,0:T(8,128)(2,1)S(1)}, bf16[16,1024]{1,0:T(8,128)(2,1)S(1)}, u32[]{:S(2)}, u32[]{:S(2)}) collective-permute-start(bf16[16,1024]{1,0:T(8,128)(2,1)S(1)} %blocks.1), channel_id=1, source_target_pairs={{0,1},{1,0},{2,3},{3,2},{4,5},{5,4},{6,7},{7,6},{8,9},{9,8},{10,11... | collective-permute-start | bytes 98312 | tf_op jit(solution)/shard_map/ppermute | solution.py:36
  12.2 6.5 %collective-permute-start.5 = (bf16[16,1024]{1,0:T(8,128)(2,1)S(1)}, bf16[16,1024]{1,0:T(8,128)(2,1)S(1)}, u32[]{:S(2)}, u32[]{:S(2)}) collective-permute-start(bf16[16,1024]{1,0:T(8,128)(2,1)S(1)} %blocks.1), channel_id=1, source_target_pairs={{0,9},{1,8},{2,11},{3,10},{4,13},{5,12},{6,15},{7,14},{8,1},{9,0},... | collective-permute-start | bytes 98312 | tf_op jit(solution)/shard_map/ppermute | solution.py:36
  12.4 9.6 %collective-permute-start = (bf16[32,2304]{1,0:T(8,128)(2,1)S(1)}, bf16[32,2304]{1,0:T(8,128)(2,1)S(1)}, u32[]{:S(2)}, u32[]{:S(2)}) collective-permute-start(bf16[32,2304]{1,0:T(8,128)(2,1)S(1)} %get-tuple-element.23), channel_id=1, source_target_pairs={{0,0},{1,32},{2,2},{3,34},{4,4},{5,36},{6,6},{7,38},{8,8},{9,40},{... | collective-permute-start | bytes 442376 | tf_op jit(solution)/shard_map/ppermute | solution.py:36
  16.8 8.9 %collective-permute-start.1 = (bf16[32,2304]{1,0:T(8,128)(2,1)S(1)}, bf16[32,2304]{1,0:T(8,128)(2,1)S(1)}, u32[]{:S(2)}, u32[]{:S(2)}) collective-permute-start(bf16[32,2304]{1,0:T(8,128)(2,1)S(1)} %get-tuple-element.24), channel_id=1, source_target_pairs={{0,8},{1,40},{2,10},{3,42},{4,12},{5,44},{6,14},{7,46},{8,0},{9,32... | collective-permute-start | bytes 442376 | tf_op jit(solution)/shard_map/ppermute | solution.py:36
  25.7 11.9 %collective-permute-start.6 = (bf16[80,2304]{1,0:T(8,128)(2,1)S(1)}, bf16[80,2304]{1,0:T(8,128)(2,1)S(1)}, u32[]{:S(2)}, u32[]{:S(2)}) collective-permute-start(bf16[80,2304]{1,0:T(8,128)(2,1)S(1)} %fusion.5), channel_id=1, source_target_pairs={{0,2},{1,3},{2,4},{3,5},{4,6},{5,7},{6,0},{7,1},{8,24},{9,25},{10,... | collective-permute-start | bytes 1105928 | tf_op jit(solution)/shard_map/ppermute | solution.py:36
  27.0 10.7 %collective-permute-start.7 = (bf16[80,2304]{1,0:T(8,128)(2,1)S(1)}, bf16[80,2304]{1,0:T(8,128)(2,1)S(1)}, u32[]{:S(2)}, u32[]{:S(2)}) collective-permute-start(bf16[80,2304]{1,0:T(8,128)(2,1)S(1)} %fusion.5), channel_id=1, source_target_pairs={{0,4},{1,5},{2,6},{3,7},{4,0},{5,1},{6,2},{7,3},{8,40},{9,41},{10,... | collective-permute-start | bytes 1105928 | tf_op jit(solution)/shard_map/ppermute | solution.py:36
  27.1 11.4 %collective-permute-start.8 = (bf16[80,2304]{1,0:T(8,128)(2,1)S(1)}, bf16[80,2304]{1,0:T(8,128)(2,1)S(1)}, u32[]{:S(2)}, u32[]{:S(2)}) collective-permute-start(bf16[80,2304]{1,0:T(8,128)(2,1)S(1)} %fusion.5), channel_id=1, source_target_pairs={{0,6},{1,7},{2,0},{3,1},{4,2},{5,3},{6,4},{7,5},{8,56},{9,57},{10,... | collective-permute-start | bytes 1105928 | tf_op jit(solution)/shard_map/ppermute | solution.py:36
  38.5 31.2 %copy-start.6 = (s32[64,2]{0,1:T(2,128)S(1)}, s32[64,2]{0,1:T(2,128)}, u32[]{:S(2)}) copy-start(s32[64,2]{0,1:T(2,128)} %param.5) | copy-start | bytes 1540
  38.7 34.9 %copy-start.3 = (bf16[4,8,8,2304]{3,1,0,2:T(8,128)(2,1)}, bf16[4,8,8,2304]{3,1,0,2:T(8,128)(2,1)S(1)}, u32[]{:S(2)}) copy-start(bf16[4,8,8,2304]{3,1,0,2:T(8,128)(2,1)S(1)} %pad_maximum_fusion) | copy-start | bytes 3538948
  38.7 34.0 %collective-permute-start.15 = (bf16[256,2304]{1,0:T(8,128)(2,1)S(1)}, bf16[256,2304]{1,0:T(8,128)(2,1)S(1)}, u32[]{:S(2)}, u32[]{:S(2)}) collective-permute-start(bf16[256,2304]{1,0:T(8,128)(2,1)S(1)} %bitcast.61), channel_id=1, source_target_pairs={{0,16},{1,17},{2,18},{3,19},{4,20},{5,21},{6,22},{7,23},{8,10},{9,... | collective-permute-start | bytes 3538952 | tf_op jit(solution)/shard_map/ppermute | solution.py:36
  40.0 32.7 %collective-permute-start.16 = (bf16[256,2304]{1,0:T(8,128)(2,1)S(1)}, bf16[256,2304]{1,0:T(8,128)(2,1)S(1)}, u32[]{:S(2)}, u32[]{:S(2)}) collective-permute-start(bf16[256,2304]{1,0:T(8,128)(2,1)S(1)} %bitcast.62), channel_id=1, source_target_pairs={{0,32},{1,33},{2,34},{3,35},{4,36},{5,37},{6,38},{7,39},{8,12},{9,... | collective-permute-start | bytes 3538952 | tf_op jit(solution)/shard_map/ppermute | solution.py:36
  42.4 30.3 %collective-permute-start.17 = (bf16[256,2304]{1,0:T(8,128)(2,1)S(1)}, bf16[256,2304]{1,0:T(8,128)(2,1)}, u32[]{:S(2)}, u32[]{:S(2)}) collective-permute-start(bf16[256,2304]{1,0:T(8,128)(2,1)S(1)} %bitcast.63), channel_id=1, source_target_pairs={{0,48},{1,49},{2,50},{3,51},{4,52},{5,53},{6,54},{7,55},{8,14},{9,... | collective-permute-start | bytes 3538952 | tf_op jit(solution)/shard_map/ppermute | solution.py:36
  43.6 8.9 %collective-permute-start.10 = (bf16[16,1024]{1,0:T(8,128)(2,1)S(1)}, bf16[16,1024]{1,0:T(8,128)(2,1)S(1)}, u32[]{:S(2)}, u32[]{:S(2)}) collective-permute-start(bf16[16,1024]{1,0:T(8,128)(2,1)S(1)} %fusion.33), channel_id=1, source_target_pairs={{0,128},{1,129},{2,130},{3,131},{4,132},{5,133},{6,134},{7,135},{8... | collective-permute-start | bytes 98312 | tf_op jit(solution)/shard_map/ppermute | solution.py:36
  50.2 6.3 %collective-permute-start.11 = (bf16[16,1024]{1,0:T(8,128)(2,1)S(1)}, bf16[16,1024]{1,0:T(8,128)(2,1)S(1)}, u32[]{:S(2)}, u32[]{:S(2)}) collective-permute-start(bf16[16,1024]{1,0:T(8,128)(2,1)S(1)} %fusion.33), channel_id=1, source_target_pairs={{0,192},{1,193},{2,194},{3,195},{4,196},{5,197},{6,198},{7,199},{8... | collective-permute-start | bytes 98312 | tf_op jit(solution)/shard_map/ppermute | solution.py:36
  52.4 4.6 %collective-permute-start.9 = (bf16[16,1024]{1,0:T(8,128)(2,1)S(1)}, bf16[16,1024]{1,0:T(8,128)(2,1)S(1)}, u32[]{:S(2)}, u32[]{:S(2)}) collective-permute-start(bf16[16,1024]{1,0:T(8,128)(2,1)S(1)} %fusion.33), channel_id=1, source_target_pairs={{0,64},{1,65},{2,66},{3,67},{4,68},{5,69},{6,70},{7,71},{8,72},{9,... | collective-permute-start | bytes 98312 | tf_op jit(solution)/shard_map/ppermute | solution.py:36
  57.1 12.2 %collective-permute-start.12 = (bf16[16,1024]{1,0:T(8,128)(2,1)S(1)}, bf16[16,1024]{1,0:T(8,128)(2,1)S(1)}, u32[]{:S(2)}, u32[]{:S(2)}) collective-permute-start(bf16[16,1024]{1,0:T(8,128)(2,1)S(1)} %add_add_fusion.1), channel_id=1, source_target_pairs={{0,16},{1,17},{2,18},{3,19},{4,20},{5,21},{6,22},{7,23},{8,10},{9,... | collective-permute-start | bytes 98312 | tf_op jit(solution)/shard_map/ppermute | solution.py:36
  57.2 12.5 %collective-permute-start.13 = (bf16[16,1024]{1,0:T(8,128)(2,1)S(1)}, bf16[16,1024]{1,0:T(8,128)(2,1)S(1)}, u32[]{:S(2)}, u32[]{:S(2)}) collective-permute-start(bf16[16,1024]{1,0:T(8,128)(2,1)S(1)} %add_add_fusion.1), channel_id=1, source_target_pairs={{0,32},{1,33},{2,34},{3,35},{4,36},{5,37},{6,38},{7,39},{8,12},{9,... | collective-permute-start | bytes 98312 | tf_op jit(solution)/shard_map/ppermute | solution.py:36
  69.3 2.8 %collective-permute-start.14 = (bf16[16,1024]{1,0:T(8,128)(2,1)S(1)}, bf16[16,1024]{1,0:T(8,128)(2,1)S(1)}, u32[]{:S(2)}, u32[]{:S(2)}) collective-permute-start(bf16[16,1024]{1,0:T(8,128)(2,1)S(1)} %add_add_fusion.1), channel_id=1, source_target_pairs={{0,48},{1,49},{2,50},{3,51},{4,52},{5,53},{6,54},{7,55},{8,14},{9,... | collective-permute-start | bytes 98312 | tf_op jit(solution)/shard_map/ppermute | solution.py:36
  72.7 1.0 copy-start.4
  72.7 1.5 %copy-start.5 = (bf16[256,2304]{1,0:T(8,128)(2,1)}, bf16[256,2304]{1,0:T(8,128)(2,1)S(1)}, u32[]{:S(2)}) copy-start(bf16[256,2304]{1,0:T(8,128)(2,1)S(1)} %collective-permute-done.16.refs_2_) | copy-start | bytes 3538948
  86.5 4.8 %collective-permute-start.18 = (f32[17,4,16,128]{3,2,1,0:T(8,128)}, f32[17,4,16,128]{3,2,1,0:T(8,128)S(1)}, u32[]{:S(2)}, u32[]{:S(2)}) collective-permute-start(f32[17,4,16,128]{3,2,1,0:T(8,128)} %get-tuple-element.11), channel_id=1, source_target_pairs={{0,8},{1,9},{2,10},{3,11},{4,12},{5,13},{6,14},{7,15},{8,0},{9,1},... | collective-permute-start | bytes 1671176 | tf_op jit(solution)/shard_map/ppermute | solution.py:36
  89.5 2.6 %collective-permute-start.19 = (f32[17,4,16,128]{3,2,1,0:T(8,128)}, f32[17,4,16,128]{3,2,1,0:T(8,128)S(1)}, u32[]{:S(2)}, u32[]{:S(2)}) collective-permute-start(f32[17,4,16,128]{3,2,1,0:T(8,128)} %get-tuple-element.12), channel_id=1, source_target_pairs={{0,8},{1,9},{2,10},{3,11},{4,12},{5,13},{6,14},{7,15},{8,0},{9,1},... | collective-permute-start | bytes 1671176 | tf_op jit(solution)/shard_map/ppermute | solution.py:36
  89.6 3.3 %collective-permute-start.21 = (f32[17,4,16,128]{3,2,1,0:T(8,128)}, f32[17,4,16,128]{3,2,1,0:T(8,128)S(1)}, u32[]{:S(2)}, u32[]{:S(2)}) collective-permute-start(f32[17,4,16,128]{3,2,1,0:T(8,128)} %get-tuple-element.13), channel_id=1, source_target_pairs={{0,8},{1,9},{2,10},{3,11},{4,12},{5,13},{6,14},{7,15},{8,0},{9,1},... | collective-permute-start | bytes 1671176 | tf_op jit(solution)/shard_map/ppermute | solution.py:36
  90.0 3.7 %collective-permute-start.23 = (f32[17,4,16,128]{3,2,1,0:T(8,128)}, f32[17,4,16,128]{3,2,1,0:T(8,128)S(1)}, u32[]{:S(2)}, u32[]{:S(2)}) collective-permute-start(f32[17,4,16,128]{3,2,1,0:T(8,128)} %get-tuple-element.14), channel_id=1, source_target_pairs={{0,8},{1,9},{2,10},{3,11},{4,12},{5,13},{6,14},{7,15},{8,0},{9,1},... | collective-permute-start | bytes 1671176 | tf_op jit(solution)/shard_map/ppermute | solution.py:36
  96.0 6.7 %collective-permute-start.20 = (f16[17,4,16,128]{3,2,1,0:T(8,128)(2,1)S(1)}, f16[17,4,16,128]{3,2,1,0:T(8,128)(2,1)S(1)}, u32[]{:S(2)}, u32[]{:S(2)}) collective-permute-start(f16[17,4,16,128]{3,2,1,0:T(8,128)(2,1)S(1)} %pad_maximum_fusion.4), channel_id=1, source_target_pairs={{0,64},{1,65},{2,66},{3,67},{4,68},{5,69},{6,70},{7,71},{8,10},{9,... | collective-permute-start | bytes 835592 | tf_op jit(solution)/shard_map/ppermute | solution.py:36
  97.9 8.8 %collective-permute-start.22 = (f16[17,4,16,128]{3,2,1,0:T(8,128)(2,1)S(1)}, f16[17,4,16,128]{3,2,1,0:T(8,128)(2,1)S(1)}, u32[]{:S(2)}, u32[]{:S(2)}) collective-permute-start(f16[17,4,16,128]{3,2,1,0:T(8,128)(2,1)S(1)} %pad_maximum_fusion.5), channel_id=1, source_target_pairs={{0,128},{1,129},{2,130},{3,131},{4,132},{5,133},{6,134},{7,135},{8... | collective-permute-start | bytes 835592 | tf_op jit(solution)/shard_map/ppermute | solution.py:36
  100.1 6.7 %collective-permute-start.24 = (f16[17,4,16,128]{3,2,1,0:T(8,128)(2,1)S(1)}, f16[17,4,16,128]{3,2,1,0:T(8,128)(2,1)S(1)}, u32[]{:S(2)}, u32[]{:S(2)}) collective-permute-start(f16[17,4,16,128]{3,2,1,0:T(8,128)(2,1)S(1)} %pad_maximum_fusion.6), channel_id=1, source_target_pairs={{0,192},{1,193},{2,194},{3,195},{4,196},{5,197},{6,198},{7,199},{8... | collective-permute-start | bytes 835592 | tf_op jit(solution)/shard_map/ppermute | solution.py:36
  107.9 11.9 %collective-permute-start.28 = (f16[17,4,16,128]{3,2,1,0:T(8,128)(2,1)S(1)}, f16[17,4,16,128]{3,2,1,0:T(8,128)(2,1)S(1)}, u32[]{:S(2)}, u32[]{:S(2)}) collective-permute-start(f16[17,4,16,128]{3,2,1,0:T(8,128)(2,1)S(1)} %get-tuple-element.19), channel_id=1, source_target_pairs={{0,6},{1,7},{2,0},{3,1},{4,2},{5,3},{6,4},{7,5},{8,24},{9,56},{10,... | collective-permute-start | bytes 835592 | tf_op jit(solution)/shard_map/ppermute | solution.py:36
  109.8 13.0 %collective-permute-start.27 = (f16[17,4,16,128]{3,2,1,0:T(8,128)(2,1)S(1)}, f16[17,4,16,128]{3,2,1,0:T(8,128)(2,1)S(1)}, u32[]{:S(2)}, u32[]{:S(2)}) collective-permute-start(f16[17,4,16,128]{3,2,1,0:T(8,128)(2,1)S(1)} %get-tuple-element.20), channel_id=1, source_target_pairs={{0,4},{1,5},{2,6},{3,7},{4,0},{5,1},{6,2},{7,3},{8,24},{9,56},{10,... | collective-permute-start | bytes 835592 | tf_op jit(solution)/shard_map/ppermute | solution.py:36
  111.8 14.0 %collective-permute-start.26 = (f16[17,4,16,128]{3,2,1,0:T(8,128)(2,1)S(1)}, f16[17,4,16,128]{3,2,1,0:T(8,128)(2,1)S(1)}, u32[]{:S(2)}, u32[]{:S(2)}) collective-permute-start(f16[17,4,16,128]{3,2,1,0:T(8,128)(2,1)S(1)} %get-tuple-element.21), channel_id=1, source_target_pairs={{0,2},{1,3},{2,4},{3,5},{4,6},{5,7},{6,0},{7,1},{8,8},{9,40},{10,1... | collective-permute-start | bytes 835592 | tf_op jit(solution)/shard_map/ppermute | solution.py:36
  113.7 15.0 %collective-permute-start.25 = (f16[17,4,16,128]{3,2,1,0:T(8,128)(2,1)S(1)}, f16[17,4,16,128]{3,2,1,0:T(8,128)(2,1)S(1)}, u32[]{:S(2)}, u32[]{:S(2)}) collective-permute-start(f16[17,4,16,128]{3,2,1,0:T(8,128)(2,1)S(1)} %get-tuple-element.22), channel_id=1, source_target_pairs={{0,0},{1,1},{2,2},{3,3},{4,4},{5,5},{6,6},{7,7},{8,8},{9,40},{10,1... | collective-permute-start | bytes 835592 | tf_op jit(solution)/shard_map/ppermute | solution.py:36
  129.0 8.9 %collective-permute-start.29 = (f32[4,8,4,16,128]{4,3,2,1,0:T(8,128)S(1)}, f32[4,8,4,16,128]{4,3,2,1,0:T(8,128)S(1)}, u32[]{:S(2)}, u32[]{:S(2)}) collective-permute-start(f32[4,8,4,16,128]{4,3,2,1,0:T(8,128)S(1)} %split.1), channel_id=1, source_target_pairs={{0,8},{1,9},{2,10},{3,11},{4,12},{5,13},{6,14},{7,15},{8,0},{9,1},... | collective-permute-start | bytes 3145736 | tf_op jit(solution)/shard_map/ppermute | solution.py:36
Sparse Core Ops, SparseCore 0:
  18.8 42.6 all-gather.1

commit v5 on v4

--- a/solution.py
+++ b/solution.py
@@ -356,19 +356,18 @@
     ]
     me = me[None]
     t = own_blocks(me, offsets, amplitudes, mixed)
+    def near(n):
+        return lambda x, y, z, c: (x + n * (1 - c), y + n * c, z, c)
+
+    def far(n):
+        return lambda x, y, z, c: (x + n * c, y + n * (1 - c), z, c)
+
     t = (
         t
         + send(t, core)
-        + send(t, lambda x, y, z, c: (x, y, z ^ 1, c))
-        + send(t, lambda x, y, z, c: (x, y, z ^ 1, c + 1))
+        + send(t, far(2))
+        + send(t, lambda x, y, z, c: (x + 2 * (1 - c), y + 2 * c, z, 1 - c))
     )
-
-    def near(n):
-        return lambda x, y, z, c: (x + n * (1 - c), y + n * c, z, c)
-
-    def far(n):
-        return lambda x, y, z, c: (x + n * c, y + n * (1 - c), z, c)
-
     t = jnp.pad(t, ((0, 0), (0, DEPTH - 1024)))
     first = [jnp.concatenate(cols + [t])]
     first += [send(first[0], near(n)) for n in range(1, 4)]
@@ -377,8 +376,9 @@
     second = [cols] + [send(cols, far(n)) for n in range(1, 4)]
     t = sum(m[64:, :1024] for m in first[1:]) + first[0][64:, :1024]
     t = t + cols[:16, :1024] * 0
-    t = t + sum(send(t, lambda x, y, z, c, n=n: (x, y, z ^ n, c)) for n in (2, 4, 6))
-    t = t + sum(send(t, far(n)) for n in range(1, 4))
+    for n in (1, 2, 4):
+        t = t + send(t, lambda x, y, z, c, n=n: (x, y, z ^ n, c))
+    t = t + send(t, far(1))
     offdiag = (pairs[:, 0] != pairs[:, 1]).astype(jnp.float32)
     offdiag = jnp.broadcast_to(offdiag[:, None], (P_SIZE, 128))
     swap = jnp.asarray(transposed_forward(), jnp.bfloat16)

time: 148 us -> 145 us (0.980)
  waiting for transfers between devices: 55.6 us -> 52.3 us
    ppermute x30 -> x28, waiting for transfers between devices: 55.6 us -> 52.3 us  [send(): return lax.ppermute(block, AXES, pairs)]
    ppermute x30 -> x28, starting transfers between devices: 54.2 us -> 55.1 us  [send(): return lax.ppermute(block, AXES, pairs)]
  transfers between devices with their start and end apart: 31 -> 29, of which waited for: 21 -> 20; matrix products, arithmetic and copies ran while one was open for 1% -> 1% of each run, Pallas kernels for 0% -> 0%
where the time goes in v5:
time: 145 us
  starting transfers between devices  55.1 us (38%)
  waiting for transfers between devices  52.3 us (36%)
  Pallas kernels  15.6 us (11%)
  between operations  13.9 us (10%)
  other arithmetic  4.88 us (3%)
  local copies, waits for them, and re-layouts  3.11 us (2%)
    ppermute x28, starting transfers between devices, send(): return lax.ppermute(block, AXES, pairs)  55.1 us
    ppermute x28, waiting for transfers between devices, send(): return lax.ppermute(block, AXES, pairs)  52.3 us
    pallas_call x1, Pallas kernels, ladder(): pl.pallas_call(ladder_kernel, out_shape=[jax.ShapeDtypeStruct((4, 17, 4,...  12.3 us
  transfers between devices with their start and end apart: 29, of which 20 were waited for; matrix products, arithmetic and copies ran while one was open for 1% of the time, Pallas kernels for 0%

profile of v5, /device:TPU:33, one launch (start us, length us, event | category | flops | bytes accessed | tf_op | source)
XLA Modules:
  0.0 144.8 jit_solution(12685417004454836082)
XLA Ops:
  6.5 1.2 dynamic-slice_bitcast_fusion.3
  7.8 0.8 collective-permute-start.2
  8.5 1.0 collective-permute-done.2
  9.6 0.6 blocks.1
  10.2 0.5 collective-permute-start.3
  10.7 2.7 %collective-permute-start.4 = (bf16[16,1024]{1,0:T(8,128)(2,1)S(1)}, bf16[16,1024]{1,0:T(8,128)(2,1)S(1)}, u32[]{:S(2)}, u32[]{:S(2)}) collective-permute-start(bf16[16,1024]{1,0:T(8,128)(2,1)S(1)} %blocks.1), channel_id=1, source_target_pairs={{0,32},{1,33},{2,34},{3,35},{4,36},{5,37},{6,38},{7,39},{8,12},{9,... | collective-permute-start | bytes 98312 | tf_op jit(solution)/shard_map/ppermute | solution.py:36
  13.4 0.5 collective-permute-start.5
  13.9 4.4 %collective-permute-start = (bf16[32,2304]{1,0:T(8,128)(2,1)S(1)}, bf16[32,2304]{1,0:T(8,128)(2,1)S(1)}, u32[]{:S(2)}, u32[]{:S(2)}) collective-permute-start(bf16[32,2304]{1,0:T(8,128)(2,1)S(1)} %get-tuple-element.23), channel_id=1, source_target_pairs={{0,0},{1,32},{2,2},{3,34},{4,4},{5,36},{6,6},{7,38},{8,8},{9,40},{... | collective-permute-start | bytes 442376 | tf_op jit(solution)/shard_map/ppermute | solution.py:36
  18.3 1.7 %collective-permute-start.1 = (bf16[32,2304]{1,0:T(8,128)(2,1)S(1)}, bf16[32,2304]{1,0:T(8,128)(2,1)S(1)}, u32[]{:S(2)}, u32[]{:S(2)}) collective-permute-start(bf16[32,2304]{1,0:T(8,128)(2,1)S(1)} %get-tuple-element.24), channel_id=1, source_target_pairs={{0,8},{1,40},{2,10},{3,42},{4,12},{5,44},{6,14},{7,46},{8,0},{9,32... | collective-permute-start | bytes 442376 | tf_op jit(solution)/shard_map/ppermute | solution.py:36
  20.1 3.5 %collective-permute-done = bf16[32,2304]{1,0:T(8,128)(2,1)S(1)} collective-permute-done((bf16[32,2304]{1,0:T(8,128)(2,1)S(1)}, bf16[32,2304]{1,0:T(8,128)(2,1)S(1)}, u32[]{:S(2)}, u32[]{:S(2)}) %collective-permute-start) | collective-permute-done | bytes 147488 | tf_op jit(solution)/shard_map/ppermute | solution.py:36
  23.6 3.4 %collective-permute-done.1 = bf16[32,2304]{1,0:T(8,128)(2,1)S(1)} collective-permute-done((bf16[32,2304]{1,0:T(8,128)(2,1)S(1)}, bf16[32,2304]{1,0:T(8,128)(2,1)S(1)}, u32[]{:S(2)}, u32[]{:S(2)}) %collective-permute-start.1) | collective-permute-done | bytes 147488 | tf_op jit(solution)/shard_map/ppermute | solution.py:36
  27.1 1.3 collective-permute-start.6
  28.5 0.1 collective-permute-start.7
  28.6 2.4 %collective-permute-start.8 = (bf16[80,2304]{1,0:T(8,128)(2,1)S(1)}, bf16[80,2304]{1,0:T(8,128)(2,1)S(1)}, u32[]{:S(2)}, u32[]{:S(2)}) collective-permute-start(bf16[80,2304]{1,0:T(8,128)(2,1)S(1)} %fusion.5), channel_id=1, source_target_pairs={{0,6},{1,7},{2,0},{3,1},{4,2},{5,3},{6,4},{7,5},{8,56},{9,57},{10,... | collective-permute-start | bytes 1105928 | tf_op jit(solution)/shard_map/ppermute | solution.py:36
  31.0 8.0 %collective-permute-done.6 = bf16[80,2304]{1,0:T(8,128)(2,1)S(1)} collective-permute-done((bf16[80,2304]{1,0:T(8,128)(2,1)S(1)}, bf16[80,2304]{1,0:T(8,128)(2,1)S(1)}, u32[]{:S(2)}, u32[]{:S(2)}) %collective-permute-start.6) | collective-permute-done | bytes 368672 | tf_op jit(solution)/shard_map/ppermute | solution.py:36
  39.2 0.6 collective-permute-done.8
  39.9 0.1 pad_maximum_fusion
  40.0 1.3 collective-permute-start.13
  41.3 2.5 %collective-permute-start.14 = (bf16[256,2304]{1,0:T(8,128)(2,1)S(1)}, bf16[256,2304]{1,0:T(8,128)(2,1)S(1)}, u32[]{:S(2)}, u32[]{:S(2)}) collective-permute-start(bf16[256,2304]{1,0:T(8,128)(2,1)S(1)} %bitcast.62), channel_id=1, source_target_pairs={{0,32},{1,33},{2,34},{3,35},{4,36},{5,37},{6,38},{7,39},{8,12},{9,... | collective-permute-start | bytes 3538952 | tf_op jit(solution)/shard_map/ppermute | solution.py:36
  43.8 1.2 collective-permute-start.15
  45.0 0.1 collective-permute-start.9
  45.1 3.3 %collective-permute-done.9 = bf16[16,1024]{1,0:T(8,128)(2,1)S(1)} collective-permute-done((bf16[16,1024]{1,0:T(8,128)(2,1)S(1)}, bf16[16,1024]{1,0:T(8,128)(2,1)S(1)}, u32[]{:S(2)}, u32[]{:S(2)}) %collective-permute-start.9) | collective-permute-done | bytes 32800 | tf_op jit(solution)/shard_map/ppermute | solution.py:36
  48.4 3.5 %collective-permute-start.10 = (bf16[16,1024]{1,0:T(8,128)(2,1)S(1)}, bf16[16,1024]{1,0:T(8,128)(2,1)S(1)}, u32[]{:S(2)}, u32[]{:S(2)}) collective-permute-start(bf16[16,1024]{1,0:T(8,128)(2,1)S(1)} %add.88), channel_id=1, source_target_pairs={{0,64},{1,65},{2,66},{3,67},{4,68},{5,69},{6,70},{7,71},{8,72},{9,... | collective-permute-start | bytes 98312 | tf_op jit(solution)/shard_map/ppermute | solution.py:36
  51.9 2.2 %collective-permute-done.10 = bf16[16,1024]{1,0:T(8,128)(2,1)S(1)} collective-permute-done((bf16[16,1024]{1,0:T(8,128)(2,1)S(1)}, bf16[16,1024]{1,0:T(8,128)(2,1)S(1)}, u32[]{:S(2)}, u32[]{:S(2)}) %collective-permute-start.10) | collective-permute-done | bytes 32800 | tf_op jit(solution)/shard_map/ppermute | solution.py:36
  54.1 5.5 %collective-permute-start.11 = (bf16[16,1024]{1,0:T(8,128)(2,1)S(1)}, bf16[16,1024]{1,0:T(8,128)(2,1)S(1)}, u32[]{:S(2)}, u32[]{:S(2)}) collective-permute-start(bf16[16,1024]{1,0:T(8,128)(2,1)S(1)} %add.89), channel_id=1, source_target_pairs={{0,128},{1,129},{2,130},{3,131},{4,132},{5,133},{6,134},{7,135},{8... | collective-permute-start | bytes 98312 | tf_op jit(solution)/shard_map/ppermute | solution.py:36
  59.6 1.8 %collective-permute-done.11 = bf16[16,1024]{1,0:T(8,128)(2,1)S(1)} collective-permute-done((bf16[16,1024]{1,0:T(8,128)(2,1)S(1)}, bf16[16,1024]{1,0:T(8,128)(2,1)S(1)}, u32[]{:S(2)}, u32[]{:S(2)}) %collective-permute-start.11) | collective-permute-done | bytes 32800 | tf_op jit(solution)/shard_map/ppermute | solution.py:36
  61.4 1.3 collective-permute-start.12
  62.7 8.0 %collective-permute-done.12 = bf16[16,1024]{1,0:T(8,128)(2,1)S(1)} collective-permute-done((bf16[16,1024]{1,0:T(8,128)(2,1)S(1)}, bf16[16,1024]{1,0:T(8,128)(2,1)S(1)}, u32[]{:S(2)}, u32[]{:S(2)}) %collective-permute-start.12) | collective-permute-done | bytes 32800 | tf_op jit(solution)/shard_map/ppermute | solution.py:36
  70.7 0.6 add.91.blocks
  71.3 0.8 broadcast_in_dim.17.offdiag
  72.2 0.1 copy-done.4
  72.3 0.4 copy-done.5
  72.8 12.3 %ladder.1 = (f32[4,17,4,16,128]{4,3,2,1,0:T(8,128)}, f32[17,4,16,128]{3,2,1,0:T(8,128)}, f32[17,4,16,128]{3,2,1,0:T(8,128)}, f32[17,4,16,128]{3,2,1,0:T(8,128)}, f32[17,4,16,128]{3,2,1,0:T(8,128)}) custom-call(s32[1]{0:T(128)} %bitcast.me, f32[64,128]{1,0:T(8,128)} %broadcast_in_dim.17.offdiag, bf16[128,128]{1,0:T(8,128)(2,1)} %constant.65.clone.swap, ...), custom_call_target="tpu_custom_call" | custom-call | tf_op jit(solution)/shard_map/ladder/pallas_call | solution.py:197
  85.1 1.5 %collective-permute-start.16 = (f32[17,4,16,128]{3,2,1,0:T(8,128)}, f32[17,4,16,128]{3,2,1,0:T(8,128)S(1)}, u32[]{:S(2)}, u32[]{:S(2)}) collective-permute-start(f32[17,4,16,128]{3,2,1,0:T(8,128)} %get-tuple-element.11), channel_id=1, source_target_pairs={{0,8},{1,9},{2,10},{3,11},{4,12},{5,13},{6,14},{7,15},{8,0},{9,1},... | collective-permute-start | bytes 1671176 | tf_op jit(solution)/shard_map/ppermute | solution.py:36
  86.5 0.1 collective-permute-start.17
  86.6 0.4 collective-permute-start.19
  87.0 0.1 collective-permute-start.21
  87.1 1.2 collective-permute-done.16
  88.3 0.8 collective-permute-done.17
  89.1 0.8 collective-permute-done.19
  89.9 0.8 collective-permute-done.21
  90.7 2.0 %bitcast_add_fusion.1 = (f32[17,4,16,128]{3,2,1,0:T(8,128)S(1)}, f32[17,4,16,128]{3,2,1,0:T(8,128)S(1)}, f32[17,4,16,128]{3,2,1,0:T(8,128)S(1)}, f32[17,4,16,128]{3,2,1,0:T(8,128)S(1)}) fusion(f32[17,4,16,128]{3,2,1,0:T(8,128)S(1)} %collective-permute-done.19, f32[4,17,4,16,128]{4,3,2,1,0:T(8,128)} %get-tuple-element.10, ...), kind=kLoop, calls=%fused_computation.5 | loop fusion | flops 557056 | bytes 6684672 | tf_op jit(solution)/shard_map/add | solution.py:387
  92.9 0.1 pad_maximum_fusion.4
  93.0 1.8 %collective-permute-start.18 = (f16[17,4,16,128]{3,2,1,0:T(8,128)(2,1)S(1)}, f16[17,4,16,128]{3,2,1,0:T(8,128)(2,1)S(1)}, u32[]{:S(2)}, u32[]{:S(2)}) collective-permute-start(f16[17,4,16,128]{3,2,1,0:T(8,128)(2,1)S(1)} %pad_maximum_fusion.4), channel_id=1, source_target_pairs={{0,64},{1,65},{2,66},{3,67},{4,68},{5,69},{6,70},{7,71},{8,10},{9,... | collective-permute-start | bytes 835592 | tf_op jit(solution)/shard_map/ppermute | solution.py:36
  94.9 0.1 pad_maximum_fusion.5
  95.0 1.9 %collective-permute-start.20 = (f16[17,4,16,128]{3,2,1,0:T(8,128)(2,1)S(1)}, f16[17,4,16,128]{3,2,1,0:T(8,128)(2,1)S(1)}, u32[]{:S(2)}, u32[]{:S(2)}) collective-permute-start(f16[17,4,16,128]{3,2,1,0:T(8,128)(2,1)S(1)} %pad_maximum_fusion.5), channel_id=1, source_target_pairs={{0,128},{1,129},{2,130},{3,131},{4,132},{5,133},{6,134},{7,135},{8... | collective-permute-start | bytes 835592 | tf_op jit(solution)/shard_map/ppermute | solution.py:36
  97.0 0.1 pad_maximum_fusion.6
  97.1 1.3 collective-permute-start.22
  98.6 1.1 collective-permute-done.18
  99.7 4.1 %collective-permute-done.20 = f16[17,4,16,128]{3,2,1,0:T(8,128)(2,1)S(1)} collective-permute-done((f16[17,4,16,128]{3,2,1,0:T(8,128)(2,1)S(1)}, f16[17,4,16,128]{3,2,1,0:T(8,128)(2,1)S(1)}, u32[]{:S(2)}, u32[]{:S(2)}) %collective-permute-start.20) | collective-permute-done | bytes 278560 | tf_op jit(solution)/shard_map/ppermute | solution.py:36
  103.8 0.4 pad_maximum_fusion.1
  104.5 0.5 maximum_select_fusion.2
  105.0 1.3 collective-permute-start.26
  106.3 2.6 %collective-permute-start.25 = (f16[17,4,16,128]{3,2,1,0:T(8,128)(2,1)S(1)}, f16[17,4,16,128]{3,2,1,0:T(8,128)(2,1)S(1)}, u32[]{:S(2)}, u32[]{:S(2)}) collective-permute-start(f16[17,4,16,128]{3,2,1,0:T(8,128)(2,1)S(1)} %get-tuple-element.20), channel_id=1, source_target_pairs={{0,4},{1,5},{2,6},{3,7},{4,0},{5,1},{6,2},{7,3},{8,24},{9,56},{10,... | collective-permute-start | bytes 835592 | tf_op jit(solution)/shard_map/ppermute | solution.py:36
  108.8 2.2 %collective-permute-start.24 = (f16[17,4,16,128]{3,2,1,0:T(8,128)(2,1)S(1)}, f16[17,4,16,128]{3,2,1,0:T(8,128)(2,1)S(1)}, u32[]{:S(2)}, u32[]{:S(2)}) collective-permute-start(f16[17,4,16,128]{3,2,1,0:T(8,128)(2,1)S(1)} %get-tuple-element.21), channel_id=1, source_target_pairs={{0,2},{1,3},{2,4},{3,5},{4,6},{5,7},{6,0},{7,1},{8,8},{9,40},{10,1... | collective-permute-start | bytes 835592 | tf_op jit(solution)/shard_map/ppermute | solution.py:36
  111.1 5.4 %collective-permute-start.23 = (f16[17,4,16,128]{3,2,1,0:T(8,128)(2,1)S(1)}, f16[17,4,16,128]{3,2,1,0:T(8,128)(2,1)S(1)}, u32[]{:S(2)}, u32[]{:S(2)}) collective-permute-start(f16[17,4,16,128]{3,2,1,0:T(8,128)(2,1)S(1)} %get-tuple-element.22), channel_id=1, source_target_pairs={{0,0},{1,1},{2,2},{3,3},{4,4},{5,5},{6,6},{7,7},{8,8},{9,40},{10,1... | collective-permute-start | bytes 835592 | tf_op jit(solution)/shard_map/ppermute | solution.py:36
  116.5 0.7 collective-permute-done.26
  117.3 2.9 %collective-permute-done.25 = f16[17,4,16,128]{3,2,1,0:T(8,128)(2,1)S(1)} collective-permute-done((f16[17,4,16,128]{3,2,1,0:T(8,128)(2,1)S(1)}, f16[17,4,16,128]{3,2,1,0:T(8,128)(2,1)S(1)}, u32[]{:S(2)}, u32[]{:S(2)}) %collective-permute-start.25) | collective-permute-done | bytes 278560 | tf_op jit(solution)/shard_map/ppermute | solution.py:36
  120.4 2.8 %collective-permute-done.24 = f16[17,4,16,128]{3,2,1,0:T(8,128)(2,1)S(1)} collective-permute-done((f16[17,4,16,128]{3,2,1,0:T(8,128)(2,1)S(1)}, f16[17,4,16,128]{3,2,1,0:T(8,128)(2,1)S(1)}, u32[]{:S(2)}, u32[]{:S(2)}) %collective-permute-start.24) | collective-permute-done | bytes 278560 | tf_op jit(solution)/shard_map/ppermute | solution.py:36
  123.3 2.9 %collective-permute-done.23 = f16[17,4,16,128]{3,2,1,0:T(8,128)(2,1)S(1)} collective-permute-done((f16[17,4,16,128]{3,2,1,0:T(8,128)(2,1)S(1)}, f16[17,4,16,128]{3,2,1,0:T(8,128)(2,1)S(1)}, u32[]{:S(2)}, u32[]{:S(2)}) %collective-permute-start.23) | collective-permute-done | bytes 278560 | tf_op jit(solution)/shard_map/ppermute | solution.py:36
  126.3 0.1 split.1
  126.3 6.8 %collective-permute-start.27 = (f32[4,8,4,16,128]{4,3,2,1,0:T(8,128)S(1)}, f32[4,8,4,16,128]{4,3,2,1,0:T(8,128)S(1)}, u32[]{:S(2)}, u32[]{:S(2)}) collective-permute-start(f32[4,8,4,16,128]{4,3,2,1,0:T(8,128)S(1)} %split.1), channel_id=1, source_target_pairs={{0,8},{1,9},{2,10},{3,11},{4,12},{5,13},{6,14},{7,15},{8,0},{9,1},... | collective-permute-start | bytes 3145736 | tf_op jit(solution)/shard_map/ppermute | solution.py:36
  133.1 2.3 %collective-permute-done.27.refs_4_ = f32[4,8,4,16,128]{4,3,2,1,0:T(8,128)S(1)} collective-permute-done((f32[4,8,4,16,128]{4,3,2,1,0:T(8,128)S(1)}, f32[4,8,4,16,128]{4,3,2,1,0:T(8,128)S(1)}, u32[]{:S(2)}, u32[]{:S(2)}) %collective-permute-start.27) | collective-permute-done | bytes 1048608 | tf_op jit(solution)/shard_map/ppermute | solution.py:36
  135.4 2.6 %finish.1 = f32[64,32,128]{2,1,0:T(8,128)} custom-call(s32[1]{0:T(128)} %bitcast.me, f32[16,4,16,128]{3,2,1,0:T(8,128)S(1)} %slice_multiply_fusion.3.refs_0_, f32[16,4,16,128]{3,2,1,0:T(8,128)S(1)} %slice_multiply_fusion.2.refs_1_, f32[16,4,16,128]{3,2,1,0:T(8,128)S(1)} %slice_multiply_fusion.1.refs_2_, f32[16,4,16,128]{3,2,1,0:T(8,128)S(1)} %slice_multiply_fusion.refs_3_, ...), custom_call_target="tpu_custom_call" | custom-call | tf_op jit(solution)/shard_map/finish/pallas_call | solution.py:314
  (64 shorter events, 1.5 us)
Async XLA Ops:
  6.5 3.0 %copy-start.2 = (s32[2,2]{1,0:T(2,128)S(1)}, s32[2,2]{1,0:T(2,128)}, u32[]{:S(2)}) copy-start(s32[2,2]{1,0:T(2,128)} %offsets.1) | copy-start | bytes 52
  6.5 3.0 %copy-start.1 = (bf16[64,32,128]{2,1,0:T(8,128)(2,1)S(1)}, bf16[64,32,128]{2,1,0:T(8,128)(2,1)}, u32[]{:S(2)}) copy-start(bf16[64,32,128]{2,1,0:T(8,128)(2,1)} %amplitudes.1) | copy-start | bytes 1572868
  6.5 64.8 %all-gather.2.cloned.1.call-start = ((), (), s32[]{:S(2)}) async-start(), calls=%async_computation | async-start | bytes 2654208 | tf_op jit(solution)/shard_map/all_gather | solution.py:352
  7.8 1.8 %collective-permute-start.2 = (bf16[32,2304]{1,0:T(8,128)(2,1)S(1)}, bf16[32,2304]{1,0:T(8,128)(2,1)S(1)}, u32[]{:S(2)}, u32[]{:S(2)}) collective-permute-start(bf16[32,2304]{1,0:T(8,128)(2,1)S(1)} %get-tuple-element.25), channel_id=1, source_target_pairs={{0,8},{1,9},{2,10},{3,11},{4,12},{5,13},{6,14},{7,15},{8,0},{9,1},... | collective-permute-start | bytes 442376 | tf_op jit(solution)/shard_map/ppermute | solution.py:36
  9.6 10.5 %copy-start = (bf16[64,2304]{1,0:T(8,128)(2,1)}, bf16[64,2304]{1,0:T(8,128)(2,1)S(1)}, u32[]{:S(2)}) copy-start(bf16[64,2304]{1,0:T(8,128)(2,1)S(1)} %pad_maximum_fusion.2._) | copy-start | bytes 884740
  10.2 9.9 %collective-permute-start.3 = (bf16[16,1024]{1,0:T(8,128)(2,1)S(1)}, bf16[16,1024]{1,0:T(8,128)(2,1)S(1)}, u32[]{:S(2)}, u32[]{:S(2)}) collective-permute-start(bf16[16,1024]{1,0:T(8,128)(2,1)S(1)} %blocks.1), channel_id=1, source_target_pairs={{0,8},{1,9},{2,10},{3,11},{4,12},{5,13},{6,14},{7,15},{8,0},{9,1},... | collective-permute-start | bytes 98312 | tf_op jit(solution)/shard_map/ppermute | solution.py:36
  10.7 9.4 %collective-permute-start.4 = (bf16[16,1024]{1,0:T(8,128)(2,1)S(1)}, bf16[16,1024]{1,0:T(8,128)(2,1)S(1)}, u32[]{:S(2)}, u32[]{:S(2)}) collective-permute-start(bf16[16,1024]{1,0:T(8,128)(2,1)S(1)} %blocks.1), channel_id=1, source_target_pairs={{0,32},{1,33},{2,34},{3,35},{4,36},{5,37},{6,38},{7,39},{8,12},{9,... | collective-permute-start | bytes 98312 | tf_op jit(solution)/shard_map/ppermute | solution.py:36
  13.4 6.7 %collective-permute-start.5 = (bf16[16,1024]{1,0:T(8,128)(2,1)S(1)}, bf16[16,1024]{1,0:T(8,128)(2,1)S(1)}, u32[]{:S(2)}, u32[]{:S(2)}) collective-permute-start(bf16[16,1024]{1,0:T(8,128)(2,1)S(1)} %blocks.1), channel_id=1, source_target_pairs={{0,12},{1,13},{2,14},{3,15},{4,8},{5,9},{6,10},{7,11},{8,32},{9,33... | collective-permute-start | bytes 98312 | tf_op jit(solution)/shard_map/ppermute | solution.py:36
  13.9 9.7 %collective-permute-start = (bf16[32,2304]{1,0:T(8,128)(2,1)S(1)}, bf16[32,2304]{1,0:T(8,128)(2,1)S(1)}, u32[]{:S(2)}, u32[]{:S(2)}) collective-permute-start(bf16[32,2304]{1,0:T(8,128)(2,1)S(1)} %get-tuple-element.23), channel_id=1, source_target_pairs={{0,0},{1,32},{2,2},{3,34},{4,4},{5,36},{6,6},{7,38},{8,8},{9,40},{... | collective-permute-start | bytes 442376 | tf_op jit(solution)/shard_map/ppermute | solution.py:36
  18.3 8.8 %collective-permute-start.1 = (bf16[32,2304]{1,0:T(8,128)(2,1)S(1)}, bf16[32,2304]{1,0:T(8,128)(2,1)S(1)}, u32[]{:S(2)}, u32[]{:S(2)}) collective-permute-start(bf16[32,2304]{1,0:T(8,128)(2,1)S(1)} %get-tuple-element.24), channel_id=1, source_target_pairs={{0,8},{1,40},{2,10},{3,42},{4,12},{5,44},{6,14},{7,46},{8,0},{9,32... | collective-permute-start | bytes 442376 | tf_op jit(solution)/shard_map/ppermute | solution.py:36
  27.1 11.9 %collective-permute-start.6 = (bf16[80,2304]{1,0:T(8,128)(2,1)S(1)}, bf16[80,2304]{1,0:T(8,128)(2,1)S(1)}, u32[]{:S(2)}, u32[]{:S(2)}) collective-permute-start(bf16[80,2304]{1,0:T(8,128)(2,1)S(1)} %fusion.5), channel_id=1, source_target_pairs={{0,2},{1,3},{2,4},{3,5},{4,6},{5,7},{6,0},{7,1},{8,24},{9,25},{10,... | collective-permute-start | bytes 1105928 | tf_op jit(solution)/shard_map/ppermute | solution.py:36
  28.5 10.6 %collective-permute-start.7 = (bf16[80,2304]{1,0:T(8,128)(2,1)S(1)}, bf16[80,2304]{1,0:T(8,128)(2,1)S(1)}, u32[]{:S(2)}, u32[]{:S(2)}) collective-permute-start(bf16[80,2304]{1,0:T(8,128)(2,1)S(1)} %fusion.5), channel_id=1, source_target_pairs={{0,4},{1,5},{2,6},{3,7},{4,0},{5,1},{6,2},{7,3},{8,40},{9,41},{10,... | collective-permute-start | bytes 1105928 | tf_op jit(solution)/shard_map/ppermute | solution.py:36
  28.6 11.2 %collective-permute-start.8 = (bf16[80,2304]{1,0:T(8,128)(2,1)S(1)}, bf16[80,2304]{1,0:T(8,128)(2,1)S(1)}, u32[]{:S(2)}, u32[]{:S(2)}) collective-permute-start(bf16[80,2304]{1,0:T(8,128)(2,1)S(1)} %fusion.5), channel_id=1, source_target_pairs={{0,6},{1,7},{2,0},{3,1},{4,2},{5,3},{6,4},{7,5},{8,56},{9,57},{10,... | collective-permute-start | bytes 1105928 | tf_op jit(solution)/shard_map/ppermute | solution.py:36
  39.9 22.8 %copy-start.6 = (s32[64,2]{0,1:T(2,128)S(1)}, s32[64,2]{0,1:T(2,128)}, u32[]{:S(2)}) copy-start(s32[64,2]{0,1:T(2,128)} %param.5) | copy-start | bytes 1540
  40.0 32.2 %copy-start.3 = (bf16[4,8,8,2304]{3,1,0,2:T(8,128)(2,1)}, bf16[4,8,8,2304]{3,1,0,2:T(8,128)(2,1)S(1)}, u32[]{:S(2)}) copy-start(bf16[4,8,8,2304]{3,1,0,2:T(8,128)(2,1)S(1)} %pad_maximum_fusion) | copy-start | bytes 3538948
  40.0 31.2 %collective-permute-start.13 = (bf16[256,2304]{1,0:T(8,128)(2,1)S(1)}, bf16[256,2304]{1,0:T(8,128)(2,1)S(1)}, u32[]{:S(2)}, u32[]{:S(2)}) collective-permute-start(bf16[256,2304]{1,0:T(8,128)(2,1)S(1)} %bitcast.61), channel_id=1, source_target_pairs={{0,16},{1,17},{2,18},{3,19},{4,20},{5,21},{6,22},{7,23},{8,10},{9,... | collective-permute-start | bytes 3538952 | tf_op jit(solution)/shard_map/ppermute | solution.py:36
  41.3 30.0 %collective-permute-start.14 = (bf16[256,2304]{1,0:T(8,128)(2,1)S(1)}, bf16[256,2304]{1,0:T(8,128)(2,1)S(1)}, u32[]{:S(2)}, u32[]{:S(2)}) collective-permute-start(bf16[256,2304]{1,0:T(8,128)(2,1)S(1)} %bitcast.62), channel_id=1, source_target_pairs={{0,32},{1,33},{2,34},{3,35},{4,36},{5,37},{6,38},{7,39},{8,12},{9,... | collective-permute-start | bytes 3538952 | tf_op jit(solution)/shard_map/ppermute | solution.py:36
  43.8 27.5 %collective-permute-start.15 = (bf16[256,2304]{1,0:T(8,128)(2,1)S(1)}, bf16[256,2304]{1,0:T(8,128)(2,1)}, u32[]{:S(2)}, u32[]{:S(2)}) collective-permute-start(bf16[256,2304]{1,0:T(8,128)(2,1)S(1)} %bitcast.63), channel_id=1, source_target_pairs={{0,48},{1,49},{2,50},{3,51},{4,52},{5,53},{6,54},{7,55},{8,14},{9,... | collective-permute-start | bytes 3538952 | tf_op jit(solution)/shard_map/ppermute | solution.py:36
  45.0 3.4 %collective-permute-start.9 = (bf16[16,1024]{1,0:T(8,128)(2,1)S(1)}, bf16[16,1024]{1,0:T(8,128)(2,1)S(1)}, u32[]{:S(2)}, u32[]{:S(2)}) collective-permute-start(bf16[16,1024]{1,0:T(8,128)(2,1)S(1)} %fusion.33), channel_id=1, source_target_pairs={{0,1},{1,0},{2,3},{3,2},{4,5},{5,4},{6,7},{7,6},{8,9},{9,8},{10,11... | collective-permute-start | bytes 98312 | tf_op jit(solution)/shard_map/ppermute | solution.py:36
  48.4 5.7 %collective-permute-start.10 = (bf16[16,1024]{1,0:T(8,128)(2,1)S(1)}, bf16[16,1024]{1,0:T(8,128)(2,1)S(1)}, u32[]{:S(2)}, u32[]{:S(2)}) collective-permute-start(bf16[16,1024]{1,0:T(8,128)(2,1)S(1)} %add.88), channel_id=1, source_target_pairs={{0,64},{1,65},{2,66},{3,67},{4,68},{5,69},{6,70},{7,71},{8,72},{9,... | collective-permute-start | bytes 98312 | tf_op jit(solution)/shard_map/ppermute | solution.py:36
  54.1 7.2 %collective-permute-start.11 = (bf16[16,1024]{1,0:T(8,128)(2,1)S(1)}, bf16[16,1024]{1,0:T(8,128)(2,1)S(1)}, u32[]{:S(2)}, u32[]{:S(2)}) collective-permute-start(bf16[16,1024]{1,0:T(8,128)(2,1)S(1)} %add.89), channel_id=1, source_target_pairs={{0,128},{1,129},{2,130},{3,131},{4,132},{5,133},{6,134},{7,135},{8... | collective-permute-start | bytes 98312 | tf_op jit(solution)/shard_map/ppermute | solution.py:36
  61.4 9.3 %collective-permute-start.12 = (bf16[16,1024]{1,0:T(8,128)(2,1)S(1)}, bf16[16,1024]{1,0:T(8,128)(2,1)S(1)}, u32[]{:S(2)}, u32[]{:S(2)}) collective-permute-start(bf16[16,1024]{1,0:T(8,128)(2,1)S(1)} %add.90), channel_id=1, source_target_pairs={{0,16},{1,17},{2,18},{3,19},{4,20},{5,21},{6,22},{7,23},{8,10},{9,... | collective-permute-start | bytes 98312 | tf_op jit(solution)/shard_map/ppermute | solution.py:36
  71.3 1.0 copy-start.4
  71.3 1.5 %copy-start.5 = (bf16[256,2304]{1,0:T(8,128)(2,1)}, bf16[256,2304]{1,0:T(8,128)(2,1)S(1)}, u32[]{:S(2)}) copy-start(bf16[256,2304]{1,0:T(8,128)(2,1)S(1)} %collective-permute-done.14.refs_2_) | copy-start | bytes 3538948
  85.1 3.3 %collective-permute-start.16 = (f32[17,4,16,128]{3,2,1,0:T(8,128)}, f32[17,4,16,128]{3,2,1,0:T(8,128)S(1)}, u32[]{:S(2)}, u32[]{:S(2)}) collective-permute-start(f32[17,4,16,128]{3,2,1,0:T(8,128)} %get-tuple-element.11), channel_id=1, source_target_pairs={{0,8},{1,9},{2,10},{3,11},{4,12},{5,13},{6,14},{7,15},{8,0},{9,1},... | collective-permute-start | bytes 1671176 | tf_op jit(solution)/shard_map/ppermute | solution.py:36
  86.5 2.6 %collective-permute-start.17 = (f32[17,4,16,128]{3,2,1,0:T(8,128)}, f32[17,4,16,128]{3,2,1,0:T(8,128)S(1)}, u32[]{:S(2)}, u32[]{:S(2)}) collective-permute-start(f32[17,4,16,128]{3,2,1,0:T(8,128)} %get-tuple-element.12), channel_id=1, source_target_pairs={{0,8},{1,9},{2,10},{3,11},{4,12},{5,13},{6,14},{7,15},{8,0},{9,1},... | collective-permute-start | bytes 1671176 | tf_op jit(solution)/shard_map/ppermute | solution.py:36
  86.6 3.3 %collective-permute-start.19 = (f32[17,4,16,128]{3,2,1,0:T(8,128)}, f32[17,4,16,128]{3,2,1,0:T(8,128)S(1)}, u32[]{:S(2)}, u32[]{:S(2)}) collective-permute-start(f32[17,4,16,128]{3,2,1,0:T(8,128)} %get-tuple-element.13), channel_id=1, source_target_pairs={{0,8},{1,9},{2,10},{3,11},{4,12},{5,13},{6,14},{7,15},{8,0},{9,1},... | collective-permute-start | bytes 1671176 | tf_op jit(solution)/shard_map/ppermute | solution.py:36
  87.0 3.7 %collective-permute-start.21 = (f32[17,4,16,128]{3,2,1,0:T(8,128)}, f32[17,4,16,128]{3,2,1,0:T(8,128)S(1)}, u32[]{:S(2)}, u32[]{:S(2)}) collective-permute-start(f32[17,4,16,128]{3,2,1,0:T(8,128)} %get-tuple-element.14), channel_id=1, source_target_pairs={{0,8},{1,9},{2,10},{3,11},{4,12},{5,13},{6,14},{7,15},{8,0},{9,1},... | collective-permute-start | bytes 1671176 | tf_op jit(solution)/shard_map/ppermute | solution.py:36
  93.0 6.7 %collective-permute-start.18 = (f16[17,4,16,128]{3,2,1,0:T(8,128)(2,1)S(1)}, f16[17,4,16,128]{3,2,1,0:T(8,128)(2,1)S(1)}, u32[]{:S(2)}, u32[]{:S(2)}) collective-permute-start(f16[17,4,16,128]{3,2,1,0:T(8,128)(2,1)S(1)} %pad_maximum_fusion.4), channel_id=1, source_target_pairs={{0,64},{1,65},{2,66},{3,67},{4,68},{5,69},{6,70},{7,71},{8,10},{9,... | collective-permute-start | bytes 835592 | tf_op jit(solution)/shard_map/ppermute | solution.py:36
  95.0 8.8 %collective-permute-start.20 = (f16[17,4,16,128]{3,2,1,0:T(8,128)(2,1)S(1)}, f16[17,4,16,128]{3,2,1,0:T(8,128)(2,1)S(1)}, u32[]{:S(2)}, u32[]{:S(2)}) collective-permute-start(f16[17,4,16,128]{3,2,1,0:T(8,128)(2,1)S(1)} %pad_maximum_fusion.5), channel_id=1, source_target_pairs={{0,128},{1,129},{2,130},{3,131},{4,132},{5,133},{6,134},{7,135},{8... | collective-permute-start | bytes 835592 | tf_op jit(solution)/shard_map/ppermute | solution.py:36
  97.1 6.7 %collective-permute-start.22 = (f16[17,4,16,128]{3,2,1,0:T(8,128)(2,1)S(1)}, f16[17,4,16,128]{3,2,1,0:T(8,128)(2,1)S(1)}, u32[]{:S(2)}, u32[]{:S(2)}) collective-permute-start(f16[17,4,16,128]{3,2,1,0:T(8,128)(2,1)S(1)} %pad_maximum_fusion.6), channel_id=1, source_target_pairs={{0,192},{1,193},{2,194},{3,195},{4,196},{5,197},{6,198},{7,199},{8... | collective-permute-start | bytes 835592 | tf_op jit(solution)/shard_map/ppermute | solution.py:36
  105.0 12.3 %collective-permute-start.26 = (f16[17,4,16,128]{3,2,1,0:T(8,128)(2,1)S(1)}, f16[17,4,16,128]{3,2,1,0:T(8,128)(2,1)S(1)}, u32[]{:S(2)}, u32[]{:S(2)}) collective-permute-start(f16[17,4,16,128]{3,2,1,0:T(8,128)(2,1)S(1)} %get-tuple-element.19), channel_id=1, source_target_pairs={{0,6},{1,7},{2,0},{3,1},{4,2},{5,3},{6,4},{7,5},{8,24},{9,56},{10,... | collective-permute-start | bytes 835592 | tf_op jit(solution)/shard_map/ppermute | solution.py:36
  106.3 14.0 %collective-permute-start.25 = (f16[17,4,16,128]{3,2,1,0:T(8,128)(2,1)S(1)}, f16[17,4,16,128]{3,2,1,0:T(8,128)(2,1)S(1)}, u32[]{:S(2)}, u32[]{:S(2)}) collective-permute-start(f16[17,4,16,128]{3,2,1,0:T(8,128)(2,1)S(1)} %get-tuple-element.20), channel_id=1, source_target_pairs={{0,4},{1,5},{2,6},{3,7},{4,0},{5,1},{6,2},{7,3},{8,24},{9,56},{10,... | collective-permute-start | bytes 835592 | tf_op jit(solution)/shard_map/ppermute | solution.py:36
  108.8 14.3 %collective-permute-start.24 = (f16[17,4,16,128]{3,2,1,0:T(8,128)(2,1)S(1)}, f16[17,4,16,128]{3,2,1,0:T(8,128)(2,1)S(1)}, u32[]{:S(2)}, u32[]{:S(2)}) collective-permute-start(f16[17,4,16,128]{3,2,1,0:T(8,128)(2,1)S(1)} %get-tuple-element.21), channel_id=1, source_target_pairs={{0,2},{1,3},{2,4},{3,5},{4,6},{5,7},{6,0},{7,1},{8,8},{9,40},{10,1... | collective-permute-start | bytes 835592 | tf_op jit(solution)/shard_map/ppermute | solution.py:36
  111.1 15.1 %collective-permute-start.23 = (f16[17,4,16,128]{3,2,1,0:T(8,128)(2,1)S(1)}, f16[17,4,16,128]{3,2,1,0:T(8,128)(2,1)S(1)}, u32[]{:S(2)}, u32[]{:S(2)}) collective-permute-start(f16[17,4,16,128]{3,2,1,0:T(8,128)(2,1)S(1)} %get-tuple-element.22), channel_id=1, source_target_pairs={{0,0},{1,1},{2,2},{3,3},{4,4},{5,5},{6,6},{7,7},{8,8},{9,40},{10,1... | collective-permute-start | bytes 835592 | tf_op jit(solution)/shard_map/ppermute | solution.py:36
  126.3 9.0 %collective-permute-start.27 = (f32[4,8,4,16,128]{4,3,2,1,0:T(8,128)S(1)}, f32[4,8,4,16,128]{4,3,2,1,0:T(8,128)S(1)}, u32[]{:S(2)}, u32[]{:S(2)}) collective-permute-start(f32[4,8,4,16,128]{4,3,2,1,0:T(8,128)S(1)} %split.1), channel_id=1, source_target_pairs={{0,8},{1,9},{2,10},{3,11},{4,12},{5,13},{6,14},{7,15},{8,0},{9,1},... | collective-permute-start | bytes 3145736 | tf_op jit(solution)/shard_map/ppermute | solution.py:36
Sparse Core Ops, SparseCore 0:
  20.2 41.1 all-gather.1

commit v6 on v5

--- a/solution.py
+++ b/solution.py
@@ -133,7 +133,10 @@
     t = jnp.dot(t, swap[...], preferred_element_type=jnp.float32)
     forward, mirror = t[:, :64], t[:, 64:]
     plus = 0.5 * (forward + mirror)
-    minus = 0.5 * (forward - mirror) * offdiag[:, :64]
+    here = lax.broadcasted_iota(jnp.int32, (P_SIZE, P_SIZE), 0)
+    here = here == lax.broadcasted_iota(jnp.int32, (P_SIZE, P_SIZE), 1)
+    column = jnp.sum(jnp.where(here, offdiag[...], 0.0), axis=1, keepdims=True)
+    minus = 0.5 * (forward - mirror) * column
     u = jnp.concatenate([plus + minus, plus - minus])
     hi = u.astype(jnp.bfloat16)
     lo = (u - hi.astype(jnp.float32)).astype(jnp.bfloat16)
@@ -380,7 +383,7 @@
         t = t + send(t, lambda x, y, z, c, n=n: (x, y, z ^ n, c))
     t = t + send(t, far(1))
     offdiag = (pairs[:, 0] != pairs[:, 1]).astype(jnp.float32)
-    offdiag = jnp.broadcast_to(offdiag[:, None], (P_SIZE, 128))
+    offdiag = offdiag[None, :]
     swap = jnp.asarray(transposed_forward(), jnp.bfloat16)
     keep, *give = ladder(me, offdiag, swap, t, rows, second)
 

time: 145 us -> 145 us (level)
  transfers between devices with their start and end apart: 29 -> 29, of which waited for: 20 -> 20; matrix products, arithmetic and copies ran while one was open for 1% -> 2% of each run, Pallas kernels for 0% -> 0%
where the time goes in v6:
time: 145 us
  starting transfers between devices  55.1 us (38%)
  waiting for transfers between devices  51.5 us (36%)
  Pallas kernels  15.5 us (11%)
  between operations  13.9 us (10%)
  other arithmetic  5.42 us (4%)
  local copies, waits for them, and re-layouts  3.09 us (2%)
    ppermute x28, starting transfers between devices, send(): return lax.ppermute(block, AXES, pairs)  55.1 us
    ppermute x28, waiting for transfers between devices, send(): return lax.ppermute(block, AXES, pairs)  51.5 us
    pallas_call x1, Pallas kernels, ladder(): pl.pallas_call(ladder_kernel, out_shape=[jax.ShapeDtypeStruct((4, 17, 4,...  12.3 us
  transfers between devices with their start and end apart: 29, of which 20 were waited for; matrix products, arithmetic and copies ran while one was open for 2% of the time, Pallas kernels for 0%

profile of v6, /device:TPU:33, one launch (start us, length us, event | category | flops | bytes accessed | tf_op | source)
XLA Modules:
  0.0 144.6 jit_solution(11209038707455093426)
XLA Ops:
  6.5 1.2 dynamic-slice_bitcast_fusion.3
  7.8 0.8 collective-permute-start.2
  8.5 1.0 collective-permute-done.2
  9.6 0.6 blocks.1
  10.2 0.5 collective-permute-start.3
  10.7 2.7 %collective-permute-start.4 = (bf16[16,1024]{1,0:T(8,128)(2,1)S(1)}, bf16[16,1024]{1,0:T(8,128)(2,1)S(1)}, u32[]{:S(2)}, u32[]{:S(2)}) collective-permute-start(bf16[16,1024]{1,0:T(8,128)(2,1)S(1)} %blocks.1), channel_id=1, source_target_pairs={{0,32},{1,33},{2,34},{3,35},{4,36},{5,37},{6,38},{7,39},{8,12},{9,... | collective-permute-start | bytes 98312 | tf_op jit(solution)/shard_map/ppermute | solution.py:36
  13.4 0.5 collective-permute-start.5
  13.9 4.4 %collective-permute-start = (bf16[32,2304]{1,0:T(8,128)(2,1)S(1)}, bf16[32,2304]{1,0:T(8,128)(2,1)S(1)}, u32[]{:S(2)}, u32[]{:S(2)}) collective-permute-start(bf16[32,2304]{1,0:T(8,128)(2,1)S(1)} %get-tuple-element.23), channel_id=1, source_target_pairs={{0,0},{1,32},{2,2},{3,34},{4,4},{5,36},{6,6},{7,38},{8,8},{9,40},{... | collective-permute-start | bytes 442376 | tf_op jit(solution)/shard_map/ppermute | solution.py:36
  18.3 1.7 %collective-permute-start.1 = (bf16[32,2304]{1,0:T(8,128)(2,1)S(1)}, bf16[32,2304]{1,0:T(8,128)(2,1)S(1)}, u32[]{:S(2)}, u32[]{:S(2)}) collective-permute-start(bf16[32,2304]{1,0:T(8,128)(2,1)S(1)} %get-tuple-element.24), channel_id=1, source_target_pairs={{0,8},{1,40},{2,10},{3,42},{4,12},{5,44},{6,14},{7,46},{8,0},{9,32... | collective-permute-start | bytes 442376 | tf_op jit(solution)/shard_map/ppermute | solution.py:36
  20.1 3.5 %collective-permute-done = bf16[32,2304]{1,0:T(8,128)(2,1)S(1)} collective-permute-done((bf16[32,2304]{1,0:T(8,128)(2,1)S(1)}, bf16[32,2304]{1,0:T(8,128)(2,1)S(1)}, u32[]{:S(2)}, u32[]{:S(2)}) %collective-permute-start) | collective-permute-done | bytes 147488 | tf_op jit(solution)/shard_map/ppermute | solution.py:36
  23.6 3.4 %collective-permute-done.1 = bf16[32,2304]{1,0:T(8,128)(2,1)S(1)} collective-permute-done((bf16[32,2304]{1,0:T(8,128)(2,1)S(1)}, bf16[32,2304]{1,0:T(8,128)(2,1)S(1)}, u32[]{:S(2)}, u32[]{:S(2)}) %collective-permute-start.1) | collective-permute-done | bytes 147488 | tf_op jit(solution)/shard_map/ppermute | solution.py:36
  27.1 1.3 collective-permute-start.6
  28.5 0.1 collective-permute-start.7
  28.6 2.4 %collective-permute-start.8 = (bf16[80,2304]{1,0:T(8,128)(2,1)S(1)}, bf16[80,2304]{1,0:T(8,128)(2,1)S(1)}, u32[]{:S(2)}, u32[]{:S(2)}) collective-permute-start(bf16[80,2304]{1,0:T(8,128)(2,1)S(1)} %fusion.5), channel_id=1, source_target_pairs={{0,6},{1,7},{2,0},{3,1},{4,2},{5,3},{6,4},{7,5},{8,56},{9,57},{10,... | collective-permute-start | bytes 1105928 | tf_op jit(solution)/shard_map/ppermute | solution.py:36
  31.0 8.0 %collective-permute-done.6 = bf16[80,2304]{1,0:T(8,128)(2,1)S(1)} collective-permute-done((bf16[80,2304]{1,0:T(8,128)(2,1)S(1)}, bf16[80,2304]{1,0:T(8,128)(2,1)S(1)}, u32[]{:S(2)}, u32[]{:S(2)}) %collective-permute-start.6) | collective-permute-done | bytes 368672 | tf_op jit(solution)/shard_map/ppermute | solution.py:36
  39.2 0.6 collective-permute-done.8
  39.9 0.1 pad_maximum_fusion
  40.0 1.3 collective-permute-start.13
  41.3 2.5 %collective-permute-start.14 = (bf16[256,2304]{1,0:T(8,128)(2,1)S(1)}, bf16[256,2304]{1,0:T(8,128)(2,1)S(1)}, u32[]{:S(2)}, u32[]{:S(2)}) collective-permute-start(bf16[256,2304]{1,0:T(8,128)(2,1)S(1)} %bitcast.62), channel_id=1, source_target_pairs={{0,32},{1,33},{2,34},{3,35},{4,36},{5,37},{6,38},{7,39},{8,12},{9,... | collective-permute-start | bytes 3538952 | tf_op jit(solution)/shard_map/ppermute | solution.py:36
  43.8 1.4 collective-permute-start.15
  45.2 0.1 collective-permute-start.9
  45.3 3.4 %collective-permute-done.9 = bf16[16,1024]{1,0:T(8,128)(2,1)S(1)} collective-permute-done((bf16[16,1024]{1,0:T(8,128)(2,1)S(1)}, bf16[16,1024]{1,0:T(8,128)(2,1)S(1)}, u32[]{:S(2)}, u32[]{:S(2)}) %collective-permute-start.9) | collective-permute-done | bytes 32800 | tf_op jit(solution)/shard_map/ppermute | solution.py:36
  48.7 3.3 %collective-permute-start.10 = (bf16[16,1024]{1,0:T(8,128)(2,1)S(1)}, bf16[16,1024]{1,0:T(8,128)(2,1)S(1)}, u32[]{:S(2)}, u32[]{:S(2)}) collective-permute-start(bf16[16,1024]{1,0:T(8,128)(2,1)S(1)} %add.88), channel_id=1, source_target_pairs={{0,64},{1,65},{2,66},{3,67},{4,68},{5,69},{6,70},{7,71},{8,72},{9,... | collective-permute-start | bytes 98312 | tf_op jit(solution)/shard_map/ppermute | solution.py:36
  51.9 2.2 %collective-permute-done.10 = bf16[16,1024]{1,0:T(8,128)(2,1)S(1)} collective-permute-done((bf16[16,1024]{1,0:T(8,128)(2,1)S(1)}, bf16[16,1024]{1,0:T(8,128)(2,1)S(1)}, u32[]{:S(2)}, u32[]{:S(2)}) %collective-permute-start.10) | collective-permute-done | bytes 32800 | tf_op jit(solution)/shard_map/ppermute | solution.py:36
  54.1 5.5 %collective-permute-start.11 = (bf16[16,1024]{1,0:T(8,128)(2,1)S(1)}, bf16[16,1024]{1,0:T(8,128)(2,1)S(1)}, u32[]{:S(2)}, u32[]{:S(2)}) collective-permute-start(bf16[16,1024]{1,0:T(8,128)(2,1)S(1)} %add.89), channel_id=1, source_target_pairs={{0,128},{1,129},{2,130},{3,131},{4,132},{5,133},{6,134},{7,135},{8... | collective-permute-start | bytes 98312 | tf_op jit(solution)/shard_map/ppermute | solution.py:36
  59.6 1.8 %collective-permute-done.11 = bf16[16,1024]{1,0:T(8,128)(2,1)S(1)} collective-permute-done((bf16[16,1024]{1,0:T(8,128)(2,1)S(1)}, bf16[16,1024]{1,0:T(8,128)(2,1)S(1)}, u32[]{:S(2)}, u32[]{:S(2)}) %collective-permute-start.11) | collective-permute-done | bytes 32800 | tf_op jit(solution)/shard_map/ppermute | solution.py:36
  61.4 1.3 collective-permute-start.12
  62.7 0.5 fusion.39.offdiag
  63.2 7.4 %collective-permute-done.12 = bf16[16,1024]{1,0:T(8,128)(2,1)S(1)} collective-permute-done((bf16[16,1024]{1,0:T(8,128)(2,1)S(1)}, bf16[16,1024]{1,0:T(8,128)(2,1)S(1)}, u32[]{:S(2)}, u32[]{:S(2)}) %collective-permute-start.12) | collective-permute-done | bytes 32800 | tf_op jit(solution)/shard_map/ppermute | solution.py:36
  70.7 0.6 add.91.blocks
  71.4 1.0 copy-done.4
  72.3 0.4 copy-done.5
  72.8 12.3 %ladder.1 = (f32[4,17,4,16,128]{4,3,2,1,0:T(8,128)}, f32[17,4,16,128]{3,2,1,0:T(8,128)}, f32[17,4,16,128]{3,2,1,0:T(8,128)}, f32[17,4,16,128]{3,2,1,0:T(8,128)}, f32[17,4,16,128]{3,2,1,0:T(8,128)}) custom-call(s32[1]{0:T(128)} %bitcast.me, f32[1,64]{1,0:T(1,128)} %fusion.39.offdiag, bf16[128,128]{1,0:T(8,128)(2,1)} %constant.65.clone.swap, ...), custom_call_target="tpu_custom_call" | custom-call | tf_op jit(solution)/shard_map/ladder/pallas_call | solution.py:200
  85.0 1.5 %collective-permute-start.16 = (f32[17,4,16,128]{3,2,1,0:T(8,128)}, f32[17,4,16,128]{3,2,1,0:T(8,128)S(1)}, u32[]{:S(2)}, u32[]{:S(2)}) collective-permute-start(f32[17,4,16,128]{3,2,1,0:T(8,128)} %get-tuple-element.11), channel_id=1, source_target_pairs={{0,8},{1,9},{2,10},{3,11},{4,12},{5,13},{6,14},{7,15},{8,0},{9,1},... | collective-permute-start | bytes 1671176 | tf_op jit(solution)/shard_map/ppermute | solution.py:36
  86.5 0.1 collective-permute-start.17
  86.6 0.4 collective-permute-start.19
  87.0 0.1 collective-permute-start.21
  87.1 1.2 collective-permute-done.16
  88.3 0.8 collective-permute-done.17
  89.1 0.8 collective-permute-done.19
  89.9 0.8 collective-permute-done.21
  90.7 2.0 %bitcast_add_fusion.1 = (f32[17,4,16,128]{3,2,1,0:T(8,128)S(1)}, f32[17,4,16,128]{3,2,1,0:T(8,128)S(1)}, f32[17,4,16,128]{3,2,1,0:T(8,128)S(1)}, f32[17,4,16,128]{3,2,1,0:T(8,128)S(1)}) fusion(f32[17,4,16,128]{3,2,1,0:T(8,128)S(1)} %collective-permute-done.19, f32[4,17,4,16,128]{4,3,2,1,0:T(8,128)} %get-tuple-element.10, ...), kind=kLoop, calls=%fused_computation.5 | loop fusion | flops 557056 | bytes 6684672 | tf_op jit(solution)/shard_map/add | solution.py:390
  92.9 0.1 pad_maximum_fusion.4
  93.0 1.8 %collective-permute-start.18 = (f16[17,4,16,128]{3,2,1,0:T(8,128)(2,1)S(1)}, f16[17,4,16,128]{3,2,1,0:T(8,128)(2,1)S(1)}, u32[]{:S(2)}, u32[]{:S(2)}) collective-permute-start(f16[17,4,16,128]{3,2,1,0:T(8,128)(2,1)S(1)} %pad_maximum_fusion.4), channel_id=1, source_target_pairs={{0,64},{1,65},{2,66},{3,67},{4,68},{5,69},{6,70},{7,71},{8,10},{9,... | collective-permute-start | bytes 835592 | tf_op jit(solution)/shard_map/ppermute | solution.py:36
  94.9 0.1 pad_maximum_fusion.5
  95.0 1.9 %collective-permute-start.20 = (f16[17,4,16,128]{3,2,1,0:T(8,128)(2,1)S(1)}, f16[17,4,16,128]{3,2,1,0:T(8,128)(2,1)S(1)}, u32[]{:S(2)}, u32[]{:S(2)}) collective-permute-start(f16[17,4,16,128]{3,2,1,0:T(8,128)(2,1)S(1)} %pad_maximum_fusion.5), channel_id=1, source_target_pairs={{0,128},{1,129},{2,130},{3,131},{4,132},{5,133},{6,134},{7,135},{8... | collective-permute-start | bytes 835592 | tf_op jit(solution)/shard_map/ppermute | solution.py:36
  97.0 0.1 pad_maximum_fusion.6
  97.1 1.6 %collective-permute-start.22 = (f16[17,4,16,128]{3,2,1,0:T(8,128)(2,1)S(1)}, f16[17,4,16,128]{3,2,1,0:T(8,128)(2,1)S(1)}, u32[]{:S(2)}, u32[]{:S(2)}) collective-permute-start(f16[17,4,16,128]{3,2,1,0:T(8,128)(2,1)S(1)} %pad_maximum_fusion.6), channel_id=1, source_target_pairs={{0,192},{1,193},{2,194},{3,195},{4,196},{5,197},{6,198},{7,199},{8... | collective-permute-start | bytes 835592 | tf_op jit(solution)/shard_map/ppermute | solution.py:36
  98.8 0.9 collective-permute-done.18
  99.7 4.2 %collective-permute-done.20 = f16[17,4,16,128]{3,2,1,0:T(8,128)(2,1)S(1)} collective-permute-done((f16[17,4,16,128]{3,2,1,0:T(8,128)(2,1)S(1)}, f16[17,4,16,128]{3,2,1,0:T(8,128)(2,1)S(1)}, u32[]{:S(2)}, u32[]{:S(2)}) %collective-permute-start.20) | collective-permute-done | bytes 278560 | tf_op jit(solution)/shard_map/ppermute | solution.py:36
  103.8 0.4 pad_maximum_fusion.1
  104.4 0.5 maximum_select_fusion.2
  104.9 1.3 collective-permute-start.26
  106.3 2.5 %collective-permute-start.25 = (f16[17,4,16,128]{3,2,1,0:T(8,128)(2,1)S(1)}, f16[17,4,16,128]{3,2,1,0:T(8,128)(2,1)S(1)}, u32[]{:S(2)}, u32[]{:S(2)}) collective-permute-start(f16[17,4,16,128]{3,2,1,0:T(8,128)(2,1)S(1)} %get-tuple-element.20), channel_id=1, source_target_pairs={{0,4},{1,5},{2,6},{3,7},{4,0},{5,1},{6,2},{7,3},{8,24},{9,56},{10,... | collective-permute-start | bytes 835592 | tf_op jit(solution)/shard_map/ppermute | solution.py:36
  108.8 1.9 %collective-permute-start.24 = (f16[17,4,16,128]{3,2,1,0:T(8,128)(2,1)S(1)}, f16[17,4,16,128]{3,2,1,0:T(8,128)(2,1)S(1)}, u32[]{:S(2)}, u32[]{:S(2)}) collective-permute-start(f16[17,4,16,128]{3,2,1,0:T(8,128)(2,1)S(1)} %get-tuple-element.21), channel_id=1, source_target_pairs={{0,2},{1,3},{2,4},{3,5},{4,6},{5,7},{6,0},{7,1},{8,8},{9,40},{10,1... | collective-permute-start | bytes 835592 | tf_op jit(solution)/shard_map/ppermute | solution.py:36
  110.8 5.7 %collective-permute-start.23 = (f16[17,4,16,128]{3,2,1,0:T(8,128)(2,1)S(1)}, f16[17,4,16,128]{3,2,1,0:T(8,128)(2,1)S(1)}, u32[]{:S(2)}, u32[]{:S(2)}) collective-permute-start(f16[17,4,16,128]{3,2,1,0:T(8,128)(2,1)S(1)} %get-tuple-element.22), channel_id=1, source_target_pairs={{0,0},{1,1},{2,2},{3,3},{4,4},{5,5},{6,6},{7,7},{8,8},{9,40},{10,1... | collective-permute-start | bytes 835592 | tf_op jit(solution)/shard_map/ppermute | solution.py:36
  116.5 0.7 collective-permute-done.26
  117.3 2.8 %collective-permute-done.25 = f16[17,4,16,128]{3,2,1,0:T(8,128)(2,1)S(1)} collective-permute-done((f16[17,4,16,128]{3,2,1,0:T(8,128)(2,1)S(1)}, f16[17,4,16,128]{3,2,1,0:T(8,128)(2,1)S(1)}, u32[]{:S(2)}, u32[]{:S(2)}) %collective-permute-start.25) | collective-permute-done | bytes 278560 | tf_op jit(solution)/shard_map/ppermute | solution.py:36
  120.3 2.9 %collective-permute-done.24 = f16[17,4,16,128]{3,2,1,0:T(8,128)(2,1)S(1)} collective-permute-done((f16[17,4,16,128]{3,2,1,0:T(8,128)(2,1)S(1)}, f16[17,4,16,128]{3,2,1,0:T(8,128)(2,1)S(1)}, u32[]{:S(2)}, u32[]{:S(2)}) %collective-permute-start.24) | collective-permute-done | bytes 278560 | tf_op jit(solution)/shard_map/ppermute | solution.py:36
  123.2 2.9 %collective-permute-done.23 = f16[17,4,16,128]{3,2,1,0:T(8,128)(2,1)S(1)} collective-permute-done((f16[17,4,16,128]{3,2,1,0:T(8,128)(2,1)S(1)}, f16[17,4,16,128]{3,2,1,0:T(8,128)(2,1)S(1)}, u32[]{:S(2)}, u32[]{:S(2)}) %collective-permute-start.23) | collective-permute-done | bytes 278560 | tf_op jit(solution)/shard_map/ppermute | solution.py:36
  126.2 0.1 split.1
  126.3 6.6 %collective-permute-start.27 = (f32[4,8,4,16,128]{4,3,2,1,0:T(8,128)S(1)}, f32[4,8,4,16,128]{4,3,2,1,0:T(8,128)S(1)}, u32[]{:S(2)}, u32[]{:S(2)}) collective-permute-start(f32[4,8,4,16,128]{4,3,2,1,0:T(8,128)S(1)} %split.1), channel_id=1, source_target_pairs={{0,8},{1,9},{2,10},{3,11},{4,12},{5,13},{6,14},{7,15},{8,0},{9,1},... | collective-permute-start | bytes 3145736 | tf_op jit(solution)/shard_map/ppermute | solution.py:36
  132.9 2.3 %collective-permute-done.27.refs_4_ = f32[4,8,4,16,128]{4,3,2,1,0:T(8,128)S(1)} collective-permute-done((f32[4,8,4,16,128]{4,3,2,1,0:T(8,128)S(1)}, f32[4,8,4,16,128]{4,3,2,1,0:T(8,128)S(1)}, u32[]{:S(2)}, u32[]{:S(2)}) %collective-permute-start.27) | collective-permute-done | bytes 1048608 | tf_op jit(solution)/shard_map/ppermute | solution.py:36
  135.2 2.6 %finish.1 = f32[64,32,128]{2,1,0:T(8,128)} custom-call(s32[1]{0:T(128)} %bitcast.me, f32[16,4,16,128]{3,2,1,0:T(8,128)S(1)} %slice_multiply_fusion.3.refs_0_, f32[16,4,16,128]{3,2,1,0:T(8,128)S(1)} %slice_multiply_fusion.2.refs_1_, f32[16,4,16,128]{3,2,1,0:T(8,128)S(1)} %slice_multiply_fusion.1.refs_2_, f32[16,4,16,128]{3,2,1,0:T(8,128)S(1)} %slice_multiply_fusion.refs_3_, ...), custom_call_target="tpu_custom_call" | custom-call | tf_op jit(solution)/shard_map/finish/pallas_call | solution.py:317
  (63 shorter events, 1.5 us)
Async XLA Ops:
  6.5 3.0 %copy-start.2 = (s32[2,2]{1,0:T(2,128)S(1)}, s32[2,2]{1,0:T(2,128)}, u32[]{:S(2)}) copy-start(s32[2,2]{1,0:T(2,128)} %offsets.1) | copy-start | bytes 52
  6.5 3.0 %copy-start.1 = (bf16[64,32,128]{2,1,0:T(8,128)(2,1)S(1)}, bf16[64,32,128]{2,1,0:T(8,128)(2,1)}, u32[]{:S(2)}) copy-start(bf16[64,32,128]{2,1,0:T(8,128)(2,1)} %amplitudes.1) | copy-start | bytes 1572868
  6.5 64.8 %all-gather.2.cloned.1.call-start = ((), (), s32[]{:S(2)}) async-start(), calls=%async_computation | async-start | bytes 2654208 | tf_op jit(solution)/shard_map/all_gather | solution.py:355
  7.8 1.8 %collective-permute-start.2 = (bf16[32,2304]{1,0:T(8,128)(2,1)S(1)}, bf16[32,2304]{1,0:T(8,128)(2,1)S(1)}, u32[]{:S(2)}, u32[]{:S(2)}) collective-permute-start(bf16[32,2304]{1,0:T(8,128)(2,1)S(1)} %get-tuple-element.25), channel_id=1, source_target_pairs={{0,8},{1,9},{2,10},{3,11},{4,12},{5,13},{6,14},{7,15},{8,0},{9,1},... | collective-permute-start | bytes 442376 | tf_op jit(solution)/shard_map/ppermute | solution.py:36
  9.6 10.5 %copy-start = (bf16[64,2304]{1,0:T(8,128)(2,1)}, bf16[64,2304]{1,0:T(8,128)(2,1)S(1)}, u32[]{:S(2)}) copy-start(bf16[64,2304]{1,0:T(8,128)(2,1)S(1)} %pad_maximum_fusion.2._) | copy-start | bytes 884740
  10.2 9.9 %collective-permute-start.3 = (bf16[16,1024]{1,0:T(8,128)(2,1)S(1)}, bf16[16,1024]{1,0:T(8,128)(2,1)S(1)}, u32[]{:S(2)}, u32[]{:S(2)}) collective-permute-start(bf16[16,1024]{1,0:T(8,128)(2,1)S(1)} %blocks.1), channel_id=1, source_target_pairs={{0,8},{1,9},{2,10},{3,11},{4,12},{5,13},{6,14},{7,15},{8,0},{9,1},... | collective-permute-start | bytes 98312 | tf_op jit(solution)/shard_map/ppermute | solution.py:36
  10.7 9.4 %collective-permute-start.4 = (bf16[16,1024]{1,0:T(8,128)(2,1)S(1)}, bf16[16,1024]{1,0:T(8,128)(2,1)S(1)}, u32[]{:S(2)}, u32[]{:S(2)}) collective-permute-start(bf16[16,1024]{1,0:T(8,128)(2,1)S(1)} %blocks.1), channel_id=1, source_target_pairs={{0,32},{1,33},{2,34},{3,35},{4,36},{5,37},{6,38},{7,39},{8,12},{9,... | collective-permute-start | bytes 98312 | tf_op jit(solution)/shard_map/ppermute | solution.py:36
  13.4 6.7 %collective-permute-start.5 = (bf16[16,1024]{1,0:T(8,128)(2,1)S(1)}, bf16[16,1024]{1,0:T(8,128)(2,1)S(1)}, u32[]{:S(2)}, u32[]{:S(2)}) collective-permute-start(bf16[16,1024]{1,0:T(8,128)(2,1)S(1)} %blocks.1), channel_id=1, source_target_pairs={{0,12},{1,13},{2,14},{3,15},{4,8},{5,9},{6,10},{7,11},{8,32},{9,33... | collective-permute-start | bytes 98312 | tf_op jit(solution)/shard_map/ppermute | solution.py:36
  13.9 9.7 %collective-permute-start = (bf16[32,2304]{1,0:T(8,128)(2,1)S(1)}, bf16[32,2304]{1,0:T(8,128)(2,1)S(1)}, u32[]{:S(2)}, u32[]{:S(2)}) collective-permute-start(bf16[32,2304]{1,0:T(8,128)(2,1)S(1)} %get-tuple-element.23), channel_id=1, source_target_pairs={{0,0},{1,32},{2,2},{3,34},{4,4},{5,36},{6,6},{7,38},{8,8},{9,40},{... | collective-permute-start | bytes 442376 | tf_op jit(solution)/shard_map/ppermute | solution.py:36
  18.3 8.8 %collective-permute-start.1 = (bf16[32,2304]{1,0:T(8,128)(2,1)S(1)}, bf16[32,2304]{1,0:T(8,128)(2,1)S(1)}, u32[]{:S(2)}, u32[]{:S(2)}) collective-permute-start(bf16[32,2304]{1,0:T(8,128)(2,1)S(1)} %get-tuple-element.24), channel_id=1, source_target_pairs={{0,8},{1,40},{2,10},{3,42},{4,12},{5,44},{6,14},{7,46},{8,0},{9,32... | collective-permute-start | bytes 442376 | tf_op jit(solution)/shard_map/ppermute | solution.py:36
  27.1 11.9 %collective-permute-start.6 = (bf16[80,2304]{1,0:T(8,128)(2,1)S(1)}, bf16[80,2304]{1,0:T(8,128)(2,1)S(1)}, u32[]{:S(2)}, u32[]{:S(2)}) collective-permute-start(bf16[80,2304]{1,0:T(8,128)(2,1)S(1)} %fusion.5), channel_id=1, source_target_pairs={{0,2},{1,3},{2,4},{3,5},{4,6},{5,7},{6,0},{7,1},{8,24},{9,25},{10,... | collective-permute-start | bytes 1105928 | tf_op jit(solution)/shard_map/ppermute | solution.py:36
  28.5 10.6 %collective-permute-start.7 = (bf16[80,2304]{1,0:T(8,128)(2,1)S(1)}, bf16[80,2304]{1,0:T(8,128)(2,1)S(1)}, u32[]{:S(2)}, u32[]{:S(2)}) collective-permute-start(bf16[80,2304]{1,0:T(8,128)(2,1)S(1)} %fusion.5), channel_id=1, source_target_pairs={{0,4},{1,5},{2,6},{3,7},{4,0},{5,1},{6,2},{7,3},{8,40},{9,41},{10,... | collective-permute-start | bytes 1105928 | tf_op jit(solution)/shard_map/ppermute | solution.py:36
  28.6 11.2 %collective-permute-start.8 = (bf16[80,2304]{1,0:T(8,128)(2,1)S(1)}, bf16[80,2304]{1,0:T(8,128)(2,1)S(1)}, u32[]{:S(2)}, u32[]{:S(2)}) collective-permute-start(bf16[80,2304]{1,0:T(8,128)(2,1)S(1)} %fusion.5), channel_id=1, source_target_pairs={{0,6},{1,7},{2,0},{3,1},{4,2},{5,3},{6,4},{7,5},{8,56},{9,57},{10,... | collective-permute-start | bytes 1105928 | tf_op jit(solution)/shard_map/ppermute | solution.py:36
  39.9 22.8 %copy-start.6 = (s32[64,2]{0,1:T(2,128)S(1)}, s32[64,2]{0,1:T(2,128)}, u32[]{:S(2)}) copy-start(s32[64,2]{0,1:T(2,128)} %param.5) | copy-start | bytes 1540
  40.0 31.3 %copy-start.3 = (bf16[4,8,8,2304]{3,1,0,2:T(8,128)(2,1)}, bf16[4,8,8,2304]{3,1,0,2:T(8,128)(2,1)S(1)}, u32[]{:S(2)}) copy-start(bf16[4,8,8,2304]{3,1,0,2:T(8,128)(2,1)S(1)} %pad_maximum_fusion) | copy-start | bytes 3538948
  40.0 31.2 %collective-permute-start.13 = (bf16[256,2304]{1,0:T(8,128)(2,1)S(1)}, bf16[256,2304]{1,0:T(8,128)(2,1)S(1)}, u32[]{:S(2)}, u32[]{:S(2)}) collective-permute-start(bf16[256,2304]{1,0:T(8,128)(2,1)S(1)} %bitcast.61), channel_id=1, source_target_pairs={{0,16},{1,17},{2,18},{3,19},{4,20},{5,21},{6,22},{7,23},{8,10},{9,... | collective-permute-start | bytes 3538952 | tf_op jit(solution)/shard_map/ppermute | solution.py:36
  41.3 30.0 %collective-permute-start.14 = (bf16[256,2304]{1,0:T(8,128)(2,1)S(1)}, bf16[256,2304]{1,0:T(8,128)(2,1)S(1)}, u32[]{:S(2)}, u32[]{:S(2)}) collective-permute-start(bf16[256,2304]{1,0:T(8,128)(2,1)S(1)} %bitcast.62), channel_id=1, source_target_pairs={{0,32},{1,33},{2,34},{3,35},{4,36},{5,37},{6,38},{7,39},{8,12},{9,... | collective-permute-start | bytes 3538952 | tf_op jit(solution)/shard_map/ppermute | solution.py:36
  43.8 27.5 %collective-permute-start.15 = (bf16[256,2304]{1,0:T(8,128)(2,1)S(1)}, bf16[256,2304]{1,0:T(8,128)(2,1)}, u32[]{:S(2)}, u32[]{:S(2)}) collective-permute-start(bf16[256,2304]{1,0:T(8,128)(2,1)S(1)} %bitcast.63), channel_id=1, source_target_pairs={{0,48},{1,49},{2,50},{3,51},{4,52},{5,53},{6,54},{7,55},{8,14},{9,... | collective-permute-start | bytes 3538952 | tf_op jit(solution)/shard_map/ppermute | solution.py:36
  45.2 3.5 %collective-permute-start.9 = (bf16[16,1024]{1,0:T(8,128)(2,1)S(1)}, bf16[16,1024]{1,0:T(8,128)(2,1)S(1)}, u32[]{:S(2)}, u32[]{:S(2)}) collective-permute-start(bf16[16,1024]{1,0:T(8,128)(2,1)S(1)} %fusion.33), channel_id=1, source_target_pairs={{0,1},{1,0},{2,3},{3,2},{4,5},{5,4},{6,7},{7,6},{8,9},{9,8},{10,11... | collective-permute-start | bytes 98312 | tf_op jit(solution)/shard_map/ppermute | solution.py:36
  48.7 5.5 %collective-permute-start.10 = (bf16[16,1024]{1,0:T(8,128)(2,1)S(1)}, bf16[16,1024]{1,0:T(8,128)(2,1)S(1)}, u32[]{:S(2)}, u32[]{:S(2)}) collective-permute-start(bf16[16,1024]{1,0:T(8,128)(2,1)S(1)} %add.88), channel_id=1, source_target_pairs={{0,64},{1,65},{2,66},{3,67},{4,68},{5,69},{6,70},{7,71},{8,72},{9,... | collective-permute-start | bytes 98312 | tf_op jit(solution)/shard_map/ppermute | solution.py:36
  54.1 7.2 %collective-permute-start.11 = (bf16[16,1024]{1,0:T(8,128)(2,1)S(1)}, bf16[16,1024]{1,0:T(8,128)(2,1)S(1)}, u32[]{:S(2)}, u32[]{:S(2)}) collective-permute-start(bf16[16,1024]{1,0:T(8,128)(2,1)S(1)} %add.89), channel_id=1, source_target_pairs={{0,128},{1,129},{2,130},{3,131},{4,132},{5,133},{6,134},{7,135},{8... | collective-permute-start | bytes 98312 | tf_op jit(solution)/shard_map/ppermute | solution.py:36
  61.4 9.3 %collective-permute-start.12 = (bf16[16,1024]{1,0:T(8,128)(2,1)S(1)}, bf16[16,1024]{1,0:T(8,128)(2,1)S(1)}, u32[]{:S(2)}, u32[]{:S(2)}) collective-permute-start(bf16[16,1024]{1,0:T(8,128)(2,1)S(1)} %add.90), channel_id=1, source_target_pairs={{0,16},{1,17},{2,18},{3,19},{4,20},{5,21},{6,22},{7,23},{8,10},{9,... | collective-permute-start | bytes 98312 | tf_op jit(solution)/shard_map/ppermute | solution.py:36
  71.3 1.0 copy-start.4
  71.3 1.5 %copy-start.5 = (bf16[256,2304]{1,0:T(8,128)(2,1)}, bf16[256,2304]{1,0:T(8,128)(2,1)S(1)}, u32[]{:S(2)}) copy-start(bf16[256,2304]{1,0:T(8,128)(2,1)S(1)} %collective-permute-done.14.refs_2_) | copy-start | bytes 3538948
  85.0 3.3 %collective-permute-start.16 = (f32[17,4,16,128]{3,2,1,0:T(8,128)}, f32[17,4,16,128]{3,2,1,0:T(8,128)S(1)}, u32[]{:S(2)}, u32[]{:S(2)}) collective-permute-start(f32[17,4,16,128]{3,2,1,0:T(8,128)} %get-tuple-element.11), channel_id=1, source_target_pairs={{0,8},{1,9},{2,10},{3,11},{4,12},{5,13},{6,14},{7,15},{8,0},{9,1},... | collective-permute-start | bytes 1671176 | tf_op jit(solution)/shard_map/ppermute | solution.py:36
  86.5 2.6 %collective-permute-start.17 = (f32[17,4,16,128]{3,2,1,0:T(8,128)}, f32[17,4,16,128]{3,2,1,0:T(8,128)S(1)}, u32[]{:S(2)}, u32[]{:S(2)}) collective-permute-start(f32[17,4,16,128]{3,2,1,0:T(8,128)} %get-tuple-element.12), channel_id=1, source_target_pairs={{0,8},{1,9},{2,10},{3,11},{4,12},{5,13},{6,14},{7,15},{8,0},{9,1},... | collective-permute-start | bytes 1671176 | tf_op jit(solution)/shard_map/ppermute | solution.py:36
  86.6 3.3 %collective-permute-start.19 = (f32[17,4,16,128]{3,2,1,0:T(8,128)}, f32[17,4,16,128]{3,2,1,0:T(8,128)S(1)}, u32[]{:S(2)}, u32[]{:S(2)}) collective-permute-start(f32[17,4,16,128]{3,2,1,0:T(8,128)} %get-tuple-element.13), channel_id=1, source_target_pairs={{0,8},{1,9},{2,10},{3,11},{4,12},{5,13},{6,14},{7,15},{8,0},{9,1},... | collective-permute-start | bytes 1671176 | tf_op jit(solution)/shard_map/ppermute | solution.py:36
  87.0 3.7 %collective-permute-start.21 = (f32[17,4,16,128]{3,2,1,0:T(8,128)}, f32[17,4,16,128]{3,2,1,0:T(8,128)S(1)}, u32[]{:S(2)}, u32[]{:S(2)}) collective-permute-start(f32[17,4,16,128]{3,2,1,0:T(8,128)} %get-tuple-element.14), channel_id=1, source_target_pairs={{0,8},{1,9},{2,10},{3,11},{4,12},{5,13},{6,14},{7,15},{8,0},{9,1},... | collective-permute-start | bytes 1671176 | tf_op jit(solution)/shard_map/ppermute | solution.py:36
  93.0 6.7 %collective-permute-start.18 = (f16[17,4,16,128]{3,2,1,0:T(8,128)(2,1)S(1)}, f16[17,4,16,128]{3,2,1,0:T(8,128)(2,1)S(1)}, u32[]{:S(2)}, u32[]{:S(2)}) collective-permute-start(f16[17,4,16,128]{3,2,1,0:T(8,128)(2,1)S(1)} %pad_maximum_fusion.4), channel_id=1, source_target_pairs={{0,64},{1,65},{2,66},{3,67},{4,68},{5,69},{6,70},{7,71},{8,10},{9,... | collective-permute-start | bytes 835592 | tf_op jit(solution)/shard_map/ppermute | solution.py:36
  95.0 8.8 %collective-permute-start.20 = (f16[17,4,16,128]{3,2,1,0:T(8,128)(2,1)S(1)}, f16[17,4,16,128]{3,2,1,0:T(8,128)(2,1)S(1)}, u32[]{:S(2)}, u32[]{:S(2)}) collective-permute-start(f16[17,4,16,128]{3,2,1,0:T(8,128)(2,1)S(1)} %pad_maximum_fusion.5), channel_id=1, source_target_pairs={{0,128},{1,129},{2,130},{3,131},{4,132},{5,133},{6,134},{7,135},{8... | collective-permute-start | bytes 835592 | tf_op jit(solution)/shard_map/ppermute | solution.py:36
  97.1 6.7 %collective-permute-start.22 = (f16[17,4,16,128]{3,2,1,0:T(8,128)(2,1)S(1)}, f16[17,4,16,128]{3,2,1,0:T(8,128)(2,1)S(1)}, u32[]{:S(2)}, u32[]{:S(2)}) collective-permute-start(f16[17,4,16,128]{3,2,1,0:T(8,128)(2,1)S(1)} %pad_maximum_fusion.6), channel_id=1, source_target_pairs={{0,192},{1,193},{2,194},{3,195},{4,196},{5,197},{6,198},{7,199},{8... | collective-permute-start | bytes 835592 | tf_op jit(solution)/shard_map/ppermute | solution.py:36
  104.9 12.2 %collective-permute-start.26 = (f16[17,4,16,128]{3,2,1,0:T(8,128)(2,1)S(1)}, f16[17,4,16,128]{3,2,1,0:T(8,128)(2,1)S(1)}, u32[]{:S(2)}, u32[]{:S(2)}) collective-permute-start(f16[17,4,16,128]{3,2,1,0:T(8,128)(2,1)S(1)} %get-tuple-element.19), channel_id=1, source_target_pairs={{0,6},{1,7},{2,0},{3,1},{4,2},{5,3},{6,4},{7,5},{8,24},{9,56},{10,... | collective-permute-start | bytes 835592 | tf_op jit(solution)/shard_map/ppermute | solution.py:36
  106.3 13.8 %collective-permute-start.25 = (f16[17,4,16,128]{3,2,1,0:T(8,128)(2,1)S(1)}, f16[17,4,16,128]{3,2,1,0:T(8,128)(2,1)S(1)}, u32[]{:S(2)}, u32[]{:S(2)}) collective-permute-start(f16[17,4,16,128]{3,2,1,0:T(8,128)(2,1)S(1)} %get-tuple-element.20), channel_id=1, source_target_pairs={{0,4},{1,5},{2,6},{3,7},{4,0},{5,1},{6,2},{7,3},{8,24},{9,56},{10,... | collective-permute-start | bytes 835592 | tf_op jit(solution)/shard_map/ppermute | solution.py:36
  108.8 14.3 %collective-permute-start.24 = (f16[17,4,16,128]{3,2,1,0:T(8,128)(2,1)S(1)}, f16[17,4,16,128]{3,2,1,0:T(8,128)(2,1)S(1)}, u32[]{:S(2)}, u32[]{:S(2)}) collective-permute-start(f16[17,4,16,128]{3,2,1,0:T(8,128)(2,1)S(1)} %get-tuple-element.21), channel_id=1, source_target_pairs={{0,2},{1,3},{2,4},{3,5},{4,6},{5,7},{6,0},{7,1},{8,8},{9,40},{10,1... | collective-permute-start | bytes 835592 | tf_op jit(solution)/shard_map/ppermute | solution.py:36
  110.8 15.4 %collective-permute-start.23 = (f16[17,4,16,128]{3,2,1,0:T(8,128)(2,1)S(1)}, f16[17,4,16,128]{3,2,1,0:T(8,128)(2,1)S(1)}, u32[]{:S(2)}, u32[]{:S(2)}) collective-permute-start(f16[17,4,16,128]{3,2,1,0:T(8,128)(2,1)S(1)} %get-tuple-element.22), channel_id=1, source_target_pairs={{0,0},{1,1},{2,2},{3,3},{4,4},{5,5},{6,6},{7,7},{8,8},{9,40},{10,1... | collective-permute-start | bytes 835592 | tf_op jit(solution)/shard_map/ppermute | solution.py:36
  126.3 8.9 %collective-permute-start.27 = (f32[4,8,4,16,128]{4,3,2,1,0:T(8,128)S(1)}, f32[4,8,4,16,128]{4,3,2,1,0:T(8,128)S(1)}, u32[]{:S(2)}, u32[]{:S(2)}) collective-permute-start(f32[4,8,4,16,128]{4,3,2,1,0:T(8,128)S(1)} %split.1), channel_id=1, source_target_pairs={{0,8},{1,9},{2,10},{3,11},{4,12},{5,13},{6,14},{7,15},{8,0},{9,1},... | collective-permute-start | bytes 3145736 | tf_op jit(solution)/shard_map/ppermute | solution.py:36
Sparse Core Ops, SparseCore 0:
  20.2 40.8 all-gather.1
